TPU v7x, 32 devices: a whole 2x2x4 slice. The times are simulated.
32 devices in a mesh: dp: 8 (over y, x, core), tensor: 4 (over z).
Axes of the slice: x: 2, y: 2, z: 4, core: 2. Of those that a mesh axis runs over, the one named last changes fastest.
Arguments:
- layer_input: bfloat16 [8, 640, 768], P('dp'), may hold values from -6 to 6
- segment_ids: int32 [8, 640], P('dp'), may hold values from 0 to 3, never falling along the last dimension, each value on 1 to 256 neighbouring positions
- token_types: int32 [8, 640], P('dp'), may hold values 0 or 1
- query_weight: float32 [4, 768, 768], P(None, 'dp', 'tensor'), may hold values from -0.21875 to 0.21875
- key_weight: float32 [768, 768], P('dp', 'tensor'), may hold values from -0.21875 to 0.21875
- value_weight: float32 [768, 768], P('dp', 'tensor'), may hold values from -0.21875 to 0.21875
- out_weight: float32 [768, 768], P('tensor', 'dp'), may hold values from -0.875 to 0.875
- up_weight: float32 [768, 3072], P('dp', 'tensor'), may hold values from -0.21875 to 0.21875
- down_weight: float32 [3072, 768], P('tensor', 'dp'), may hold values from -0.109375 to 0.109375
- query_bias: float32 [4, 768], P(None, 'tensor'), may hold values from -3 to 3
- value_bias: float32 [768], P('tensor'), may hold values from -3 to 3
- out_bias: float32 [768], replicated, may hold values from -2 to 2
- up_bias: float32 [3072], P('tensor'), may hold values from -3 to 3
- down_bias: float32 [768], replicated, may hold values from -2 to 2
- attn_gain: float32 [768], replicated, may hold values from 0.1 to 1.9
- attn_shift: float32 [768], replicated, may hold values from -2 to 2
- ffn_gain: float32 [768], replicated, may hold values from 0.1 to 1.9
- ffn_shift: float32 [768], replicated, may hold values from -2 to 2
- cotangent: bfloat16 [8, 640, 768], P('dp'), may hold values from -6 to 6
Outputs:
- output: bfloat16 [8, 640, 768], P('dp')
- input_grad: bfloat16 [8, 640, 768], P('dp')
- query_grad: float32 [4, 768, 768], P(None, 'dp', 'tensor')
- key_grad: float32 [768, 768], P('dp', 'tensor')
- value_grad: float32 [768, 768], P('dp', 'tensor')
- outproj_grad: float32 [768, 768], P('tensor', 'dp')
- upproj_grad: float32 [768, 3072], P('dp', 'tensor')
- downproj_grad: float32 [3072, 768], P('tensor', 'dp')
- querybias_grad: float32 [4, 768], P(None, 'tensor')
- valuebias_grad: float32 [768], P('tensor')
- outbias_grad: float32 [768], replicated
- upbias_grad: float32 [3072], P('tensor')
- downbias_grad: float32 [768], replicated
- attngain_grad: float32 [768], replicated
- attnshift_grad: float32 [768], replicated
- ffngain_grad: float32 [768], replicated
- ffnshift_grad: float32 [768], replicated
Inputs may be any that keep to these rules, and one draw needn't show every extreme that they name: `segment_ids`: along a row segment numbers never fall, and one segment spans at most 256 positions.
All inputs are finite; a program needn't handle non-finite values. No bound on the sum of `token_types` on one device may be relied on, other than what follows from the above.
Results may differ from a plain program's by a relative error of at most 0.013.
The roundings to bfloat16 on the way count: a program that leaves them out, or rounds other values in their place, can miss the bound.
Values may be sent and summed in bfloat16 or wider, within the bound.
A program may use at most 128 MiB of HBM per device.

v0:
```python
from functools import partial

import jax
import jax.numpy as jnp
from jax import lax
from jax.sharding import PartitionSpec as P

HD = 64


EPSILON = 1e-05
SCALING = 0.125
NEGATIVE = -1000000000.0


def layer_norm_keep(values, norm_gain, norm_shift):
    centre = values - jnp.mean(values, axis=-1, keepdims=True)
    inverse = lax.rsqrt(jnp.mean(centre * centre, axis=-1, keepdims=True) + EPSILON)
    normal = centre * inverse
    return (normal * norm_gain + norm_shift, normal, inverse)


def layer_norm_back(upstream, normal, inverse, norm_gain):
    scaled = upstream * norm_gain
    gain_grad = jnp.sum(upstream * normal, axis=0)
    shift_grad = jnp.sum(upstream, axis=0)
    inner_term = (
        scaled
        - jnp.mean(scaled, axis=-1, keepdims=True)
        - normal * jnp.mean(scaled * normal, axis=-1, keepdims=True)
    )
    return (inverse * inner_term, gain_grad, shift_grad)


def heads_of(matrix):
    return matrix.reshape(matrix.shape[0], -1, HD)


def pick_queries(query_rows, type_row):
    word_tok = (type_row == 0)[:, None]
    return (
        jnp.where(word_tok, query_rows[0], query_rows[2]),
        jnp.where(word_tok, query_rows[1], query_rows[3]),
    )


def score_block(word_heads, entity_heads, key_heads, segment_row, type_row):
    to_words = jnp.einsum("qhd,khd->hqk", word_heads, key_heads, preferred_element_type=jnp.float32)
    to_entities = jnp.einsum(
        "qhd,khd->hqk", entity_heads, key_heads, preferred_element_type=jnp.float32
    )
    scores = jnp.where((type_row == 0)[None, None, :], to_words, to_entities) * SCALING
    allowed = (segment_row[:, None] == segment_row[None, :])[None]
    return jnp.where(allowed, scores, NEGATIVE)


def attend_forward(packed):
    query_rows, key_seq, value_seq, segment_row, type_row = packed
    word_query, entity_query = pick_queries(query_rows, type_row)
    scores = score_block(
        heads_of(word_query), heads_of(entity_query), heads_of(key_seq), segment_row, type_row
    )
    row_top = jnp.max(scores, axis=-1, keepdims=True)
    weights = jnp.exp(scores - row_top)
    totals = jnp.sum(weights, axis=-1, keepdims=True)
    attn_probs = (weights / totals).astype(jnp.bfloat16)
    context = jnp.einsum(
        "hqk,khd->qhd", attn_probs, heads_of(value_seq), preferred_element_type=jnp.float32
    )
    log_total = (row_top + jnp.log(totals))[..., 0]
    return (context.reshape(context.shape[0], -1).astype(jnp.bfloat16), log_total)


def attend_backward(packed):
    query_rows, key_seq, value_seq, segment_row, type_row, log_total, context_grad = packed
    word_query, entity_query = pick_queries(query_rows, type_row)
    word_heads = heads_of(word_query)
    entity_heads = heads_of(entity_query)
    key_heads = heads_of(key_seq)
    value_heads = heads_of(value_seq)
    grad_heads = heads_of(context_grad)
    scores = score_block(word_heads, entity_heads, key_heads, segment_row, type_row)
    attn_probs = jnp.exp(scores - log_total[..., None])
    prob_grad = jnp.einsum(
        "qhd,khd->hqk", grad_heads, value_heads, preferred_element_type=jnp.float32
    )
    score_grad = attn_probs * (prob_grad - jnp.sum(attn_probs * prob_grad, axis=-1, keepdims=True))
    score_low = score_grad.astype(jnp.bfloat16)
    word_key = (type_row == 0)[None, None, :]
    zeroes = jnp.zeros_like(score_low)
    word_part = jnp.where(word_key, score_low, zeroes)
    entity_part = jnp.where(word_key, zeroes, score_low)
    word_qgrad = (
        jnp.einsum("hqk,khd->qhd", word_part, key_heads, preferred_element_type=jnp.float32)
        * SCALING
    )
    entity_qgrad = (
        jnp.einsum("hqk,khd->qhd", entity_part, key_heads, preferred_element_type=jnp.float32)
        * SCALING
    )
    key_delta = (
        jnp.einsum("hqk,qhd->khd", word_part, word_heads, preferred_element_type=jnp.float32)
        + jnp.einsum("hqk,qhd->khd", entity_part, entity_heads, preferred_element_type=jnp.float32)
    ) * SCALING
    value_delta = jnp.einsum(
        "hqk,qhd->khd",
        attn_probs.astype(jnp.bfloat16),
        grad_heads,
        preferred_element_type=jnp.float32,
    )
    row_count = word_qgrad.shape[0]
    return (
        word_qgrad.reshape(row_count, -1),
        entity_qgrad.reshape(row_count, -1),
        key_delta.reshape(row_count, -1),
        value_delta.reshape(row_count, -1),
    )


def row_share(partial_rows):
    return lax.psum_scatter(partial_rows, "tensor", scatter_dimension=0, tiled=True)


def row_whole(rounded_rows):
    return lax.all_gather(rounded_rows, "tensor", axis=0, tiled=True)


def shards(
    layer_input,
    segment_ids,
    token_types,
    query_weight,
    key_weight,
    value_weight,
    out_weight,
    up_weight,
    down_weight,
    query_bias,
    value_bias,
    out_bias,
    up_bias,
    down_bias,
    attn_gain,
    attn_shift,
    ffn_gain,
    ffn_shift,
    cotangent,
):
    seq_count, seq_length, model_width = layer_input.shape
    tokens = layer_input.reshape(-1, model_width)
    row_count = tokens.shape[0]
    share = row_count // lax.axis_size("tensor")
    first_row = lax.axis_index("tensor") * share

    def own_rows(matrix):
        return lax.dynamic_slice_in_dim(matrix, first_row, share, 0)

    def combine_rows(partial_rows):
        return row_share(partial_rows)

    def whole_rows(rounded_rows):
        return row_whole(rounded_rows)

    query_complete, key_full, value_full, out_full = (
        lax.all_gather(query_weight.astype(jnp.bfloat16), "dp", axis=1, tiled=True),
        lax.all_gather(key_weight.astype(jnp.bfloat16), "dp", axis=0, tiled=True),
        lax.all_gather(value_weight.astype(jnp.bfloat16), "dp", axis=0, tiled=True),
        lax.all_gather(out_weight.astype(jnp.bfloat16), "dp", axis=1, tiled=True),
    )
    local_width = key_full.shape[1]
    query_rows = jnp.einsum(
        "gow,qwk->gqok", layer_input, query_complete, preferred_element_type=jnp.float32
    )
    query_rows = (query_rows + query_bias[None, :, None, :]).astype(jnp.bfloat16)
    keys_all = jnp.dot(layer_input, key_full, preferred_element_type=jnp.float32).astype(
        jnp.bfloat16
    )
    values_all = (
        jnp.dot(layer_input, value_full, preferred_element_type=jnp.float32) + value_bias
    ).astype(jnp.bfloat16)
    context, log_total = lax.map(
        attend_forward, (query_rows, keys_all, values_all, segment_ids, token_types)
    )
    context_rows = context.reshape(-1, local_width)
    attended = combine_rows(jnp.dot(context_rows, out_full, preferred_element_type=jnp.float32))
    residual = own_rows(tokens).astype(jnp.float32) + attended + out_bias
    normed, normal_one, inverse_one = layer_norm_keep(residual, attn_gain, attn_shift)
    normed_low = whole_rows(normed.astype(jnp.bfloat16))
    up_full, down_full = (
        lax.all_gather(up_weight.astype(jnp.bfloat16), "dp", axis=0, tiled=True),
        lax.all_gather(down_weight.astype(jnp.bfloat16), "dp", axis=1, tiled=True),
    )
    pre_act = jnp.dot(normed_low, up_full, preferred_element_type=jnp.float32) + up_bias
    activated, gelu_pull = jax.vjp(partial(jax.nn.gelu, approximate=False), pre_act)
    act_low = activated.astype(jnp.bfloat16)
    ffn_out = (
        combine_rows(jnp.dot(act_low, down_full, preferred_element_type=jnp.float32)) + down_bias
    )
    normed_out, normal_two, inverse_two = layer_norm_keep(normed + ffn_out, ffn_gain, ffn_shift)
    output = whole_rows(normed_out.astype(jnp.bfloat16)).reshape(layer_input.shape)
    upstream = own_rows(cotangent.reshape(-1, model_width)).astype(jnp.float32)
    sum_grad, ffngain_grad, ffnshift_grad = layer_norm_back(
        upstream, normal_two, inverse_two, ffn_gain
    )
    downbias_grad = jnp.sum(sum_grad, axis=0)
    sum_low = whole_rows(sum_grad.astype(jnp.bfloat16))
    up_back, down_back = (
        lax.all_gather(up_weight.astype(jnp.bfloat16), "dp", axis=0, tiled=True),
        lax.all_gather(down_weight.astype(jnp.bfloat16), "dp", axis=1, tiled=True),
    )
    down_local = jnp.dot(act_low.T, sum_low, preferred_element_type=jnp.float32)
    act_grad = jnp.dot(sum_low, down_back.T, preferred_element_type=jnp.float32)
    (pre_grad,) = gelu_pull(act_grad)
    upbias_grad = jnp.sum(pre_grad, axis=0)
    pre_low = pre_grad.astype(jnp.bfloat16)
    up_local = jnp.dot(normed_low.T, pre_low, preferred_element_type=jnp.float32)
    upproj_grad, downproj_grad = (
        lax.psum_scatter(up_local, "dp", scatter_dimension=0, tiled=True),
        lax.psum_scatter(down_local, "dp", scatter_dimension=1, tiled=True),
    )
    normed_grad = (
        combine_rows(jnp.dot(pre_low, up_back.T, preferred_element_type=jnp.float32)) + sum_grad
    )
    resid_grad, attngain_grad, attnshift_grad = layer_norm_back(
        normed_grad, normal_one, inverse_one, attn_gain
    )
    outbias_grad = jnp.sum(resid_grad, axis=0)
    resid_low = whole_rows(resid_grad.astype(jnp.bfloat16))
    query_pullback, key_pullback, value_pullback, out_back = (
        lax.all_gather(query_weight.astype(jnp.bfloat16), "dp", axis=1, tiled=True),
        lax.all_gather(key_weight.astype(jnp.bfloat16), "dp", axis=0, tiled=True),
        lax.all_gather(value_weight.astype(jnp.bfloat16), "dp", axis=0, tiled=True),
        lax.all_gather(out_weight.astype(jnp.bfloat16), "dp", axis=1, tiled=True),
    )
    outproj_local = jnp.dot(context_rows.T, resid_low, preferred_element_type=jnp.float32)
    context_grad = jnp.dot(resid_low, out_back.T, preferred_element_type=jnp.float32).astype(
        jnp.bfloat16
    )
    context_grad = context_grad.reshape(seq_count, seq_length, local_width)
    word_qgrad, entity_qgrad, key_delta, value_delta = lax.map(
        attend_backward,
        (query_rows, keys_all, values_all, segment_ids, token_types, log_total, context_grad),
    )
    is_word = (token_types == 0)[..., None]
    zero_rows = jnp.zeros_like(word_qgrad)
    query_delta = jnp.stack(
        [
            jnp.where(is_word, word_qgrad, zero_rows),
            jnp.where(is_word, entity_qgrad, zero_rows),
            jnp.where(is_word, zero_rows, word_qgrad),
            jnp.where(is_word, zero_rows, entity_qgrad),
        ],
        axis=1,
    )
    querybias_grad = jnp.sum(query_delta, axis=(0, 2))
    valuebias_grad = jnp.sum(value_delta, axis=(0, 1))
    query_reduced = query_delta.astype(jnp.bfloat16)
    key_reduced = key_delta.astype(jnp.bfloat16)
    value_reduced = value_delta.astype(jnp.bfloat16)
    query_local = jnp.einsum(
        "nvh,nkvw->khw", layer_input, query_reduced, preferred_element_type=jnp.float32
    )
    key_shard = jnp.einsum(
        "pui,pun->in", layer_input, key_reduced, preferred_element_type=jnp.float32
    )
    value_local = jnp.einsum(
        "pui,pun->in", layer_input, value_reduced, preferred_element_type=jnp.float32
    )
    input_part = (
        jnp.einsum(
            "kayo,azo->kyz", query_reduced, query_pullback, preferred_element_type=jnp.float32
        )
        + jnp.einsum("ohz,wz->ohw", key_reduced, key_pullback, preferred_element_type=jnp.float32)
        + jnp.einsum(
            "ohz,wz->ohw", value_reduced, value_pullback, preferred_element_type=jnp.float32
        )
    )
    input_total = combine_rows(input_part.reshape(-1, model_width))
    input_grad = whole_rows((input_total + resid_grad).astype(jnp.bfloat16)).reshape(
        layer_input.shape
    )
    query_grad, key_grad, value_grad, outproj_grad = (
        lax.psum_scatter(query_local, "dp", scatter_dimension=1, tiled=True),
        lax.psum_scatter(key_shard, "dp", scatter_dimension=0, tiled=True),
        lax.psum_scatter(value_local, "dp", scatter_dimension=0, tiled=True),
        lax.psum_scatter(outproj_local, "dp", scatter_dimension=1, tiled=True),
    )
    querybias_grad, valuebias_grad, upbias_grad = lax.psum(
        (querybias_grad, valuebias_grad, upbias_grad), "dp"
    )
    outbias_grad, downbias_grad, attngain_grad, attnshift_grad, ffngain_grad, ffnshift_grad = (
        lax.psum(
            (
                outbias_grad,
                downbias_grad,
                attngain_grad,
                attnshift_grad,
                ffngain_grad,
                ffnshift_grad,
            ),
            ("dp", "tensor"),
        )
    )
    return (
        output,
        input_grad,
        query_grad,
        key_grad,
        value_grad,
        outproj_grad,
        upproj_grad,
        downproj_grad,
        querybias_grad,
        valuebias_grad,
        outbias_grad,
        upbias_grad,
        downbias_grad,
        attngain_grad,
        attnshift_grad,
        ffngain_grad,
        ffnshift_grad,
    )


def solution(mesh):
    in_specs = (
        P("dp", None, None),
        P("dp", None),
        P("dp", None),
        P(None, "dp", "tensor"),
        P("dp", "tensor"),
        P("dp", "tensor"),
        P("tensor", "dp"),
        P("dp", "tensor"),
        P("tensor", "dp"),
        P(None, "tensor"),
        P("tensor"),
        P(),
        P("tensor"),
        P(),
        P(),
        P(),
        P(),
        P(),
        P("dp", None, None),
    )
    out_specs = (
        P("dp", None, None),
        P("dp", None, None),
        P(None, "dp", "tensor"),
        P("dp", "tensor"),
        P("dp", "tensor"),
        P("tensor", "dp"),
        P("dp", "tensor"),
        P("tensor", "dp"),
        P(None, "tensor"),
        P("tensor"),
        P(),
        P("tensor"),
        P(),
        P(),
        P(),
        P(),
        P(),
    )
    return jax.shard_map(shards, mesh=mesh, in_specs=in_specs, out_specs=out_specs, check_vma=False)
```

profile of v0, /device:TPU:0, one launch (start us, length us, event | category | flops | bytes accessed | tf_op | source)
XLA Modules:
  0.0 601.2 jit_solution(10092308148096753260)
XLA Ops:
  7.3 2.0 copy.82
  9.3 0.9 convert_element_type.134
  10.2 0.9 convert_element_type.129
  11.1 1.0 copy.50
  12.8 11.0 %all_gather.42 = bf16[192,768]{0,1:T(8,128)(2,1)S(1)} all-gather(bf16[192,96]{0,1:T(8,128)(2,1)S(1)} %copy.50), channel_id=1, replica_groups=mesh['dp'=8,'tensor'=4] {'dp'}, dimensions={1}, use_global_device_ids=true | all-gather | bytes 331776 | tf_op jit(solution)/shard_map/all_gather | solution.py:168
  23.9 10.9 %all_gather.39 = bf16[768,192]{1,0:T(8,128)(2,1)S(1)} all-gather(bf16[96,192]{1,0:T(8,128)(2,1)S(1)} %convert_element_type.129), channel_id=1, replica_groups=mesh['dp'=8,'tensor'=4] {'dp'}, dimensions={0}, use_global_device_ids=true | all-gather | bytes 331776 | tf_op jit(solution)/shard_map/all_gather | solution.py:167
  34.7 8.5 %all_gather.41 = bf16[768,192]{1,0:T(8,128)(2,1)S(1)} all-gather(bf16[96,192]{1,0:T(8,128)(2,1)S(1)} %convert_element_type.134), channel_id=1, replica_groups=mesh['dp'=8,'tensor'=4] {'dp'}, dimensions={0}, use_global_device_ids=true | all-gather | bytes 331776 | tf_op jit(solution)/shard_map/all_gather | solution.py:166
  44.1 1.2 fusion.30
  45.3 2.9 fusion.22
  48.4 0.8 fusion.74
  49.3 1.6 fusion.95
  51.6 1.5 copy-done
  53.1 1.0 fusion.31
  54.8 1.8 fusion.96
  58.2 41.1 %reduce-scatter.19.cloned.1.call-done = f32[160,768]{1,0:T(8,128)} async-done(((f32[640,768]{1,0:T(8,128)}), f32[160,768]{1,0:T(8,128)}) %reduce-scatter.19.cloned.1.call-update) | async-done | bytes 491536 | tf_op jit(solution)/shard_map/reduce_scatter | solution.py:121
  99.3 1.2 fusion.91
  100.9 20.8 %all_gather.43 = bf16[640,768]{1,0:T(8,128)(2,1)} all-gather(bf16[160,768]{1,0:T(8,128)(2,1)S(1)} %fusion.73), channel_id=1, replica_groups=mesh['dp'=8,'tensor'=4] {'tensor'}, dimensions={0}, use_global_device_ids=true | all-gather | bytes 1228800 | tf_op jit(solution)/shard_map/all_gather | solution.py:125
  121.7 3.4 all-gather.6.cloned.1.call-done
  125.1 8.5 %multiply_convert_fusion.1 = (bf16[640,768]{1,0:T(8,128)(2,1)}, f32[640,768]{1,0:T(8,128)}, f32[640,768]{1,0:T(8,128)}) fusion(f32[768]{0:T(1024)S(1)} %copy-done.49, bf16[640,768]{1,0:T(8,128)(2,1)} %all_gather.43, bf16[768,768]{1,0:T(8,128)(2,1)} %all-gather.6.cloned.1.call-done), kind=kOutput, calls=%fused_computation.24 | convolution fusion | flops 787415040 | bytes 7080960 | tf_op jit(solution)/shard_map/dot_general | solution.py:193
  133.6 17.9 %all-gather.8.cloned.1.call-done = bf16[768,768]{0,1:T(8,128)(2,1)} async-done(((bf16[768,96]{0,1:T(8,128)(2,1)}), bf16[768,768]{0,1:T(8,128)(2,1)}) %all-gather.8.cloned.1.call-update) | async-done | bytes 1179664 | tf_op jit(solution)/shard_map/all_gather | solution.py:191
  151.5 3.9 fusion.97
  155.4 41.6 %reduce-scatter.21.cloned.1.call-done = f32[160,768]{1,0:T(8,128)} async-done(((f32[640,768]{1,0:T(8,128)}), f32[160,768]{1,0:T(8,128)}) %reduce-scatter.21.cloned.1.call-update) | async-done | bytes 491536 | tf_op jit(solution)/shard_map/reduce_scatter | solution.py:121
  197.0 1.5 fusion.89
  199.1 0.9 fusion.85
  200.1 20.2 %all_gather.47 = bf16[640,768]{1,0:T(8,128)(2,1)S(1)} all-gather(bf16[160,768]{1,0:T(8,128)(2,1)S(1)} %convert_element_type.148), channel_id=1, replica_groups=mesh['dp'=8,'tensor'=4] {'tensor'}, dimensions={0}, use_global_device_ids=true | all-gather | bytes 1228800 | tf_op jit(solution)/shard_map/all_gather | solution.py:125
  220.3 2.1 fusion.88
  222.4 0.9 copy-done.50
  223.3 2.3 fusion.71
  225.7 41.2 %reduce-scatter.23.cloned.1.call-done = f32[160,768]{1,0:T(8,128)} async-done(((f32[640,768]{1,0:T(8,128)}), f32[160,768]{1,0:T(8,128)}) %reduce-scatter.23.cloned.1.call-update) | async-done | bytes 491536 | tf_op jit(solution)/shard_map/reduce_scatter | solution.py:121
  266.9 2.0 multiply_reduce_fusion.1
  269.7 20.3 %all_gather.48 = bf16[640,768]{1,0:T(8,128)(2,1)S(1)} all-gather(bf16[160,768]{1,0:T(8,128)(2,1)S(1)} %convert_element_type.150), channel_id=1, replica_groups=mesh['dp'=8,'tensor'=4] {'tensor'}, dimensions={0}, use_global_device_ids=true | all-gather | bytes 1228800 | tf_op jit(solution)/shard_map/all_gather | solution.py:125
  290.5 1.5 convolution_bitcast_fusion.1
  292.3 3.1 fusion.98
  295.4 9.8 %convolution_multiply_fusion.1 = f32[3,64,640]{2,1,0:T(8,128)} fusion(bf16[640,3,64]{0,2,1:T(8,128)(2,1)S(1)} %bitcast.146, pred[640]{0:T(1024)(128)(4,1)S(1)} %compare_reduce_fusion, f32[3,640,640]{1,2,0:T(8,128)} %fusion.98, f32[3,640,640]{1,2,0:T(8,128)} %copy-done, f32[3,640]{1,0:T(4,128)S(1)} %log_add_fusion), kind=kOutput, calls=%fused_computation.51 | convolution fusion | flops 166013440 | bytes 10576000 | tf_op jit(solution)/shard_map/while/body/eval_jaxpr/hqk,khd->qhd/dot_general | solution.py:94
  305.2 9.6 %convolution_multiply_fusion = f32[3,64,640]{2,1,0:T(8,128)} fusion(bf16[640,3,64]{0,2,1:T(8,128)(2,1)S(1)} %bitcast.147, pred[640]{0:T(1024)(128)(4,1)S(1)} %compare_reduce_fusion, f32[3,640,640]{1,2,0:T(8,128)} %fusion.98, f32[3,640,640]{1,2,0:T(8,128)} %copy-done, f32[3,640]{1,0:T(4,128)S(1)} %log_add_fusion), kind=kOutput, calls=%fused_computation.50 | convolution fusion | flops 166013440 | bytes 10576000 | tf_op jit(solution)/shard_map/while/body/eval_jaxpr/hqk,khd->qhd/dot_general | solution.py:98
  314.8 1.3 fusion.67
  317.0 2.5 convolution_bitcast_fusion
  319.6 4.5 copy.66
  324.1 4.7 reshape.590
  329.9 9.7 %fusion.32 = f32[3,64,640]{2,1,0:T(8,128)} fusion(pred[640]{0:T(1024)(128)(4,1)S(1)} %compare_reduce_fusion, f32[3,640,640]{1,2,0:T(8,128)} %fusion.98, f32[3,640,640]{1,2,0:T(8,128)} %copy-done, f32[3,640]{1,0:T(4,128)S(1)} %log_add_fusion, bf16[640,3,64]{0,2,1:T(8,128)(2,1)S(1)} %bitcast.164, bf16[640,3,64]{0,2,1:T(8,128)(2,1)S(1)} %bitcast.162), kind=kOutput, calls=%fused_computation.57 | convolution fusion | flops 166013440 | bytes 10821760 | tf_op jit(solution)/shard_map/while/body/eval_jaxpr/hqk,qhd->khd/dot_general | solution.py:102
  339.5 9.2 %fusion.29 = bf16[3,64,640]{2,1,0:T(8,128)(2,1)S(1)} fusion(f32[3,64,640]{2,1,0:T(8,128)} %fusion.32, pred[640]{0:T(1024)(128)(4,1)S(1)} %compare_reduce_fusion, f32[3,640,640]{1,2,0:T(8,128)} %fusion.98, f32[3,640,640]{1,2,0:T(8,128)} %copy-done, f32[3,640]{1,0:T(4,128)S(1)} %log_add_fusion, bf16[640,3,64]{0,2,1:T(8,128)(2,1)S(1)} %bitcast.160, ...), kind=kOutput, calls=%fused_computation.52 | convolution fusion | flops 166382080 | bytes 11067520 | tf_op jit(solution)/shard_map/while/body/eval_jaxpr/hqk,qhd->khd/dot_general | solution.py:103
  350.7 1.3 fusion.20
  352.6 1.0 fusion.94
  353.6 1.8 fusion.12
  355.5 1.1 copy-done.8
  356.6 3.8 fusion.100
  360.4 1.1 copy-done.6
  361.6 3.7 fusion.69
  365.8 1.1 copy.70
  367.0 1.6 convert_reduce_fusion
  368.6 25.4 %all_gather.46 = bf16[640,768]{1,0:T(8,128)(2,1)S(1)} all-gather(bf16[160,768]{1,0:T(8,128)(2,1)S(1)} %copy-done.4), channel_id=1, replica_groups=mesh['dp'=8,'tensor'=4] {'tensor'}, dimensions={0}, use_global_device_ids=true | all-gather | bytes 1228800 | tf_op jit(solution)/shard_map/all_gather | solution.py:125
  394.7 1.4 convolution_bitcast_fusion.3
  396.1 1.1 copy.68
  397.3 41.3 %all-reduce = (f32[768]{0:T(1024)}, f32[768]{0:T(1024)}, f32[768]{0:T(1024)}, f32[768]{0:T(1024)}, f32[768]{0:T(1024)}, /*index=5*/f32[768]{0:T(1024)}) all-reduce(f32[768]{0:T(1024)S(1)} %copy-done.36, f32[768]{0:T(1024)S(1)} %get-tuple-element.127, ...), channel_id=1, replica_groups=mesh['dp'=8,'tensor'=4] {'dp','tensor'}, use_global_device_ids=true, to_apply=%region_26.27 | all-reduce | flops 4608 | bytes 36864 | tf_op jit(solution)/shard_map/psum | solution.py:292
  439.3 14.7 %all-reduce.1 = (f32[4,192]{1,0:T(4,128)}, f32[192]{0:T(256)}, f32[768]{0:T(1024)}) all-reduce(f32[4,192]{1,0:T(4,128)S(1)} %maximum_reduce_fusion, f32[192]{0:T(256)S(1)} %copy-done.41, f32[768]{0:T(1024)S(1)} %copy-done.42), channel_id=1, replica_groups=mesh['dp'=8,'tensor'=4] {'dp'}, use_global_device_ids=true, to_apply=%region_22.23 | all-reduce | flops 1728 | bytes 13824 | tf_op jit(solution)/shard_map/psum | solution.py:288
  454.0 1.6 copy.73
  455.6 1.3 reshape.591
  457.7 1.1 add_convert_fusion
  458.7 20.6 %all_gather.49 = bf16[640,768]{1,0:T(8,128)(2,1)S(1)} all-gather(bf16[160,768]{1,0:T(8,128)(2,1)S(1)} %add_convert_fusion), channel_id=1, replica_groups=mesh['dp'=8,'tensor'=4] {'tensor'}, dimensions={0}, use_global_device_ids=true | all-gather | bytes 1228800 | tf_op jit(solution)/shard_map/all_gather | solution.py:125
  479.3 35.1 %reduce-scatter.27.cloned.1.call-done = f32[96,768]{1,0:T(8,128)} async-done(((f32[768,768]{1,0:T(8,128)}), f32[96,768]{1,0:T(8,128)}) %reduce-scatter.27.cloned.1.call-update) | async-done | bytes 294928 | tf_op jit(solution)/shard_map/reduce_scatter | solution.py:218
  514.4 38.9 %reduce-scatter.35.cloned.1.call-done = f32[96,192]{1,0:T(8,128)} async-done(((f32[768,192]{1,0:T(8,128)}), f32[96,192]{1,0:T(8,128)}) %reduce-scatter.35.cloned.1.call-update) | async-done | bytes 73744
  553.3 39.1 %reduce-scatter.33.cloned.1.call-done = f32[96,192]{1,0:T(8,128)} async-done(((f32[768,192]{1,0:T(8,128)}), f32[96,192]{1,0:T(8,128)}) %reduce-scatter.33.cloned.1.call-update) | async-done | bytes 73744
  592.4 0.9 copy.85
  593.3 0.9 copy.86
  (168 shorter events, 14.7 us)
Async XLA Ops:
  7.2 36.1 %copy-start.43 = (s32[1,640]{1,0:T(1,128)S(1)}, s32[1,640]{1,0:T(1,128)}, u32[]{:S(2)}) copy-start(s32[1,640]{1,0:T(1,128)} %param.21) | copy-start | bytes 7684
  7.2 36.4 %copy-start.1 = (bf16[1,640,768]{2,1,0:T(8,128)(2,1)S(1)}, bf16[1,640,768]{2,1,0:T(8,128)(2,1)}, u32[]{:S(2)}) copy-start(bf16[1,640,768]{2,1,0:T(8,128)(2,1)} %param.19) | copy-start | bytes 2949124
  7.2 38.1 %all-gather.4.cloned.1.call-start = ((), (), s32[]{:S(2)}) async-start(), calls=%async_computation.10 | async-start | bytes 1769472 | tf_op jit(solution)/shard_map/all_gather | solution.py:165
  9.3 34.9 %copy-start.44 = (f32[192]{0:T(256)S(1)}, f32[192]{0:T(256)}, u32[]{:S(2)}) copy-start(f32[192]{0:T(256)} %param.29) | copy-start | bytes 2308
  9.3 90.0 %reduce-scatter.19.cloned.1.call-start = ((), (), s32[]{:S(2)}) async-start(), calls=%async_computation.11 | async-start | bytes 2457600 | tf_op jit(solution)/shard_map/reduce_scatter | solution.py:121
  34.7 10.6 %copy-start.48 = (f32[4,192]{1,0:T(4,128)S(1)}, f32[4,192]{1,0:T(4,128)}, u32[]{:S(2)}) copy-start(f32[4,192]{1,0:T(4,128)} %param.28) | copy-start | bytes 9220
  48.3 0.9 copy-start.13
  48.3 0.9 copy-start.15
  48.3 0.9 copy-start.9
  48.4 0.9 copy-start.11
  50.9 2.2 copy-start
  50.9 2.2 copy-start.19
  54.8 1.9 copy-start.22
  54.8 2.7 copy-start.23
  56.6 42.7 %copy-start.38 = (f32[768]{0:T(1024)S(1)}, f32[768]{0:T(1024)}, u32[]{:S(2)}) copy-start(f32[768]{0:T(1024)} %param.30) | copy-start | bytes 9220
  56.6 44.1 %copy-start.32 = (f32[768]{0:T(1024)S(1)}, f32[768]{0:T(1024)}, u32[]{:S(2)}) copy-start(f32[768]{0:T(1024)} %param.33) | copy-start | bytes 9220
  56.6 44.1 %copy-start.33 = (f32[768]{0:T(1024)S(1)}, f32[768]{0:T(1024)}, u32[]{:S(2)}) copy-start(f32[768]{0:T(1024)} %param.34) | copy-start | bytes 9220
  56.7 68.4 %all-gather.6.cloned.1.call-start = ((), (), s32[]{:S(2)}) async-start(), calls=%async_computation.12 | async-start | bytes 1327104 | tf_op jit(solution)/shard_map/all_gather | solution.py:190
  57.4 94.1 %all-gather.8.cloned.1.call-start = ((), (), s32[]{:S(2)}) async-start(), calls=%async_computation.13 | async-start | bytes 1327104 | tf_op jit(solution)/shard_map/all_gather | solution.py:191
  58.2 66.9 %copy-start.49 = (f32[768]{0:T(1024)S(1)}, f32[768]{0:T(1024)}, u32[]{:S(2)}) copy-start(f32[768]{0:T(1024)} %param.31) | copy-start | bytes 9220
  58.2 138.8 %reduce-scatter.21.cloned.1.call-start = ((), (), s32[]{:S(2)}) async-start(), calls=%async_computation.14 | async-start | bytes 2457600 | tf_op jit(solution)/shard_map/reduce_scatter | solution.py:121
  155.4 41.6 %copy-start.39 = (f32[768]{0:T(1024)S(1)}, f32[768]{0:T(1024)}, u32[]{:S(2)}) copy-start(f32[768]{0:T(1024)} %param.32) | copy-start | bytes 9220
  155.4 43.3 %copy-start.34 = (f32[768]{0:T(1024)S(1)}, f32[768]{0:T(1024)}, u32[]{:S(2)}) copy-start(f32[768]{0:T(1024)} %param.35) | copy-start | bytes 9220
  155.4 43.7 %copy-start.40 = (f32[768]{0:T(1024)S(1)}, f32[768]{0:T(1024)}, u32[]{:S(2)}) copy-start(f32[768]{0:T(1024)} %param.36) | copy-start | bytes 9220
  155.4 111.5 %reduce-scatter.23.cloned.1.call-start = ((), (), s32[]{:S(2)}) async-start(), calls=%async_computation.15 | async-start | bytes 2457600 | tf_op jit(solution)/shard_map/reduce_scatter | solution.py:121
  197.0 1.7 copy-start.21
  197.0 23.2 %copy-start.52 = (f32[640,768]{1,0:T(8,128)S(1)}, f32[640,768]{1,0:T(8,128)}, u32[]{:S(2)}) copy-start(f32[640,768]{1,0:T(8,128)} %get-tuple-element.161) | copy-start | bytes 5898244
  198.7 21.5 %copy-start.47 = (bf16[768,768]{0,1:T(8,128)(2,1)S(1)}, bf16[768,768]{0,1:T(8,128)(2,1)}, u32[]{:S(2)}) copy-start(bf16[768,768]{0,1:T(8,128)(2,1)} %all-gather.8.cloned.1.call-done) | copy-start | bytes 3538948
  198.7 21.5 %copy-start.51 = (f32[640,768]{1,0:T(8,128)S(1)}, f32[640,768]{1,0:T(8,128)}, u32[]{:S(2)}) copy-start(f32[640,768]{1,0:T(8,128)} %get-tuple-element.137) | copy-start | bytes 5898244
  220.2 2.1 copy-start.7
  220.3 3.0 copy-start.46
  222.3 0.9 copy-start.50
  225.6 228.3 %reduce-scatter.37.cloned.1.call-start = ((), (), s32[]{:S(2)}) async-start(), calls=%async_computation.22 | async-start | bytes 884736
  269.7 20.8 %copy-start.18 = (bf16[3,64,640]{2,1,0:T(8,128)(2,1)S(1)}, bf16[3,64,640]{2,1,0:T(8,128)(2,1)}, u32[]{:S(2)}) copy-start(bf16[3,64,640]{2,1,0:T(8,128)(2,1)} %copy-done.17) | copy-start | bytes 737284
  290.0 2.3 copy-start.20
  292.0 163.5 %reduce-scatter.31.cloned.1.call-start = ((), (), s32[]{:S(2)}) async-start(), calls=%async_computation.19 | async-start | bytes 2654208
  316.1 0.8 copy-start.26
  316.1 0.8 copy-start.28
  316.1 0.9 copy-start.30
  328.8 0.9 copy-start.14
  328.8 1.1 copy-start.16
  328.8 10.7 %copy-start.10 = (bf16[1,1,640,192]{2,3,1,0:T(8,128)(2,1)S(1)}, bf16[1,1,640,192]{2,3,1,0:T(8,128)(2,1)}, u32[]{:S(2)}) copy-start(bf16[1,1,640,192]{2,3,1,0:T(8,128)(2,1)} %copy-done.9) | copy-start | bytes 737284
  328.9 10.7 %copy-start.12 = (bf16[1,1,640,192]{2,3,1,0:T(8,128)(2,1)S(1)}, bf16[1,1,640,192]{2,3,1,0:T(8,128)(2,1)}, u32[]{:S(2)}) copy-start(bf16[1,1,640,192]{2,3,1,0:T(8,128)(2,1)} %copy-done.11) | copy-start | bytes 737284
  328.9 128.8 %reduce-scatter.25.cloned.1.call-start = ((), (), s32[]{:S(2)}) async-start(), calls=%async_computation.16 | async-start | bytes 2457600 | tf_op jit(solution)/shard_map/reduce_scatter | solution.py:121
  348.7 0.7 copy-start.5
  348.8 1.0 copy-start.25
  348.8 1.1 copy-start.27
  348.8 1.2 copy-start.29
  348.8 1.4 copy-start.31
  348.8 1.9 copy-start.45
  348.8 3.5 slice-start
  350.7 1.9 slice-start.1
  355.4 1.2 copy-start.8
  355.4 123.9 %reduce-scatter.29.cloned.1.call-start = ((), (), s32[]{:S(2)}) async-start(), calls=%async_computation.18 | async-start | bytes 2654208 | tf_op jit(solution)/shard_map/reduce_scatter | solution.py:219
  360.3 1.2 copy-start.6
  360.4 154.1 %reduce-scatter.27.cloned.1.call-start = ((), (), s32[]{:S(2)}) async-start(), calls=%async_computation.17 | async-start | bytes 2654208 | tf_op jit(solution)/shard_map/reduce_scatter | solution.py:218
  365.3 3.3 copy-start.4
  365.3 188.0 %reduce-scatter.35.cloned.1.call-start = ((), (), s32[]{:S(2)}) async-start(), calls=%async_computation.21 | async-start | bytes 884736
  367.0 225.4 %reduce-scatter.33.cloned.1.call-start = ((), (), s32[]{:S(2)}) async-start(), calls=%async_computation.20 | async-start | bytes 884736
  394.7 43.9 %copy-start.2 = (f32[3,64,640]{2,1,0:T(8,128)S(1)}, f32[3,64,640]{2,1,0:T(8,128)}, u32[]{:S(2)}) copy-start(f32[3,64,640]{2,1,0:T(8,128)} %convolution_multiply_fusion.1) | copy-start | bytes 1474564
  396.1 1.2 copy-start.35
  396.1 1.2 copy-start.36
  396.1 1.2 copy-start.37
  396.1 42.5 %copy-start.3 = (f32[3,64,640]{2,1,0:T(8,128)S(1)}, f32[3,64,640]{2,1,0:T(8,128)}, u32[]{:S(2)}) copy-start(f32[3,64,640]{2,1,0:T(8,128)} %convolution_multiply_fusion) | copy-start | bytes 1474564
  (4 other events, 2.8 us)
Sparse Core Ops, SparseCore 0:
  10.5 28.6 all-gather.3
  56.8 42.4 reduce-scatter.18
  101.8 23.2 all-gather.5
  127.4 24.0 all-gather.7
  155.5 41.4 reduce-scatter.20
  225.8 41.1 reduce-scatter.22
  292.2 34.6 reduce-scatter.36
  330.2 42.4 reduce-scatter.30
  375.2 44.9 reduce-scatter.24
  424.3 43.6 reduce-scatter.28
  471.9 42.4 reduce-scatter.26
  518.3 34.9 reduce-scatter.34
  557.4 34.9 reduce-scatter.32
where the time goes:
time: 610 us; the launch traced here: 601 us
  waiting for transfers between devices  258 us (42%)
  blocking collectives  194 us (32%)
  matrix products  86.3 us (14%)
  local copies, waits for them, and re-layouts  30.4 us (5%)
  other arithmetic  16.5 us (3%)
  between operations  15 us (2%)
    reduce_scatter x4, waiting for transfers between devices, row_share(): lax.psum_scatter(partial_rows, 'tensor', scatter_dimension=0, tiled=True)  124 us
    all_gather x5, blocking collectives, row_whole(): return lax.all_gather(rounded_rows, 'tensor', axis=0, tiled=True)  107 us
    unnamed x17, waiting for transfers between devices  78.2 us
    psum x1, blocking collectives, shards(): lax.psum((outbias_grad, downbias_grad, attngain_grad, attnshift_grad, ffn...  41.3 us
    reduce_scatter x1, waiting for transfers between devices, shards(): lax.psum_scatter(up_local, 'dp', scatter_dimension=0, tiled=True)  35.1 us
    unnamed x121, local copies, waits for them, and re-layouts  29.7 us
    all_gather x1, waiting for transfers between devices, shards(): lax.all_gather(down_weight.astype(jnp.bfloat16), 'dp', axis=1, tiled=True)  17.9 us
    psum x1, blocking collectives, shards(): lax.psum((querybias_grad, valuebias_grad, upbias_grad), 'dp')  14.7 us
  transfers between devices with their start and end apart: 13, of which 8 were waited for; matrix products, arithmetic and copies ran while one was open for 16% of the time, Pallas kernels for 0%

commit v1 on v0

--- a/solution.py
+++ b/solution.py
@@ -3,6 +3,8 @@
 import jax
 import jax.numpy as jnp
 from jax import lax
+from jax.experimental import pallas as pl
+from jax.experimental.pallas import tpu as pltpu
 from jax.sharding import PartitionSpec as P
 
 HD = 64
@@ -322,6 +324,725 @@
     )
 
 
+MESH = pl.DeviceIdType.MESH
+BF = jnp.bfloat16
+F32 = jnp.float32
+BLOCK = 128
+
+
+def fits(mesh):
+    return mesh.shape["dp"] == 8 and mesh.shape["tensor"] == 4
+
+
+def nn(a, b):
+    return lax.dot_general(a, b, (((1,), (0,)), ((), ())), preferred_element_type=F32)
+
+
+def nt(a, b):
+    return lax.dot_general(a, b, (((1,), (1,)), ((), ())), preferred_element_type=F32)
+
+
+def tn(a, b):
+    return lax.dot_general(a, b, (((0,), (0,)), ((), ())), preferred_element_type=F32)
+
+
+def norm_rows(values):
+    centre = values - jnp.mean(values, axis=-1, keepdims=True)
+    inverse = lax.rsqrt(jnp.mean(centre * centre, axis=-1, keepdims=True) + EPSILON)
+    return centre * inverse, inverse
+
+
+def norm_rows_back(upstream, normal, inverse, gain):
+    scaled = upstream * gain
+    return inverse * (
+        scaled
+        - jnp.mean(scaled, axis=-1, keepdims=True)
+        - normal * jnp.mean(scaled * normal, axis=-1, keepdims=True)
+    )
+
+
+class Net:
+    def __init__(self, send, recv, peer):
+        self.send, self.recv, self.peer = send, recv, peer
+        self.sends = 0
+        self.banks = 0
+        self.pending = []
+
+    def bank(self, count):
+        base = self.banks
+        self.banks += count
+        return base
+
+    def start(self, src, dst, sem, device, when=None):
+        slot = self.sends
+        self.sends += 1
+
+        def make():
+            return pltpu.make_async_remote_copy(
+                src_ref=src,
+                dst_ref=dst,
+                send_sem=self.send.at[slot],
+                recv_sem=self.recv.at[sem],
+                device_id=device,
+                device_id_type=MESH,
+            )
+
+        if when is None:
+            make().start()
+        else:
+            pl.when(when)(lambda: make().start())
+        self.pending.append((make, when))
+
+    def wait(self, dst, sem, when=None):
+        def make():
+            return pltpu.make_async_remote_copy(
+                src_ref=dst,
+                dst_ref=dst,
+                send_sem=self.send.at[0],
+                recv_sem=self.recv.at[sem],
+                device_id=self.peer,
+                device_id_type=MESH,
+            )
+
+        if when is None:
+            make().wait_recv()
+        else:
+            pl.when(when)(lambda: make().wait_recv())
+
+    def drain(self):
+        for make, when in self.pending:
+            if when is None:
+                make().wait_send()
+            else:
+                pl.when(when)(lambda make=make: make().wait_send())
+        self.pending = []
+
+
+SENDS = 120
+RECVS = 160
+
+
+def layer_kernel(
+    x_ref, seg_ref, typ_ref, qw_ref, kw_ref, vw_ref, ow_ref, uw_ref, dw_ref, qb_ref, vb_ref,
+    ob_ref, ub_ref, db_ref, ag_ref, as_ref, fg_ref, fs_ref, cot_ref,
+    out_ref, ig_ref, qg_ref, kg_ref, vg_ref, og_ref, ug_ref, dg_ref, small_ref,
+    wq, wo, own, wf, ubs, segc, wordc, xt, bias, qq, kv, kk, kvt, kkt, probs, ctx, ct,
+    a_s, n1_s, r1_s, act, gelu_d, gl, parts, rs_send, rs_recv, du_s, dub, dzb,
+    grad, ry, fs_b, rx, fr, dh_s, dct, dc, dco, go, go_r, so, rp, sp, rz,
+    dqkv, dxp, dxr, gq, gq_r, sq, gp, sv, vb8, sw, vz,
+    send_sems, recv_sems,
+):
+    d = lax.axis_index("dp")
+    t = lax.axis_index("tensor")
+    c = d % 2
+    x = (d // 2) % 2
+    y = d // 4
+    j = d % 4
+    chip = d // 2
+    sib = d + 1 - 2 * c
+    xn = d + 2 - 4 * x
+    yn = d + 4 - 8 * y
+    rows = x_ref.shape[1]
+    quarter = rows // 4
+    width = x_ref.shape[2]
+    strip = qw_ref.shape[1]
+    local = kw_ref.shape[1]
+    heads = local // HD
+    blocks = rows // BLOCK
+    own_rows = pl.ds(pl.multiple_of(t * quarter, 16), quarter)
+    net = Net(send_sems, recv_sems, (sib, t))
+
+    def flip_x(device):
+        return device + 2 - 4 * ((device // 2) % 2)
+
+    def flip_y(device):
+        return device + 4 - 8 * (device // 4)
+
+    dg = flip_y(xn)
+    part_m, part_o = parts.at[0:2], parts.at[2:4]
+    sums_a, sums_b = parts.reshape(rows, width), gelu_d.reshape(rows, width)
+    dqq = [sums_a.at[:, BLOCK * h : BLOCK * (h + 1)] for h in range(heads)]
+    dkk = [sums_a.at[:, BLOCK * (heads + h) : BLOCK * (heads + h + 1)] for h in range(heads)]
+    dvv = [sums_b.at[:, BLOCK * h : BLOCK * (h + 1)] for h in range(heads)]
+
+    barrier = pltpu.get_barrier_semaphore()
+    for m in range(1, 8):
+        pl.semaphore_signal(barrier, 1, device_id=((d + m) % 8, t), device_id_type=MESH)
+    for k in range(1, 4):
+        for m in range(4):
+            pl.semaphore_signal(
+                barrier, 1, device_id=(4 * y + (j + m) % 4, (t + k) % 4), device_id_type=MESH
+            )
+    pl.semaphore_wait(barrier, 19)
+
+    for h in range(heads):
+        at = slice(HD * h, HD * (h + 1))
+        piece = jnp.concatenate(
+            [qw_ref[i, :, at] for i in range(4)] + [kw_ref[:, at], vw_ref[:, at]], axis=1
+        )
+        wq[d, :, 6 * HD * h : 6 * HD * (h + 1)] = piece.astype(BF)
+
+    class PlaneGather:
+        def __init__(self, ref_of):
+            self.ref_of, self.bank = ref_of, net.bank(8)
+
+        def copy(self, block, device):
+            net.start(self.ref_of(block), self.ref_of(block), self.bank + block, (device, t))
+
+        def begin(self):
+            for device in (xn, yn, dg, sib):
+                self.copy(d, device)
+
+        def middle(self):
+            for block in (xn, yn, dg):
+                net.wait(self.ref_of(block), self.bank + block)
+                self.copy(block, sib)
+
+        def end(self):
+            for block in (sib, flip_x(sib), flip_y(sib), flip_x(flip_y(sib))):
+                net.wait(self.ref_of(block), self.bank + block)
+
+    gather_q = PlaneGather(lambda b: wq.at[b])
+    gather_q.begin()
+
+    def wide_t(value, high, wide):
+        r, w = value.shape
+        if w < wide:
+            value = jnp.concatenate([value, jnp.zeros((r, wide - w), value.dtype)], axis=1)
+        if r < high:
+            value = jnp.concatenate([value, jnp.zeros((high - r, wide), value.dtype)], axis=0)
+        return value.T
+
+    wo[t, d] = wide_t(ow_ref[...], 256, 128)[:strip, :local].astype(BF)
+    own[0] = uw_ref[...].astype(BF)
+    own[1] = dw_ref[...].astype(BF)
+    ubs[t] = jnp.broadcast_to(ub_ref[...][None], ubs.shape[1:])
+
+    wo_z = net.bank(4)
+    ub_z = net.bank(4)
+    wf_z = net.bank(8)
+    wf_y = net.bank(8)
+    for k in range(1, 4):
+        s = (t + k) % 4
+        net.start(wo.at[t, d], wo.at[t, d], wo_z + t, (d, s))
+        net.start(ubs.at[t], ubs.at[t], ub_z + t, (d, s))
+    mine = j == t
+    for i in range(2):
+        for k in range(1, 4):
+            net.start(own.at[i], wf.at[i, d], wf_z + 4 * i + j, (4 * y + t, (t + k) % 4))
+        net.start(own.at[i], wf.at[i, d], wf_z + 4 * i + j, (4 * y + t, t), when=jnp.logical_not(mine))
+
+    @pl.when(mine)
+    def _():
+        for i in range(2):
+            wf[i, d] = own[i]
+
+    for b in range(blocks):
+        at = slice(BLOCK * b, BLOCK * (b + 1))
+        segc[at, :] = jnp.broadcast_to(seg_ref[:, at].astype(F32), (BLOCK, BLOCK)).T
+        wordc[at, :] = jnp.broadcast_to((typ_ref[:, at] == 0).astype(F32), (BLOCK, BLOCK)).T
+    xt[...] = x_ref[0].T
+    for h in range(heads):
+        at = slice(HD * h, HD * (h + 1))
+        bias[:, 6 * HD * h : 6 * HD * (h + 1)] = jnp.concatenate(
+            [qb_ref[i : i + 1, at] for i in range(4)] + [jnp.zeros((1, HD), F32), vb_ref[at][None]],
+            axis=1,
+        )
+
+    gather_q.middle()
+    gather_q.end()
+
+    low_half = lax.broadcasted_iota(jnp.int32, (rows, BLOCK), 1) < HD
+    is_word = wordc[...] > 0.5
+    for h in range(heads):
+        base = 6 * HD * h
+        at = slice(BLOCK * h, BLOCK * (h + 1))
+        made = nn(x_ref[0], wq[:, :, base : base + 6 * HD].reshape(width, 6 * HD))
+        made = made + bias[:, base : base + 6 * HD]
+        qq[:, at] = jnp.where(is_word, made[:, :BLOCK], made[:, BLOCK : 2 * BLOCK]).astype(BF)
+        both = made[:, 2 * BLOCK :]
+        keys = jnp.where(low_half, both, pltpu.roll(both, HD, 1))
+        keys = jnp.where(jnp.logical_xor(is_word, low_half), 0.0, keys)
+        kv[:, at] = both.astype(BF)
+        kk[:, at] = keys.astype(BF)
+        kvt[h] = both.T.astype(BF)
+        kkt[h] = keys.T.astype(BF)
+
+    gather_o = PlaneGather(lambda b: wo.at[:, b])
+    for k in range(1, 4):
+        s = (t + k) % 4
+        net.wait(wo.at[s, d], wo_z + s)
+    gather_o.begin()
+
+    ct_z = net.bank(4)
+
+    def span(b):
+        return BLOCK * max(0, b - 2), BLOCK * min(blocks, b + 3)
+
+    kept = [0]
+    for b in range(blocks):
+        kept.append(kept[-1] + span(b)[1] - span(b)[0])
+    for b in range(blocks):
+        lo, hi = span(b)
+        at_q = slice(BLOCK * b, BLOCK * (b + 1))
+        same = segc[lo:hi, :] == seg_ref[:, at_q].astype(F32)
+        found = []
+        for h in range(heads):
+            at = slice(BLOCK * h, BLOCK * (h + 1))
+            scores = nt(kk[lo:hi, at], qq[at_q, at]) * SCALING
+            scores = jnp.where(same, scores, NEGATIVE)
+            weights = jnp.exp(scores - jnp.max(scores, axis=0, keepdims=True))
+            weights = weights * (1.0 / jnp.sum(weights, axis=0, keepdims=True))
+            probs[h, kept[b] : kept[b + 1]] = weights
+            found.append(nn(kvt[h, HD:, lo:hi], weights.astype(BF)))
+        found.append(jnp.zeros((HD, BLOCK), F32))
+        ctx[at_q, :] = jnp.concatenate(found, axis=0).T[:, :local].astype(BF)
+        if b > 0:
+            s = b - 1
+            src = ctx.at[quarter * s : quarter * (s + 1)]
+            net.start(src, ct.at[t], ct_z + t, (d, s), when=t != s)
+    ct[t] = ctx[own_rows, :]
+
+    gather_o.middle()
+
+    for i in range(1):
+        for m in range(4):
+            r = (j + m) % 4
+            net.wait(wf.at[i, 4 * y + r], wf_z + 4 * i + r, when=jnp.logical_or(r != j, j != t))
+            net.start(wf.at[i, 4 * y + r], wf.at[i, 4 * y + r], wf_y + 4 * i + r, (yn, t))
+    gather_o.end()
+
+    for k in range(1, 4):
+        s = (t + k) % 4
+        net.wait(ct.at[s], ct_z + s)
+    attended = nt(ct[0], wo[0].reshape(width, local))
+    for s in range(1, 4):
+        attended = attended + nt(ct[s], wo[s].reshape(width, local))
+    normal, inverse = norm_rows(x_ref[0, own_rows, :].astype(F32) + attended + ob_ref[...][None])
+    n1_s[...] = normal
+    r1_s[...] = jnp.broadcast_to(inverse, r1_s.shape)
+    normed = normal * ag_ref[...][None] + as_ref[...][None]
+    a_s[...] = normed
+    act[j] = normed.astype(BF)
+
+    class RowGather:
+        def __init__(self, ref):
+            self.ref, self.bank = ref, net.bank(4)
+
+        def copy(self, rank, device):
+            net.start(self.ref.at[rank], self.ref.at[rank], self.bank + rank, (device, t))
+
+        def begin(self):
+            self.copy(j, xn)
+            self.copy(j, sib)
+
+        def near(self):
+            net.wait(self.ref.at[sib % 4], self.bank + sib % 4)
+
+        def middle(self):
+            net.wait(self.ref.at[xn % 4], self.bank + xn % 4)
+            self.copy(xn % 4, sib)
+
+        def far(self):
+            net.wait(self.ref.at[flip_x(sib) % 4], self.bank + flip_x(sib) % 4)
+
+    class RowSum:
+        def __init__(self, index):
+            self.index, self.bank = index, net.bank(3)
+
+        def hand(self, slot, partial_rows):
+            where = 3 * self.index + slot
+            rs_send[where] = partial_rows.astype(BF)
+            net.start(
+                rs_send.at[where], rs_recv.at[where], self.bank + slot, (xn if slot == 2 else sib, t)
+            )
+
+        def take(self, slot):
+            where = 3 * self.index + slot
+            net.wait(rs_recv.at[where], self.bank + slot)
+            return rs_recv[where].astype(F32)
+
+        def own_half(self):
+            self.hand(0, part_m[1 - c])
+
+        def other_half(self):
+            self.hand(1, part_o[1 - c])
+            self.hand(2, part_o[c] + self.take(1))
+
+        def total(self):
+            return part_m[c] + self.take(0) + self.take(2)
+
+    rows_a = RowGather(act)
+    rows_a.begin()
+    for i in range(1, 2):
+        for m in range(4):
+            r = (j + m) % 4
+            net.wait(wf.at[i, 4 * y + r], wf_z + 4 * i + r, when=jnp.logical_or(r != j, j != t))
+            net.start(wf.at[i, 4 * y + r], wf.at[i, 4 * y + r], wf_y + 4 * i + r, (yn, t))
+    rows_a.middle()
+    rows_a.near()
+    for k in range(1, 4):
+        s = (t + k) % 4
+        net.wait(ubs.at[s], ub_z + s)
+    for m in range(4):
+        r = 4 * (1 - y) + (j + m) % 4
+        net.wait(wf.at[0, r], wf_y + (j + m) % 4)
+
+    near = pl.ds(2 * x, 2)
+    away = pl.ds(2 - 2 * x, 2)
+
+    def feed(half):
+        hidden = nn(act[half].reshape(2 * quarter, width), wf[0].reshape(width, width))
+        hidden = hidden + ubs[j][:1]
+        bell = 0.5 * (1.0 + lax.erf(hidden * 0.7071067811865476))
+        slope = bell + hidden * (0.3989422804014327 * jnp.exp(-0.5 * hidden * hidden))
+        gelu_d[half] = slope.reshape(2, quarter, width)
+        gl[half] = (hidden * bell).astype(BF).reshape(2, quarter, width)
+
+    def feed_out(half, part):
+        made = nt(gl[half].reshape(2 * quarter, width), wf[1].reshape(width, width))
+        part[...] = made.reshape(2, quarter, width)
+
+    feed(near)
+    rows_a.far()
+    feed(away)
+    for m in range(4):
+        r = 4 * (1 - y) + (j + m) % 4
+        net.wait(wf.at[1, r], wf_y + 4 + (j + m) % 4)
+    sum_f = RowSum(0)
+    feed_out(away, part_o)
+    sum_f.hand(1, part_o[1 - c])
+    feed_out(near, part_m)
+    sum_f.own_half()
+    sum_f.hand(2, part_o[c] + sum_f.take(1))
+    ffn_out = sum_f.total() + db_ref[...][None]
+
+    normal, inverse = norm_rows(a_s[...] + ffn_out)
+    out_ref[0, own_rows, :] = (normal * fg_ref[...][None] + fs_ref[...][None]).astype(BF)
+    out_z = net.bank(4)
+    for k in range(1, 4):
+        net.start(out_ref.at[0, own_rows], out_ref.at[0, own_rows], out_z + t, (d, (t + k) % 4))
+    upstream = cot_ref[0, own_rows, :].astype(F32)
+    du = norm_rows_back(upstream, normal, inverse, fg_ref[...][None])
+    dub[j] = du.astype(BF)
+    rows_u = RowGather(dub)
+    rows_u.begin()
+    du_s[...] = du
+    sv[...] = jnp.zeros_like(sv)
+    sv[0:1] = jnp.sum(upstream * normal, axis=0, keepdims=True)
+    sv[1:2] = jnp.sum(upstream, axis=0, keepdims=True)
+    sv[2:3] = jnp.sum(du, axis=0, keepdims=True)
+
+    def feed_back(half, part):
+        made = nn(dub[half].reshape(2 * quarter, width), wf[1].reshape(width, width))
+        made = made * gelu_d[half].reshape(2 * quarter, width)
+        dzb[half] = made.astype(BF).reshape(2, quarter, width)
+        back = nt(made.astype(BF), wf[0].reshape(width, width))
+        part[...] = back.reshape(2, quarter, width)
+        return jnp.sum(made, axis=0, keepdims=True)
+
+    rows_u.near()
+    up_sum = feed_back(near, part_m)
+    sum_b = RowSum(1)
+    sum_b.own_half()
+    rows_u.middle()
+    rows_u.far()
+    up_sum = up_sum + feed_back(away, part_o)
+    sum_b.hand(1, part_o[1 - c])
+    sum_b.hand(2, part_o[c] + sum_b.take(1))
+    rank_rows = lax.broadcasted_iota(jnp.int32, (4, width), 0)
+    sv[6:10] = jnp.where(rank_rows == j, up_sum, 0.0)
+
+    ry_b = net.bank(2)
+    theirs = pl.ds(4 * (1 - y), 4)
+    ours = pl.ds(4 * y, 4)
+    for i, (left, right) in ((1, (dub, gl)), (0, (act, dzb))):
+        made = tn(left[...].reshape(4 * quarter, width), right[...].reshape(4 * quarter, width))
+        grad[i] = made.astype(BF).reshape(8, strip, width)
+        net.start(grad.at[i, theirs], ry.at[i], ry_b + i, (yn, t))
+
+    da = du_s[...] + sum_b.total()
+    normal = n1_s[...]
+    dh = norm_rows_back(da, normal, r1_s[:, :1], ag_ref[...][None])
+    dh_s[...] = dh
+    dhb = dh.astype(BF)
+    dc_z = net.bank(4)
+    for k in range(1, 4):
+        s = (t + k) % 4
+        dct[s] = nn(dhb, wo[s].reshape(width, local)).astype(BF)
+        net.start(dct.at[s], dc.at[t], dc_z + t, (d, s))
+    dc[t] = nn(dhb, wo[t].reshape(width, local)).astype(BF)
+    sv[3:4] = jnp.sum(da * normal, axis=0, keepdims=True)
+    sv[4:5] = jnp.sum(da, axis=0, keepdims=True)
+    sv[5:6] = jnp.sum(dh, axis=0, keepdims=True)
+    for s in range(4):
+        made = tn(dhb, ct[s]).astype(BF).reshape(4, 2, strip, local)
+        for i in range(2):
+            go[i, :, s] = made[:, i]
+    go_b = net.bank(1)
+    net.start(go.at[1 - c], go_r, go_b, (sib, t))
+
+    rx_b = net.bank(4)
+    for i in (1, 0):
+        net.wait(ry.at[i], ry_b + i)
+        fs_b[:, i] = (grad[i, ours].astype(F32) + ry[i].astype(F32)).astype(BF)
+    for r in (sib, xn, flip_x(sib)):
+        net.start(fs_b.at[r % 4], rx.at[j], rx_b + j, (r, t))
+    rx[j] = fs_b[j]
+
+    net.wait(go_r, go_b)
+    so[...] = (go[c].astype(F32) + go_r[...].astype(F32)).astype(BF)
+    rp_b = net.bank(4)
+    for r in (xn, yn, dg):
+        net.start(so.at[r // 2], rp.at[chip], rp_b + chip, (r, t))
+    rp[chip] = so[chip]
+
+    for k in range(1, 4):
+        s = (t + k) % 4
+        net.wait(dc.at[s], dc_z + s)
+    dctx = dc[...].reshape(rows, local)
+    for h in range(heads):
+        dco[:, BLOCK * h : BLOCK * (h + 1)] = jnp.concatenate(
+            [jnp.zeros((rows, HD), BF), dctx[:, HD * h : HD * (h + 1)]], axis=1
+        )
+    for h in range(heads):
+        dkk[h][...] = jnp.zeros((rows, BLOCK), F32)
+        dvv[h][...] = jnp.zeros((rows, BLOCK), F32)
+    for b in range(blocks):
+        lo, hi = span(b)
+        at_q = slice(BLOCK * b, BLOCK * (b + 1))
+        for h in range(heads):
+            at = slice(BLOCK * h, BLOCK * (h + 1))
+            weights = probs[h, kept[b] : kept[b + 1]]
+            dp = nt(kv[lo:hi, at], dco[at_q, at])
+            ds = weights * (dp - jnp.sum(weights * dp, axis=0, keepdims=True))
+            dsb = ds.astype(BF)
+            dkk[h][lo:hi] += nn(dsb, qq[at_q, at])
+            dvv[h][lo:hi] += nn(weights.astype(BF), dco[at_q, at])
+            dqq[h][at_q] = nn(kkt[h, :, lo:hi], dsb).T * SCALING
+
+    fr_b = net.bank(4)
+    for m in range(4):
+        r = (j + m) % 4
+        if m:
+            net.wait(rx.at[r], rx_b + r)
+        net.start(rx.at[r], fr.at[t], fr_b + t, (d, r), when=r != t)
+    fr[t] = rx[t]
+
+    for h in range(heads):
+        base = 6 * HD * h
+        first = jnp.where(is_word, dqq[h][...], 0.0)
+        second = jnp.where(is_word, 0.0, dqq[h][...])
+        keys = dkk[h][...]
+        keys = jnp.where(is_word, keys, pltpu.roll(keys, HD, 1)) * SCALING
+        third = jnp.where(low_half, keys, dvv[h][...])
+        for i, part in enumerate((first, second, third)):
+            at = slice(base + BLOCK * i, base + BLOCK * (i + 1))
+            dqkv[:, at] = part.astype(BF)
+            row, col = divmod(base + BLOCK * i, width)
+            sv[10 + row : 11 + row, col : col + BLOCK] = jnp.sum(part, axis=0, keepdims=True)
+
+    made = nt(dqkv[...], wq[...].reshape(width, 6 * local))
+    dxp[...] = made.astype(BF).reshape(4, quarter, width)
+    dx_z = net.bank(4)
+    for k in range(1, 4):
+        s = (t + k) % 4
+        net.start(dxp.at[s], dxr.at[t], dx_z + t, (d, s))
+    vb8[d] = sv[...]
+    sv_b = net.bank(8)
+    for m in range(1, 8):
+        net.start(sv, vb8.at[d], sv_b + d, ((d + m) % 8, t))
+
+    made = nn(xt[...], dqkv[...]).astype(BF).reshape(4, 2, strip, 6 * local)
+    for i in range(2):
+        gq[i] = made[:, i]
+    gq_b = net.bank(1)
+    net.start(gq.at[1 - c], gq_r, gq_b, (sib, t))
+
+    for r in (xn, yn, dg):
+        net.wait(rp.at[r // 2], rp_b + r // 2)
+    total = rp[0].astype(F32)
+    for k in range(1, 4):
+        total = total + rp[k].astype(F32)
+    sp[...] = total.astype(BF)
+    rz_b = net.bank(4)
+    for k in range(1, 4):
+        s = (t + k) % 4
+        net.start(sp.at[s], rz.at[t], rz_b + t, (d, s))
+    rz[t] = sp[t]
+
+    net.wait(gq_r, gq_b)
+    sq[...] = (gq[c].astype(F32) + gq_r[...].astype(F32)).astype(BF)
+    gp_b = net.bank(4)
+    for r in (xn, yn, dg):
+        net.start(sq.at[r // 2], gp.at[chip], gp_b + chip, (r, t))
+    gp[chip] = sq[chip]
+
+    for m in range(1, 8):
+        s = (d + m) % 8
+        net.wait(vb8.at[s], sv_b + s)
+    total = vb8[0]
+    for m in range(1, 8):
+        total = total + vb8[m]
+    sw[...] = total
+    vz_b = net.bank(4)
+    for k in range(1, 4):
+        net.start(sw, vz.at[t], vz_b + t, (d, (t + k) % 4))
+    vz[t] = sw[...]
+
+    for k in range(1, 4):
+        s = (t + k) % 4
+        net.wait(dxr.at[s], dx_z + s)
+    total = dxp[t].astype(F32) + dh_s[...]
+    for k in range(1, 4):
+        total = total + dxr[(t + k) % 4].astype(F32)
+    ig_ref[0, own_rows, :] = total.astype(BF)
+    ig_z = net.bank(4)
+    for k in range(1, 4):
+        net.start(ig_ref.at[0, own_rows], ig_ref.at[0, own_rows], ig_z + t, (d, (t + k) % 4))
+
+    for k in range(1, 4):
+        s = (t + k) % 4
+        net.wait(vz.at[s], vz_b + s)
+    total = vz[0]
+    for s in range(1, 4):
+        total = total + vz[s]
+    up_total = jnp.sum(jnp.where(rank_rows == t, total[6:10], 0.0), axis=0, keepdims=True)
+    small_ref[0:6] = total[0:6]
+    small_ref[6:7] = up_total
+    small_ref[8:10] = sw[10:12]
+
+    for k in range(1, 4):
+        s = (t + k) % 4
+        net.wait(fr.at[s], fr_b + s)
+    total = fr[0].astype(F32)
+    for s in range(1, 4):
+        total = total + fr[s].astype(F32)
+    ug_ref[...] = total[0]
+    dg_ref[...] = total[1]
+
+    for k in range(1, 4):
+        s = (t + k) % 4
+        net.wait(rz.at[s], rz_b + s)
+    total = rz[0].astype(F32)
+    for s in range(1, 4):
+        total = total + rz[s].astype(F32)
+    og_ref[...] = wide_t(total, BLOCK, 256)[:local, :strip]
+
+    for r in (xn, yn, dg):
+        net.wait(gp.at[r // 2], gp_b + r // 2)
+    total = gp[0].astype(F32)
+    for k in range(1, 4):
+        total = total + gp[k].astype(F32)
+    for h in range(heads):
+        base = 6 * HD * h
+        at = slice(HD * h, HD * (h + 1))
+        for i in range(4):
+            qg_ref[i, :, at] = total[:, base + HD * i : base + HD * (i + 1)]
+        kg_ref[:, at] = total[:, base + 4 * HD : base + 5 * HD]
+        vg_ref[:, at] = total[:, base + 5 * HD : base + 6 * HD]
+
+    for k in range(1, 4):
+        s = (t + k) % 4
+        rows_s = pl.ds(pl.multiple_of(s * quarter, 16), quarter)
+        net.wait(out_ref.at[0, rows_s], out_z + s)
+        net.wait(ig_ref.at[0, rows_s], ig_z + s)
+    net.drain()
+
+
+def end_kernel(*refs):
+    sources, small = refs[:8], refs[8]
+    targets, (qbg, vbg), vectors = refs[9:17], refs[17:19], refs[19:26]
+    for source, target in zip(sources, targets):
+        target[...] = source[...]
+    fgg, fsg, dbg, agg, asg, obg, ubg = (small[i] for i in range(7))
+    for ref, value in zip(vectors, (obg, ubg, dbg, agg, asg, fgg, fsg)):
+        ref[...] = value
+    width = small.shape[1]
+    values = []
+    for h in range(vbg.shape[0] // HD):
+        row, col = divmod(6 * HD * h, width)
+        piece = small[8 + row : 9 + row, col : col + 6 * HD]
+        for i in range(4):
+            qbg[i : i + 1, HD * h : HD * (h + 1)] = piece[:, HD * i : HD * (i + 1)]
+        values.append(piece[:, 5 * HD :])
+    vbg[...] = jnp.concatenate(values, axis=1)[0]
+
+
+def fused(
+    layer_input, segment_ids, token_types, query_weight, key_weight, value_weight, out_weight,
+    up_weight, down_weight, query_bias, value_bias, out_bias, up_bias, down_bias, attn_gain,
+    attn_shift, ffn_gain, ffn_shift, cotangent,
+):
+    rows, width = layer_input.shape[1:]
+    strip, local = key_weight.shape
+    quarter, heads, blocks = rows // 4, local // HD, rows // BLOCK
+    kept = sum(BLOCK * (min(blocks, b + 3) - max(0, b - 2)) for b in range(blocks))
+    args = [
+        layer_input, segment_ids, token_types, query_weight, key_weight, value_weight, out_weight,
+        up_weight, down_weight.T, query_bias, value_bias, out_bias, up_bias, down_bias, attn_gain,
+        attn_shift, ffn_gain, ffn_shift, cotangent,
+    ]
+
+    def like(v, dtype=F32):
+        return jax.ShapeDtypeStruct(v.shape, dtype)
+
+    outs = [
+        like(layer_input, BF), like(layer_input, BF), like(query_weight), like(key_weight),
+        like(value_weight), like(out_weight), like(up_weight), jax.ShapeDtypeStruct((strip, width), F32),
+        jax.ShapeDtypeStruct((16, width), F32),
+    ]
+    v = pltpu.VMEM
+    scratch = [
+        v((8, strip, 6 * local), BF), v((4, 8, strip, local), BF), v((2, strip, width), BF),
+        v((2, 8, strip, width), BF), v((4, 8, width), F32), v((rows, BLOCK), F32),
+        v((rows, BLOCK), F32), v((width, rows), BF), v((1, 6 * local), F32),
+        v((rows, heads * BLOCK), BF), v((rows, heads * BLOCK), BF), v((rows, heads * BLOCK), BF),
+        v((heads, BLOCK, rows), BF), v((heads, BLOCK, rows), BF),
+        v((heads, kept, BLOCK), F32), v((rows, local), BF), v((4, quarter, local), BF),
+        v((quarter, width), F32), v((quarter, width), F32), v((quarter, BLOCK), F32),
+        v((4, quarter, width), BF), v((4, quarter, width), F32), v((4, quarter, width), BF),
+        v((4, quarter, width), F32),
+        v((6, quarter, width), BF), v((6, quarter, width), BF),
+        v((quarter, width), F32), v((4, quarter, width), BF), v((4, quarter, width), BF),
+        v((2, 8, strip, width), BF), v((2, 4, strip, width), BF), v((4, 2, strip, width), BF),
+        v((4, 2, strip, width), BF), v((4, 2, strip, width), BF),
+        v((quarter, width), F32), v((4, quarter, local), BF), v((4, quarter, local), BF),
+        v((rows, heads * BLOCK), BF),
+        v((2, 4, 4, strip, local), BF), v((4, 4, strip, local), BF), v((4, 4, strip, local), BF),
+        v((4, 4, strip, local), BF), v((4, strip, local), BF), v((4, strip, local), BF),
+        v((rows, 6 * local), BF), v((4, quarter, width), BF), v((4, quarter, width), BF),
+        v((2, 4, strip, 6 * local), BF), v((4, strip, 6 * local), BF),
+        v((4, strip, 6 * local), BF), v((4, strip, 6 * local), BF),
+        v((16, width), F32), v((8, 16, width), F32), v((16, width), F32), v((4, 16, width), F32),
+        pltpu.SemaphoreType.DMA((SENDS,)), pltpu.SemaphoreType.DMA((RECVS,)),
+    ]
+    spec = pl.BlockSpec(memory_space=pltpu.VMEM)
+    made = pl.pallas_call(
+        layer_kernel,
+        out_shape=outs,
+        in_specs=[spec] * len(args),
+        out_specs=[spec] * len(outs),
+        scratch_shapes=scratch,
+        compiler_params=pltpu.CompilerParams(
+            collective_id=0, has_side_effects=True, vmem_limit_bytes=58 << 20
+        ),
+        name="layer",
+    )(*args)
+    *large, small = made
+    vector = jax.ShapeDtypeStruct((width,), F32)
+    ended = pl.pallas_call(
+        end_kernel,
+        out_shape=[like(v, v.dtype) for v in large]
+        + [like(query_bias), jax.ShapeDtypeStruct((local,), F32)]
+        + [vector] * 7,
+        in_specs=[spec] * len(made),
+        out_specs=[spec] * 17,
+        name="finish",
+    )(*large, small)
+    return (*ended[:7], ended[7].T, *ended[8:])
+
+
 def solution(mesh):
     in_specs = (
         P("dp", None, None),
@@ -363,4 +1084,5 @@
         P(),
         P(),
     )
-    return jax.shard_map(shards, mesh=mesh, in_specs=in_specs, out_specs=out_specs, check_vma=False)
+    step = fused if fits(mesh) else shards
+    return jax.shard_map(step, mesh=mesh, in_specs=in_specs, out_specs=out_specs, check_vma=False)

time: 610 us -> 213 us (0.35)
  the two profiles are of different devices: /device:TPU:0 before, /device:TPU:17 now
where the time goes in v1:
time: 213 us
  Pallas kernels  212 us (100%)
    pallas_call x1, Pallas kernels, fused(): pl.pallas_call(layer_kernel, out_shape=outs, in_specs=[spec] * len(args),...  209 us

profile of v1, /device:TPU:17, one launch (start us, length us, event | category | flops | bytes accessed | tf_op | source)
XLA Modules:
  0.0 213.1 jit_solution(3941167603632946204)
XLA Ops:
  0.7 208.6 %layer.1 = (bf16[1,640,768]{2,1,0:T(8,128)(2,1)}, bf16[1,640,768]{2,1,0:T(8,128)(2,1)}, f32[4,96,192]{2,1,0:T(8,128)}, f32[96,192]{1,0:T(8,128)}, f32[96,192]{1,...) custom-call(bf16[1,640,768]{2,1,0:T(8,128)(2,1)} %x_ref.1, ...), custom_call_target="tpu_custom_call" | custom-call | tf_op jit(solution)/shard_map/layer/pallas_call | solution.py:1021
  209.3 3.6 %finish.1 = (bf16[1,640,768]{2,1,0:T(8,128)(2,1)}, bf16[1,640,768]{2,1,0:T(8,128)(2,1)}, f32[4,96,192]{2,1,0:T(8,128)}, f32[96,192]{1,0:T(8,128)}, f32[96,192]{1...) custom-call(bf16[1,640,768]{2,1,0:T(8,128)(2,1)} %get-tuple-element., ...), custom_call_target="tpu_custom_call" | custom-call | tf_op jit(solution)/shard_map/finish/pallas_call | solution.py:1034

commit v2 on v1

--- a/solution.py
+++ b/solution.py
@@ -373,7 +373,7 @@
         self.banks += count
         return base
 
-    def start(self, src, dst, sem, device, when=None):
+    def start(self, src, dst, sem, device, when=None, group=None):
         slot = self.sends
         self.sends += 1
 
@@ -391,7 +391,7 @@
             make().start()
         else:
             pl.when(when)(lambda: make().start())
-        self.pending.append((make, when))
+        self.pending.append((make, when, group))
 
     def wait(self, dst, sem, when=None):
         def make():
@@ -409,27 +409,29 @@
         else:
             pl.when(when)(lambda: make().wait_recv())
 
-    def drain(self):
-        for make, when in self.pending:
+    def settle(self, *groups):
+        for make, when, group in self.pending:
+            if groups and group not in groups:
+                continue
             if when is None:
                 make().wait_send()
             else:
                 pl.when(when)(lambda make=make: make().wait_send())
-        self.pending = []
-
-
-SENDS = 120
-RECVS = 160
+        self.pending = [p for p in self.pending if groups and p[2] not in groups]
+
+
+SENDS = 192
+RECVS = 224
 
 
 def layer_kernel(
     x_ref, seg_ref, typ_ref, qw_ref, kw_ref, vw_ref, ow_ref, uw_ref, dw_ref, qb_ref, vb_ref,
     ob_ref, ub_ref, db_ref, ag_ref, as_ref, fg_ref, fs_ref, cot_ref,
     out_ref, ig_ref, qg_ref, kg_ref, vg_ref, og_ref, ug_ref, dg_ref, small_ref,
-    wq, wo, own, wf, ubs, segc, wordc, xt, bias, qq, kv, kk, kvt, kkt, probs, ctx, ct,
-    a_s, n1_s, r1_s, act, gelu_d, gl, parts, rs_send, rs_recv, du_s, dub, dzb,
-    grad, ry, fs_b, rx, fr, dh_s, dct, dc, dco, go, go_r, so, rp, sp, rz,
-    dqkv, dxp, dxr, gq, gq_r, sq, gp, sv, vb8, sw, vz,
+    wq, wo, own, own_y, wf, ubs, segc, wordc, xt, bias, qq, kv, kk, kvt, kkt, probs, ctx, ct,
+    a_s, n1_s, r1_s, act, gelu_d, gl, parts, rs_send, rs_recv, dub, dzb,
+    ry, rx, fr_in, fr_cross, fr_back, dct, dc, dco, go_r, rp, sp, rz,
+    dqkv, dx_in, dx_cross, dx_back, gq_r, gp, sv, vb8, sw, vz,
     send_sems, recv_sems,
 ):
     d = lax.axis_index("dp")
@@ -465,15 +467,90 @@
     dkk = [sums_a.at[:, BLOCK * (heads + h) : BLOCK * (heads + h + 1)] for h in range(heads)]
     dvv = [sums_b.at[:, BLOCK * h : BLOCK * (h + 1)] for h in range(heads)]
 
+    low_z = t < 2
+    is_end = jnp.logical_or(t == 0, t == 3)
+    is_mid = jnp.logical_not(is_end)
+    z_out = jnp.where(low_z, t + 1, t - 1)
+    z_back = jnp.where(low_z, 0, 3)
+
+    def place(e):
+        return jnp.where(low_z, e, 3 - e)
+
+    def joint(one, other):
+        return other if one is None else jnp.logical_and(one, other)
+
+    class LineGather:
+        def __init__(self, view, group=None):
+            self.view, self.bank, self.group = view, net.bank(4), group
+
+        def copy(self, owner, to, when):
+            ref = self.view(owner)
+            net.start(ref, ref, self.bank + owner, (d, to), when=when, group=self.group)
+
+        def wait(self, owner, when=None):
+            net.wait(self.view(owner), self.bank + owner, when=when)
+
+        def begin(self):
+            self.copy(t, z_out, None)
+            self.copy(t, z_back, is_mid)
+
+        def step(self, n):
+            if n == 1:
+                self.wait(place(0), is_mid)
+                self.copy(place(0), z_out, is_mid)
+                self.wait(place(2), is_mid)
+                self.copy(place(2), z_back, is_mid)
+            if n == 2:
+                self.wait(place(3), is_mid)
+                self.copy(place(3), z_back, is_mid)
+            self.wait(place(n), is_end)
+
+    def new_owners(n):
+        if n == 0:
+            return ((t, None),)
+        if n == 1:
+            return ((jnp.where(is_mid, place(0), place(1)), None), (place(2), is_mid))
+        return ((jnp.where(is_mid, place(3), place(2)), None),) if n == 2 else ((place(3), is_end),)
+
+    class LineReduce:
+        def __init__(self, own, came, cross, back):
+            self.own, self.came, self.cross, self.back = own, came, cross, back
+            self.in_b, self.cross_b, self.back_b = net.bank(4), net.bank(4), net.bank(1)
+
+        def begin(self):
+            for e in (3, 2, 1):
+                net.start(self.own(e), self.came.at[e - 1], self.in_b + e, (d, z_out), when=is_end)
+
+        def add(self, e, ref):
+            @pl.when(is_mid)
+            def _():
+                ref[...] = (self.own(e)[...].astype(F32) + ref[...].astype(F32)).astype(BF)
+
+        def through(self, e):
+            ref = self.came.at[e - 1]
+            net.wait(ref, self.in_b + e, when=is_mid)
+            self.add(e, ref)
+            net.start(ref, self.cross.at[3 - e], self.cross_b + 3 - e, (d, z_out), when=is_mid)
+
+        def pass_back(self):
+            net.wait(self.cross.at[0], self.cross_b, when=is_mid)
+            self.add(0, self.cross.at[0])
+            net.start(self.cross.at[0], self.back, self.back_b, (d, z_back), when=is_mid)
+
+        def total(self):
+            net.wait(self.came.at[0], self.in_b + 1, when=is_mid)
+            net.wait(self.cross.at[1], self.cross_b + 1, when=is_mid)
+            net.wait(self.back, self.back_b, when=is_end)
+            others = self.came[0].astype(F32) + self.cross[1].astype(F32)
+            mine = self.own(jnp.where(is_mid, 1, 0))[...].astype(F32)
+            return mine + jnp.where(is_mid, others, self.back[...].astype(F32))
+
     barrier = pltpu.get_barrier_semaphore()
     for m in range(1, 8):
         pl.semaphore_signal(barrier, 1, device_id=((d + m) % 8, t), device_id_type=MESH)
     for k in range(1, 4):
-        for m in range(4):
-            pl.semaphore_signal(
-                barrier, 1, device_id=(4 * y + (j + m) % 4, (t + k) % 4), device_id_type=MESH
-            )
-    pl.semaphore_wait(barrier, 19)
+        pl.semaphore_signal(barrier, 1, device_id=(d, (t + k) % 4), device_id_type=MESH)
+    pl.semaphore_wait(barrier, 10)
 
     for h in range(heads):
         at = slice(HD * h, HD * (h + 1))
@@ -483,26 +560,42 @@
         wq[d, :, 6 * HD * h : 6 * HD * (h + 1)] = piece.astype(BF)
 
     class PlaneGather:
-        def __init__(self, ref_of):
-            self.ref_of, self.bank = ref_of, net.bank(8)
-
-        def copy(self, block, device):
-            net.start(self.ref_of(block), self.ref_of(block), self.bank + block, (device, t))
+        def __init__(self, group, *views):
+            self.views, self.bank, self.group = views, net.bank(8 * len(views)), group
+
+        def copy(self, view, block, device):
+            ref = self.views[view](block)
+            net.start(ref, ref, self.bank + 8 * view + block, (device, t), group=self.group)
+
+        def wait(self, view, block):
+            net.wait(self.views[view](block), self.bank + 8 * view + block)
 
         def begin(self):
-            for device in (xn, yn, dg, sib):
-                self.copy(d, device)
+            for view, device in ((0, yn), (1, xn), (1, yn), (0, xn), (0, sib), (1, sib)):
+                self.copy(view, d, device)
 
         def middle(self):
-            for block in (xn, yn, dg):
-                net.wait(self.ref_of(block), self.bank + block)
-                self.copy(block, sib)
+            self.wait(0, yn)
+            self.copy(0, yn, xn)
+            self.wait(1, xn)
+            self.copy(1, xn, yn)
+            self.copy(0, yn, sib)
+            self.copy(1, xn, sib)
+            for view, block in ((1, yn), (0, xn)):
+                self.wait(view, block)
+                self.copy(view, block, sib)
+
+        def late(self):
+            for view in range(2):
+                self.wait(view, dg)
+                self.copy(view, dg, sib)
 
         def end(self):
             for block in (sib, flip_x(sib), flip_y(sib), flip_x(flip_y(sib))):
-                net.wait(self.ref_of(block), self.bank + block)
-
-    gather_q = PlaneGather(lambda b: wq.at[b])
+                for view in range(len(self.views)):
+                    self.wait(view, block)
+
+    gather_q = PlaneGather("q", lambda b: wq.at[b, : strip // 2], lambda b: wq.at[b, strip // 2 :])
     gather_q.begin()
 
     def wide_t(value, high, wide):
@@ -514,29 +607,35 @@
         return value.T
 
     wo[t, d] = wide_t(ow_ref[...], 256, 128)[:strip, :local].astype(BF)
-    own[0] = uw_ref[...].astype(BF)
-    own[1] = dw_ref[...].astype(BF)
+    own[0, t] = uw_ref[...].astype(BF)
+    own[1, t] = dw_ref[...].astype(BF)
     ubs[t] = jnp.broadcast_to(ub_ref[...][None], ubs.shape[1:])
 
-    wo_z = net.bank(4)
     ub_z = net.bank(4)
-    wf_z = net.bank(8)
+    wf_x = net.bank(16)
     wf_y = net.bank(8)
+
+    line_o = LineGather(lambda s: wo.at[s, d], "o")
+    line_f = [LineGather(lambda s, i=i: own.at[i, s]) for i in range(2)]
+
+    def hop_x(i, source, row, s, when=None):
+        target = wf.at[i, row]
+        sem = wf_x + 8 * i + row
+        net.start(source, target, sem, (4 * y + s, t), when=joint(when, s != j))
+
+        @pl.when(joint(when, s == j))
+        def _():
+            target[...] = source[...]
+
+    def hop_y(n):
+        for s, when in new_owners(n):
+            net.start(own.at[0, s], own_y.at[s], wf_y + s, (yn, t), when=when)
+
+    line_o.begin()
+    line_f[0].begin()
+    hop_y(0)
     for k in range(1, 4):
-        s = (t + k) % 4
-        net.start(wo.at[t, d], wo.at[t, d], wo_z + t, (d, s))
-        net.start(ubs.at[t], ubs.at[t], ub_z + t, (d, s))
-    mine = j == t
-    for i in range(2):
-        for k in range(1, 4):
-            net.start(own.at[i], wf.at[i, d], wf_z + 4 * i + j, (4 * y + t, (t + k) % 4))
-        net.start(own.at[i], wf.at[i, d], wf_z + 4 * i + j, (4 * y + t, t), when=jnp.logical_not(mine))
-
-    @pl.when(mine)
-    def _():
-        for i in range(2):
-            wf[i, d] = own[i]
-
+        net.start(ubs.at[t], ubs.at[t], ub_z + t, (d, (t + k) % 4))
     for b in range(blocks):
         at = slice(BLOCK * b, BLOCK * (b + 1))
         segc[at, :] = jnp.broadcast_to(seg_ref[:, at].astype(F32), (BLOCK, BLOCK)).T
@@ -550,8 +649,15 @@
         )
 
     gather_q.middle()
+    line_o.step(1)
+    line_f[0].step(1)
+    hop_y(1)
+    line_f[1].begin()
+    gather_q.late()
+    line_o.step(2)
+    line_f[0].step(2)
+    hop_y(2)
     gather_q.end()
-
     low_half = lax.broadcasted_iota(jnp.int32, (rows, BLOCK), 1) < HD
     is_word = wordc[...] > 0.5
     for h in range(heads):
@@ -565,15 +671,18 @@
         keys = jnp.where(jnp.logical_xor(is_word, low_half), 0.0, keys)
         kv[:, at] = both.astype(BF)
         kk[:, at] = keys.astype(BF)
-        kvt[h] = both.T.astype(BF)
+        kvt[h] = both.T[HD:].astype(BF)
         kkt[h] = keys.T.astype(BF)
 
-    gather_o = PlaneGather(lambda b: wo.at[:, b])
-    for k in range(1, 4):
-        s = (t + k) % 4
-        net.wait(wo.at[s, d], wo_z + s)
+    line_o.step(3)
+    line_f[0].step(3)
+    hop_y(3)
+    gather_o = PlaneGather("o", lambda b: wo.at[0:2, b], lambda b: wo.at[2:4, b])
     gather_o.begin()
-
+    for n in range(4):
+        for s, when in new_owners(n):
+            hop_x(0, own.at[0, s], d, s, when)
+    line_f[1].step(1)
     ct_z = net.bank(4)
 
     def span(b):
@@ -594,24 +703,27 @@
             weights = jnp.exp(scores - jnp.max(scores, axis=0, keepdims=True))
             weights = weights * (1.0 / jnp.sum(weights, axis=0, keepdims=True))
             probs[h, kept[b] : kept[b + 1]] = weights
-            found.append(nn(kvt[h, HD:, lo:hi], weights.astype(BF)))
+            found.append(nn(kvt[h, :, lo:hi], weights.astype(BF)))
         found.append(jnp.zeros((HD, BLOCK), F32))
         ctx[at_q, :] = jnp.concatenate(found, axis=0).T[:, :local].astype(BF)
+        if b == 2:
+            line_f[1].step(2)
         if b > 0:
             s = b - 1
             src = ctx.at[quarter * s : quarter * (s + 1)]
             net.start(src, ct.at[t], ct_z + t, (d, s), when=t != s)
     ct[t] = ctx[own_rows, :]
 
+    line_f[1].step(3)
+    for n in range(4):
+        for s, when in new_owners(n):
+            hop_x(1, own.at[1, s], d, s, when)
     gather_o.middle()
-
-    for i in range(1):
-        for m in range(4):
-            r = (j + m) % 4
-            net.wait(wf.at[i, 4 * y + r], wf_z + 4 * i + r, when=jnp.logical_or(r != j, j != t))
-            net.start(wf.at[i, 4 * y + r], wf.at[i, 4 * y + r], wf_y + 4 * i + r, (yn, t))
+    for s in range(4):
+        net.wait(own_y.at[s], wf_y + s)
+        hop_x(0, own_y.at[s], yn, s)
+    gather_o.late()
     gather_o.end()
-
     for k in range(1, 4):
         s = (t + k) % 4
         net.wait(ct.at[s], ct_z + s)
@@ -625,6 +737,11 @@
     a_s[...] = normed
     act[j] = normed.astype(BF)
 
+    def rows_of(ref, first, count):
+        return lambda owner: ref.at[
+            0, pl.ds(pl.multiple_of(owner * quarter + first, 16), count)
+        ]
+
     class RowGather:
         def __init__(self, ref):
             self.ref, self.bank = ref, net.bank(4)
@@ -674,20 +791,19 @@
 
     rows_a = RowGather(act)
     rows_a.begin()
-    for i in range(1, 2):
-        for m in range(4):
-            r = (j + m) % 4
-            net.wait(wf.at[i, 4 * y + r], wf_z + 4 * i + r, when=jnp.logical_or(r != j, j != t))
-            net.start(wf.at[i, 4 * y + r], wf.at[i, 4 * y + r], wf_y + 4 * i + r, (yn, t))
+    for m in range(4):
+        r = 4 * y + (j + m) % 4
+        if m:
+            net.wait(wf.at[1, r], wf_x + 8 + r)
+        net.start(wf.at[1, r], wf.at[1, r], wf_y + 4 + (j + m) % 4, (yn, t), group="f")
     rows_a.middle()
     rows_a.near()
     for k in range(1, 4):
         s = (t + k) % 4
         net.wait(ubs.at[s], ub_z + s)
-    for m in range(4):
-        r = 4 * (1 - y) + (j + m) % 4
-        net.wait(wf.at[0, r], wf_y + (j + m) % 4)
-
+    for m in range(1, 4):
+        for r in (4 * y + (j + m) % 4, 4 * (1 - y) + (j + m) % 4):
+            net.wait(wf.at[0, r], wf_x + r)
     near = pl.ds(2 * x, 2)
     away = pl.ds(2 - 2 * x, 2)
 
@@ -719,15 +835,14 @@
 
     normal, inverse = norm_rows(a_s[...] + ffn_out)
     out_ref[0, own_rows, :] = (normal * fg_ref[...][None] + fs_ref[...][None]).astype(BF)
-    out_z = net.bank(4)
-    for k in range(1, 4):
-        net.start(out_ref.at[0, own_rows], out_ref.at[0, own_rows], out_z + t, (d, (t + k) % 4))
+    line_out = LineGather(rows_of(out_ref, 0, quarter))
+    line_out.begin()
     upstream = cot_ref[0, own_rows, :].astype(F32)
     du = norm_rows_back(upstream, normal, inverse, fg_ref[...][None])
     dub[j] = du.astype(BF)
     rows_u = RowGather(dub)
     rows_u.begin()
-    du_s[...] = du
+    a_s[...] = du
     sv[...] = jnp.zeros_like(sv)
     sv[0:1] = jnp.sum(upstream * normal, axis=0, keepdims=True)
     sv[1:2] = jnp.sum(upstream, axis=0, keepdims=True)
@@ -745,6 +860,7 @@
     up_sum = feed_back(near, part_m)
     sum_b = RowSum(1)
     sum_b.own_half()
+    line_out.step(1)
     rows_u.middle()
     rows_u.far()
     up_sum = up_sum + feed_back(away, part_o)
@@ -756,15 +872,19 @@
     ry_b = net.bank(2)
     theirs = pl.ds(4 * (1 - y), 4)
     ours = pl.ds(4 * y, 4)
-    for i, (left, right) in ((1, (dub, gl)), (0, (act, dzb))):
+    def feed_grad(i, left, right):
         made = tn(left[...].reshape(4 * quarter, width), right[...].reshape(4 * quarter, width))
-        grad[i] = made.astype(BF).reshape(8, strip, width)
-        net.start(grad.at[i, theirs], ry.at[i], ry_b + i, (yn, t))
-
-    da = du_s[...] + sum_b.total()
+        wf[i] = made.astype(BF).reshape(8, strip, width)
+
+    net.settle("f")
+    feed_grad(1, dub, gl)
+    net.start(wf.at[1, theirs], ry.at[1], ry_b + 1, (yn, t))
+    feed_grad(0, act, dzb)
+    da = a_s[...] + sum_b.total()
+    line_out.step(2)
     normal = n1_s[...]
     dh = norm_rows_back(da, normal, r1_s[:, :1], ag_ref[...][None])
-    dh_s[...] = dh
+    a_s[...] = dh
     dhb = dh.astype(BF)
     dc_z = net.bank(4)
     for k in range(1, 4):
@@ -772,30 +892,25 @@
         dct[s] = nn(dhb, wo[s].reshape(width, local)).astype(BF)
         net.start(dct.at[s], dc.at[t], dc_z + t, (d, s))
     dc[t] = nn(dhb, wo[t].reshape(width, local)).astype(BF)
+    net.start(wf.at[0, theirs], ry.at[0], ry_b, (yn, t))
     sv[3:4] = jnp.sum(da * normal, axis=0, keepdims=True)
     sv[4:5] = jnp.sum(da, axis=0, keepdims=True)
     sv[5:6] = jnp.sum(dh, axis=0, keepdims=True)
+    net.settle("o")
     for s in range(4):
-        made = tn(dhb, ct[s]).astype(BF).reshape(4, 2, strip, local)
-        for i in range(2):
-            go[i, :, s] = made[:, i]
+        wo[s] = tn(dhb, ct[s]).astype(BF).reshape(8, strip, local)
+    by_core = wo.reshape(4, 4, 2, strip, local)
     go_b = net.bank(1)
-    net.start(go.at[1 - c], go_r, go_b, (sib, t))
-
-    rx_b = net.bank(4)
-    for i in (1, 0):
+    net.start(by_core.at[:, :, 1 - c], go_r, go_b, (sib, t))
+
+    rx_b = net.bank(8)
+
+    def over_y(i):
         net.wait(ry.at[i], ry_b + i)
-        fs_b[:, i] = (grad[i, ours].astype(F32) + ry[i].astype(F32)).astype(BF)
-    for r in (sib, xn, flip_x(sib)):
-        net.start(fs_b.at[r % 4], rx.at[j], rx_b + j, (r, t))
-    rx[j] = fs_b[j]
-
-    net.wait(go_r, go_b)
-    so[...] = (go[c].astype(F32) + go_r[...].astype(F32)).astype(BF)
-    rp_b = net.bank(4)
-    for r in (xn, yn, dg):
-        net.start(so.at[r // 2], rp.at[chip], rp_b + chip, (r, t))
-    rp[chip] = so[chip]
+        ry[i] = (wf[i, ours].astype(F32) + ry[i].astype(F32)).astype(BF)
+        for r in (xn, flip_x(sib), sib):
+            net.start(ry.at[i, r % 4], rx.at[i, j], rx_b + 4 * i + j, (r, t))
+        rx[i, j] = ry[i, j]
 
     for k in range(1, 4):
         s = (t + k) % 4
@@ -821,14 +936,7 @@
             dvv[h][lo:hi] += nn(weights.astype(BF), dco[at_q, at])
             dqq[h][at_q] = nn(kkt[h, :, lo:hi], dsb).T * SCALING
 
-    fr_b = net.bank(4)
-    for m in range(4):
-        r = (j + m) % 4
-        if m:
-            net.wait(rx.at[r], rx_b + r)
-        net.start(rx.at[r], fr.at[t], fr_b + t, (d, r), when=r != t)
-    fr[t] = rx[t]
-
+    over_y(1)
     for h in range(heads):
         base = 6 * HD * h
         first = jnp.where(is_word, dqq[h][...], 0.0)
@@ -843,22 +951,95 @@
             sv[10 + row : 11 + row, col : col + BLOCK] = jnp.sum(part, axis=0, keepdims=True)
 
     made = nt(dqkv[...], wq[...].reshape(width, 6 * local))
-    dxp[...] = made.astype(BF).reshape(4, quarter, width)
-    dx_z = net.bank(4)
-    for k in range(1, 4):
-        s = (t + k) % 4
-        net.start(dxp.at[s], dxr.at[t], dx_z + t, (d, s))
+    dzb[...] = made.astype(BF).reshape(4, quarter, width)
+    part = quarter // 2
+    line_dx, line_in = [], []
+    for q in range(2):
+        cut = pl.ds(part * q, part)
+        line_dx.append(
+            LineReduce(
+                lambda e, cut=cut: dzb.at[place(e), cut],
+                dx_in.at[q], dx_cross.at[q], dx_back.at[q],
+            )
+        )
+        line_in.append(LineGather(rows_of(ig_ref, part * q, part)))
+
+    def arrive(q):
+        total = line_dx[q].total() + a_s[part * q : part * (q + 1)]
+        ig_ref[0, pl.ds(pl.multiple_of(t * quarter + part * q, 16), part)] = total.astype(BF)
+        line_in[q].begin()
+
+    line_w = [
+        LineReduce(
+            lambda e, i=i: rx.at[i, place(e)], fr_in.at[i], fr_cross.at[i], fr_back.at[i]
+        )
+        for i in range(2)
+    ]
+
+    def strips_on(i):
+        for m in range(1, 4):
+            r = (j + m) % 4
+            net.wait(rx.at[i, r], rx_b + 4 * i + r)
+        line_w[i].begin()
+
+    line_dx[0].begin()
+    line_dx[1].begin()
     vb8[d] = sv[...]
     sv_b = net.bank(8)
     for m in range(1, 8):
         net.start(sv, vb8.at[d], sv_b + d, ((d + m) % 8, t))
 
-    made = nn(xt[...], dqkv[...]).astype(BF).reshape(4, 2, strip, 6 * local)
-    for i in range(2):
-        gq[i] = made[:, i]
+    net.settle("q")
+    wq[...] = nn(xt[...], dqkv[...]).astype(BF).reshape(8, strip, 6 * local)
+    q_by_core = wq.reshape(4, 2, strip, 6 * local)
     gq_b = net.bank(1)
-    net.start(gq.at[1 - c], gq_r, gq_b, (sib, t))
-
+    net.start(q_by_core.at[:, 1 - c], gq_r, gq_b, (sib, t))
+    line_dx[0].through(3)
+    line_dx[0].through(2)
+    net.wait(go_r, go_b)
+    go_r[...] = (by_core[:, :, c].astype(F32) + go_r[...].astype(F32)).astype(BF)
+    rp_b = net.bank(4)
+    for r in (xn, yn, dg):
+        net.start(go_r.at[:, r // 2], rp.at[chip], rp_b + chip, (r, t))
+    rp[chip] = go_r[:, chip]
+
+    strips_on(1)
+    line_dx[1].through(3)
+    line_dx[1].through(2)
+    line_dx[0].pass_back()
+    over_y(0)
+    net.wait(gq_r, gq_b)
+    gq_r[...] = (q_by_core[:, c].astype(F32) + gq_r[...].astype(F32)).astype(BF)
+    gp_b = net.bank(4)
+    for r in (xn, yn, dg):
+        net.start(gq_r.at[r // 2], gp.at[chip], gp_b + chip, (r, t))
+    gp[chip] = gq_r[chip]
+
+    line_dx[1].pass_back()
+    arrive(0)
+    line_w[1].through(3)
+    line_w[1].through(2)
+    arrive(1)
+    for m in range(1, 8):
+        s = (d + m) % 8
+        net.wait(vb8.at[s], sv_b + s)
+    total = vb8[0]
+    for m in range(1, 8):
+        total = total + vb8[m]
+    sw[...] = total
+    vz_b = net.bank(4)
+    for k in range(1, 4):
+        net.start(sw, vz.at[t], vz_b + t, (d, (t + k) % 4))
+    vz[t] = sw[...]
+
+    line_in[0].step(1)
+    strips_on(0)
+    line_in[1].step(1)
+    line_w[1].pass_back()
+    line_in[0].step(2)
+    line_in[1].step(2)
+    line_w[0].through(3)
+    line_w[0].through(2)
     for r in (xn, yn, dg):
         net.wait(rp.at[r // 2], rp_b + r // 2)
     total = rp[0].astype(F32)
@@ -871,36 +1052,6 @@
         net.start(sp.at[s], rz.at[t], rz_b + t, (d, s))
     rz[t] = sp[t]
 
-    net.wait(gq_r, gq_b)
-    sq[...] = (gq[c].astype(F32) + gq_r[...].astype(F32)).astype(BF)
-    gp_b = net.bank(4)
-    for r in (xn, yn, dg):
-        net.start(sq.at[r // 2], gp.at[chip], gp_b + chip, (r, t))
-    gp[chip] = sq[chip]
-
-    for m in range(1, 8):
-        s = (d + m) % 8
-        net.wait(vb8.at[s], sv_b + s)
-    total = vb8[0]
-    for m in range(1, 8):
-        total = total + vb8[m]
-    sw[...] = total
-    vz_b = net.bank(4)
-    for k in range(1, 4):
-        net.start(sw, vz.at[t], vz_b + t, (d, (t + k) % 4))
-    vz[t] = sw[...]
-
-    for k in range(1, 4):
-        s = (t + k) % 4
-        net.wait(dxr.at[s], dx_z + s)
-    total = dxp[t].astype(F32) + dh_s[...]
-    for k in range(1, 4):
-        total = total + dxr[(t + k) % 4].astype(F32)
-    ig_ref[0, own_rows, :] = total.astype(BF)
-    ig_z = net.bank(4)
-    for k in range(1, 4):
-        net.start(ig_ref.at[0, own_rows], ig_ref.at[0, own_rows], ig_z + t, (d, (t + k) % 4))
-
     for k in range(1, 4):
         s = (t + k) % 4
         net.wait(vz.at[s], vz_b + s)
@@ -912,15 +1063,9 @@
     small_ref[6:7] = up_total
     small_ref[8:10] = sw[10:12]
 
-    for k in range(1, 4):
-        s = (t + k) % 4
-        net.wait(fr.at[s], fr_b + s)
-    total = fr[0].astype(F32)
-    for s in range(1, 4):
-        total = total + fr[s].astype(F32)
-    ug_ref[...] = total[0]
-    dg_ref[...] = total[1]
-
+    line_w[0].pass_back()
+    dg_ref[...] = line_w[1].total()
+    ug_ref[...] = line_w[0].total()
     for k in range(1, 4):
         s = (t + k) % 4
         net.wait(rz.at[s], rz_b + s)
@@ -942,12 +1087,11 @@
         kg_ref[:, at] = total[:, base + 4 * HD : base + 5 * HD]
         vg_ref[:, at] = total[:, base + 5 * HD : base + 6 * HD]
 
-    for k in range(1, 4):
-        s = (t + k) % 4
-        rows_s = pl.ds(pl.multiple_of(s * quarter, 16), quarter)
-        net.wait(out_ref.at[0, rows_s], out_z + s)
-        net.wait(ig_ref.at[0, rows_s], ig_z + s)
-    net.drain()
+    line_out.step(3)
+    for q in range(2):
+        line_in[q].step(3)
+    net.settle()
+    assert net.sends <= SENDS and net.banks <= RECVS, (net.sends, net.banks)
 
 
 def end_kernel(*refs):
@@ -994,25 +1138,27 @@
     ]
     v = pltpu.VMEM
     scratch = [
-        v((8, strip, 6 * local), BF), v((4, 8, strip, local), BF), v((2, strip, width), BF),
+        v((8, strip, 6 * local), BF), v((4, 8, strip, local), BF), v((2, 4, strip, width), BF), v((4, strip, width), BF),
         v((2, 8, strip, width), BF), v((4, 8, width), F32), v((rows, BLOCK), F32),
         v((rows, BLOCK), F32), v((width, rows), BF), v((1, 6 * local), F32),
         v((rows, heads * BLOCK), BF), v((rows, heads * BLOCK), BF), v((rows, heads * BLOCK), BF),
-        v((heads, BLOCK, rows), BF), v((heads, BLOCK, rows), BF),
+        v((heads, HD, rows), BF), v((heads, BLOCK, rows), BF),
         v((heads, kept, BLOCK), F32), v((rows, local), BF), v((4, quarter, local), BF),
         v((quarter, width), F32), v((quarter, width), F32), v((quarter, BLOCK), F32),
         v((4, quarter, width), BF), v((4, quarter, width), F32), v((4, quarter, width), BF),
         v((4, quarter, width), F32),
         v((6, quarter, width), BF), v((6, quarter, width), BF),
-        v((quarter, width), F32), v((4, quarter, width), BF), v((4, quarter, width), BF),
-        v((2, 8, strip, width), BF), v((2, 4, strip, width), BF), v((4, 2, strip, width), BF),
-        v((4, 2, strip, width), BF), v((4, 2, strip, width), BF),
-        v((quarter, width), F32), v((4, quarter, local), BF), v((4, quarter, local), BF),
+        v((4, quarter, width), BF), v((4, quarter, width), BF),
+        v((2, 4, strip, width), BF),
+        v((2, 4, strip, width), BF), v((2, 3, strip, width), BF),
+        v((2, 2, strip, width), BF), v((2, strip, width), BF),
+        v((4, quarter, local), BF), v((4, quarter, local), BF),
         v((rows, heads * BLOCK), BF),
-        v((2, 4, 4, strip, local), BF), v((4, 4, strip, local), BF), v((4, 4, strip, local), BF),
-        v((4, 4, strip, local), BF), v((4, strip, local), BF), v((4, strip, local), BF),
-        v((rows, 6 * local), BF), v((4, quarter, width), BF), v((4, quarter, width), BF),
-        v((2, 4, strip, 6 * local), BF), v((4, strip, 6 * local), BF),
+        v((4, 4, strip, local), BF), v((4, 4, strip, local), BF), v((4, strip, local), BF),
+        v((4, strip, local), BF),
+        v((rows, 6 * local), BF),
+        v((2, 3, quarter // 2, width), BF), v((2, 2, quarter // 2, width), BF),
+        v((2, quarter // 2, width), BF),
         v((4, strip, 6 * local), BF), v((4, strip, 6 * local), BF),
         v((16, width), F32), v((8, 16, width), F32), v((16, width), F32), v((4, 16, width), F32),
         pltpu.SemaphoreType.DMA((SENDS,)), pltpu.SemaphoreType.DMA((RECVS,)),

time: 213 us -> 168 us (0.79)
  the two profiles are of different devices: /device:TPU:17 before, /device:TPU:0 now
where the time goes in v2:
time: 168 us
  Pallas kernels  167 us (99%)
    pallas_call x1, Pallas kernels, fused(): pl.pallas_call(layer_kernel, out_shape=outs, in_specs=[spec] * len(args),...  164 us
    pallas_call x1, Pallas kernels, fused(): pl.pallas_call(end_kernel, out_shape=[like(v, v.dtype) for v in large] +...  3.65 us

profile of v2, /device:TPU:0, one launch (start us, length us, event | category | flops | bytes accessed | tf_op | source)
XLA Modules:
  0.0 168.0 jit_solution(6654562795696958841)
XLA Ops:
  0.7 163.5 %layer.1 = (bf16[1,640,768]{2,1,0:T(8,128)(2,1)}, bf16[1,640,768]{2,1,0:T(8,128)(2,1)}, f32[4,96,192]{2,1,0:T(8,128)}, f32[96,192]{1,0:T(8,128)}, f32[96,192]{1,...) custom-call(bf16[1,640,768]{2,1,0:T(8,128)(2,1)} %x_ref.1, ...), custom_call_target="tpu_custom_call" | custom-call | tf_op jit(solution)/shard_map/layer/pallas_call | solution.py:1167
  164.2 3.6 %finish.1 = (bf16[1,640,768]{2,1,0:T(8,128)(2,1)}, bf16[1,640,768]{2,1,0:T(8,128)(2,1)}, f32[4,96,192]{2,1,0:T(8,128)}, f32[96,192]{1,0:T(8,128)}, f32[96,192]{1...) custom-call(bf16[1,640,768]{2,1,0:T(8,128)(2,1)} %get-tuple-element., ...), custom_call_target="tpu_custom_call" | custom-call | tf_op jit(solution)/shard_map/finish/pallas_call | solution.py:1180

commit v3 on v2

--- a/solution.py
+++ b/solution.py
@@ -428,10 +428,10 @@
     x_ref, seg_ref, typ_ref, qw_ref, kw_ref, vw_ref, ow_ref, uw_ref, dw_ref, qb_ref, vb_ref,
     ob_ref, ub_ref, db_ref, ag_ref, as_ref, fg_ref, fs_ref, cot_ref,
     out_ref, ig_ref, qg_ref, kg_ref, vg_ref, og_ref, ug_ref, dg_ref, small_ref,
-    wq, wo, own, own_y, wf, ubs, segc, wordc, xt, bias, qq, kv, kk, kvt, kkt, probs, ctx, ct,
+    wq, wo, own, wf, ubs, segc, wordc, xt, bias, qq, kv, kk, kvt, kkt, probs, ctx, ct,
     a_s, n1_s, r1_s, act, gelu_d, gl, parts, rs_send, rs_recv, dub, dzb,
-    ry, rx, fr_in, fr_cross, fr_back, dct, dc, dco, go_r, rp, sp, rz,
-    dqkv, dx_in, dx_cross, dx_back, gq_r, gp, sv, vb8, sw, vz,
+    st_a, st_b, st_c, st_d, st_e, st_f, dct, dc, dco, go_r, rp, sp, rz,
+    dqkv, dx_in, dx_cross, dx_back, gq_r, gp, sv, small_s, small_r, sw, vz,
     send_sems, recv_sems,
 ):
     d = lax.axis_index("dp")
@@ -439,7 +439,13 @@
     c = d % 2
     x = (d // 2) % 2
     y = d // 4
-    j = d % 4
+    pair = t % 2
+    j = 2 * pair + c
+    block = pair + 2 * c
+    home = block == t
+    zp = t + 1 - 2 * pair
+    zq = (t + 2) % 4
+    host = 2 * (d // 2) + t // 2
     chip = d // 2
     sib = d + 1 - 2 * c
     xn = d + 2 - 4 * x
@@ -505,21 +511,13 @@
                 self.copy(place(3), z_back, is_mid)
             self.wait(place(n), is_end)
 
-    def new_owners(n):
-        if n == 0:
-            return ((t, None),)
-        if n == 1:
-            return ((jnp.where(is_mid, place(0), place(1)), None), (place(2), is_mid))
-        return ((jnp.where(is_mid, place(3), place(2)), None),) if n == 2 else ((place(3), is_end),)
-
     class LineReduce:
         def __init__(self, own, came, cross, back):
             self.own, self.came, self.cross, self.back = own, came, cross, back
             self.in_b, self.cross_b, self.back_b = net.bank(4), net.bank(4), net.bank(1)
 
-        def begin(self):
-            for e in (3, 2, 1):
-                net.start(self.own(e), self.came.at[e - 1], self.in_b + e, (d, z_out), when=is_end)
+        def depart(self, e):
+            net.start(self.own(e), self.came.at[e - 1], self.in_b + e, (d, z_out), when=is_end)
 
         def add(self, e, ref):
             @pl.when(is_mid)
@@ -550,7 +548,8 @@
         pl.semaphore_signal(barrier, 1, device_id=((d + m) % 8, t), device_id_type=MESH)
     for k in range(1, 4):
         pl.semaphore_signal(barrier, 1, device_id=(d, (t + k) % 4), device_id_type=MESH)
-    pl.semaphore_wait(barrier, 10)
+    pl.semaphore_signal(barrier, 1, device_id=(sib, zq), device_id_type=MESH)
+    pl.semaphore_wait(barrier, 11)
 
     for h in range(heads):
         at = slice(HD * h, HD * (h + 1))
@@ -607,35 +606,56 @@
         return value.T
 
     wo[t, d] = wide_t(ow_ref[...], 256, 128)[:strip, :local].astype(BF)
-    own[0, t] = uw_ref[...].astype(BF)
-    own[1, t] = dw_ref[...].astype(BF)
+    own[0] = uw_ref[...].astype(BF)
+    own[1] = dw_ref[...].astype(BF)
     ubs[t] = jnp.broadcast_to(ub_ref[...][None], ubs.shape[1:])
 
-    ub_z = net.bank(4)
-    wf_x = net.bank(16)
-    wf_y = net.bank(8)
-
-    line_o = LineGather(lambda s: wo.at[s, d], "o")
-    line_f = [LineGather(lambda s, i=i: own.at[i, s]) for i in range(2)]
-
-    def hop_x(i, source, row, s, when=None):
-        target = wf.at[i, row]
-        sem = wf_x + 8 * i + row
-        net.start(source, target, sem, (4 * y + s, t), when=joint(when, s != j))
-
-        @pl.when(joint(when, s == j))
-        def _():
-            target[...] = source[...]
-
-    def hop_y(n):
-        for s, when in new_owners(n):
-            net.start(own.at[0, s], own_y.at[s], wf_y + s, (yn, t), when=when)
-
-    line_o.begin()
-    line_f[0].begin()
-    hop_y(0)
-    for k in range(1, 4):
-        net.start(ubs.at[t], ubs.at[t], ub_z + t, (d, (t + k) % 4))
+    ub_z = net.bank(1)
+    wf_a = net.bank(4)
+
+    class ChipGather:
+        def __init__(self, i):
+            self.i, self.bank = i, net.bank(8)
+
+        def send(self):
+            i = self.i
+            for plane, when in ((zq, None), (t, host != d)):
+                net.start(own.at[i], wf.at[i, d], wf_a + 2 * i + c, (host, plane), when=when)
+
+            @pl.when(host == d)
+            def _():
+                wf[i, d] = own[i]
+
+        def copy(self, view, of, device):
+            ref = wf.at[self.i, 2 * (of // 2) + view]
+            net.start(ref, ref, self.bank + 2 * (of // 2) + view, (device, t), group="f")
+
+        def wait(self, view, of):
+            net.wait(wf.at[self.i, 2 * (of // 2) + view], self.bank + 2 * (of // 2) + view)
+
+        def begin(self):
+            i = self.i
+            net.wait(wf.at[i, d], wf_a + 2 * i + c, when=jnp.logical_not(home))
+            net.wait(wf.at[i, sib], wf_a + 2 * i + 1 - c)
+            for view, device in ((0, yn), (1, xn), (1, yn), (0, xn)):
+                self.copy(view, d, device)
+
+        def middle(self):
+            self.wait(0, yn)
+            self.copy(0, yn, xn)
+            self.wait(1, xn)
+            self.copy(1, xn, yn)
+
+        def end(self):
+            for view, of in ((1, yn), (0, xn), (0, dg), (1, dg)):
+                self.wait(view, of)
+
+    up, down = ChipGather(0), ChipGather(1)
+    wo_z = net.bank(4)
+    for k in (2, 1, 3):
+        net.start(wo.at[t, d], wo.at[t, d], wo_z + t, (d, (t + k) % 4), group="o")
+    net.start(ubs.at[t], ubs.at[t], ub_z, (d, zq))
+    up.send()
     for b in range(blocks):
         at = slice(BLOCK * b, BLOCK * (b + 1))
         segc[at, :] = jnp.broadcast_to(seg_ref[:, at].astype(F32), (BLOCK, BLOCK)).T
@@ -649,14 +669,13 @@
         )
 
     gather_q.middle()
-    line_o.step(1)
-    line_f[0].step(1)
-    hop_y(1)
-    line_f[1].begin()
+    down.send()
+    for k in range(1, 4):
+        s = (t + k) % 4
+        net.wait(wo.at[s, d], wo_z + s)
+    gather_o = PlaneGather("o", lambda b: wo.at[0:2, b], lambda b: wo.at[2:4, b])
+    gather_o.begin()
     gather_q.late()
-    line_o.step(2)
-    line_f[0].step(2)
-    hop_y(2)
     gather_q.end()
     low_half = lax.broadcasted_iota(jnp.int32, (rows, BLOCK), 1) < HD
     is_word = wordc[...] > 0.5
@@ -674,15 +693,8 @@
         kvt[h] = both.T[HD:].astype(BF)
         kkt[h] = keys.T.astype(BF)
 
-    line_o.step(3)
-    line_f[0].step(3)
-    hop_y(3)
-    gather_o = PlaneGather("o", lambda b: wo.at[0:2, b], lambda b: wo.at[2:4, b])
-    gather_o.begin()
-    for n in range(4):
-        for s, when in new_owners(n):
-            hop_x(0, own.at[0, s], d, s, when)
-    line_f[1].step(1)
+    gather_o.middle()
+    up.begin()
     ct_z = net.bank(4)
 
     def span(b):
@@ -706,22 +718,15 @@
             found.append(nn(kvt[h, :, lo:hi], weights.astype(BF)))
         found.append(jnp.zeros((HD, BLOCK), F32))
         ctx[at_q, :] = jnp.concatenate(found, axis=0).T[:, :local].astype(BF)
-        if b == 2:
-            line_f[1].step(2)
+        if b == 3:
+            down.begin()
         if b > 0:
             s = b - 1
             src = ctx.at[quarter * s : quarter * (s + 1)]
             net.start(src, ct.at[t], ct_z + t, (d, s), when=t != s)
     ct[t] = ctx[own_rows, :]
 
-    line_f[1].step(3)
-    for n in range(4):
-        for s, when in new_owners(n):
-            hop_x(1, own.at[1, s], d, s, when)
-    gather_o.middle()
-    for s in range(4):
-        net.wait(own_y.at[s], wf_y + s)
-        hop_x(0, own_y.at[s], yn, s)
+    up.middle()
     gather_o.late()
     gather_o.end()
     for k in range(1, 4):
@@ -742,160 +747,250 @@
             0, pl.ds(pl.multiple_of(owner * quarter + first, 16), count)
         ]
 
+    part = quarter // 2
+    chunk = [slice(part * q, part * (q + 1)) for q in range(2)]
+
     class RowGather:
         def __init__(self, ref):
-            self.ref, self.bank = ref, net.bank(4)
-
-        def copy(self, rank, device):
-            net.start(self.ref.at[rank], self.ref.at[rank], self.bank + rank, (device, t))
-
-        def begin(self):
-            self.copy(j, xn)
-            self.copy(j, sib)
-
-        def near(self):
-            net.wait(self.ref.at[sib % 4], self.bank + sib % 4)
-
-        def middle(self):
-            net.wait(self.ref.at[xn % 4], self.bank + xn % 4)
-            self.copy(xn % 4, sib)
-
-        def far(self):
-            net.wait(self.ref.at[flip_x(sib) % 4], self.bank + flip_x(sib) % 4)
+            self.ref, self.bank = ref, net.bank(8)
+
+        def copy(self, q, rank, device):
+            ref = self.ref.at[rank, chunk[q]]
+            net.start(ref, ref, self.bank + 4 * q + rank, device)
+
+        def wait(self, q, rank):
+            net.wait(self.ref.at[rank, chunk[q]], self.bank + 4 * q + rank)
+
+        def begin(self, q):
+            self.copy(q, j, (d, zp))
+            self.copy(q, j, (sib, t))
+
+        def near(self, q):
+            self.wait(q, 2 * pair + 1 - c)
+
+        def middle(self, q):
+            self.wait(q, 2 - 2 * pair + c)
+            self.copy(q, 2 - 2 * pair + c, (sib, t))
+
+        def far(self, q):
+            self.wait(q, 3 - 2 * pair - c)
 
     class RowSum:
         def __init__(self, index):
-            self.index, self.bank = index, net.bank(3)
-
-        def hand(self, slot, partial_rows):
+            self.index, self.bank = index, net.bank(6)
+
+        def hand(self, q, slot, partial_rows):
             where = 3 * self.index + slot
-            rs_send[where] = partial_rows.astype(BF)
+            rs_send[where, chunk[q]] = partial_rows.astype(BF)
             net.start(
-                rs_send.at[where], rs_recv.at[where], self.bank + slot, (xn if slot == 2 else sib, t)
+                rs_send.at[where, chunk[q]], rs_recv.at[where, chunk[q]], self.bank + 3 * q + slot,
+                (d, zp) if slot == 2 else (sib, t),
             )
 
-        def take(self, slot):
+        def take(self, q, slot):
             where = 3 * self.index + slot
-            net.wait(rs_recv.at[where], self.bank + slot)
-            return rs_recv[where].astype(F32)
-
-        def own_half(self):
-            self.hand(0, part_m[1 - c])
-
-        def other_half(self):
-            self.hand(1, part_o[1 - c])
-            self.hand(2, part_o[c] + self.take(1))
-
-        def total(self):
-            return part_m[c] + self.take(0) + self.take(2)
+            net.wait(rs_recv.at[where, chunk[q]], self.bank + 3 * q + slot)
+            return rs_recv[where, chunk[q]].astype(F32)
+
+        def near(self, q):
+            self.hand(q, 0, part_m[1 - c, chunk[q]])
+
+        def away(self, q):
+            self.hand(q, 1, part_o[1 - c, chunk[q]])
+
+        def across(self, q):
+            self.hand(q, 2, part_o[c, chunk[q]] + self.take(q, 1))
+
+        def total(self, q):
+            return part_m[c, chunk[q]] + self.take(q, 0) + self.take(q, 2)
 
     rows_a = RowGather(act)
-    rows_a.begin()
-    for m in range(4):
-        r = 4 * y + (j + m) % 4
-        if m:
-            net.wait(wf.at[1, r], wf_x + 8 + r)
-        net.start(wf.at[1, r], wf.at[1, r], wf_y + 4 + (j + m) % 4, (yn, t), group="f")
-    rows_a.middle()
-    rows_a.near()
-    for k in range(1, 4):
-        s = (t + k) % 4
-        net.wait(ubs.at[s], ub_z + s)
-    for m in range(1, 4):
-        for r in (4 * y + (j + m) % 4, 4 * (1 - y) + (j + m) % 4):
-            net.wait(wf.at[0, r], wf_x + r)
-    near = pl.ds(2 * x, 2)
-    away = pl.ds(2 - 2 * x, 2)
-
-    def feed(half):
-        hidden = nn(act[half].reshape(2 * quarter, width), wf[0].reshape(width, width))
-        hidden = hidden + ubs[j][:1]
+    rows_a.begin(0)
+    rows_a.begin(1)
+    down.middle()
+    rows_a.middle(0)
+    rows_a.middle(1)
+    rows_a.near(0)
+    rows_a.near(1)
+    net.wait(ubs.at[zq], ub_z)
+    up.end()
+    near = pl.ds(2 * pair, 2)
+    away = pl.ds(2 - 2 * pair, 2)
+
+    def feed(half, q):
+        hidden = nn(act[half, chunk[q]].reshape(2 * part, width), wf[0].reshape(width, width))
+        hidden = hidden + ubs[block][:1]
         bell = 0.5 * (1.0 + lax.erf(hidden * 0.7071067811865476))
         slope = bell + hidden * (0.3989422804014327 * jnp.exp(-0.5 * hidden * hidden))
-        gelu_d[half] = slope.reshape(2, quarter, width)
-        gl[half] = (hidden * bell).astype(BF).reshape(2, quarter, width)
-
-    def feed_out(half, part):
-        made = nt(gl[half].reshape(2 * quarter, width), wf[1].reshape(width, width))
-        part[...] = made.reshape(2, quarter, width)
-
-    feed(near)
-    rows_a.far()
-    feed(away)
-    for m in range(4):
-        r = 4 * (1 - y) + (j + m) % 4
-        net.wait(wf.at[1, r], wf_y + 4 + (j + m) % 4)
+        gelu_d[half, chunk[q]] = slope.reshape(2, part, width)
+        gl[half, chunk[q]] = (hidden * bell).astype(BF).reshape(2, part, width)
+
+    def feed_out(half, q, partial_ref):
+        made = nt(gl[half, chunk[q]].reshape(2 * part, width), wf[1].reshape(width, width))
+        partial_ref[:, chunk[q]] = made.reshape(2, part, width)
+
+    feed(near, 0)
+    feed(near, 1)
+    for q in range(2):
+        rows_a.far(q)
+        feed(away, q)
+    down.end()
     sum_f = RowSum(0)
-    feed_out(away, part_o)
-    sum_f.hand(1, part_o[1 - c])
-    feed_out(near, part_m)
-    sum_f.own_half()
-    sum_f.hand(2, part_o[c] + sum_f.take(1))
-    ffn_out = sum_f.total() + db_ref[...][None]
-
-    normal, inverse = norm_rows(a_s[...] + ffn_out)
-    out_ref[0, own_rows, :] = (normal * fg_ref[...][None] + fs_ref[...][None]).astype(BF)
-    line_out = LineGather(rows_of(out_ref, 0, quarter))
-    line_out.begin()
-    upstream = cot_ref[0, own_rows, :].astype(F32)
-    du = norm_rows_back(upstream, normal, inverse, fg_ref[...][None])
-    dub[j] = du.astype(BF)
+    feed_out(away, 0, part_o)
+    sum_f.away(0)
+    feed_out(near, 0, part_m)
+    sum_f.near(0)
+    feed_out(away, 1, part_o)
+    sum_f.away(1)
+    sum_f.across(0)
+    feed_out(near, 1, part_m)
+    sum_f.near(1)
+    sum_f.across(1)
     rows_u = RowGather(dub)
-    rows_u.begin()
-    a_s[...] = du
+    gain_sum, shift_sum, bias_sum = 0.0, 0.0, 0.0
+    for q in range(2):
+        ffn_out = sum_f.total(q) + db_ref[...][None]
+        normal, inverse = norm_rows(a_s[chunk[q]] + ffn_out)
+        rows_q = pl.ds(pl.multiple_of(t * quarter + part * q, 16), part)
+        out_ref[0, rows_q, :] = (normal * fg_ref[...][None] + fs_ref[...][None]).astype(BF)
+        upstream = cot_ref[0, rows_q, :].astype(F32)
+        du = norm_rows_back(upstream, normal, inverse, fg_ref[...][None])
+        dub[j, chunk[q]] = du.astype(BF)
+        rows_u.begin(q)
+        a_s[chunk[q]] = du
+        gain_sum = gain_sum + jnp.sum(upstream * normal, axis=0, keepdims=True)
+        shift_sum = shift_sum + jnp.sum(upstream, axis=0, keepdims=True)
+        bias_sum = bias_sum + jnp.sum(du, axis=0, keepdims=True)
+    line_out = [LineGather(rows_of(out_ref, part * q, part)) for q in range(2)]
+    line_out[0].begin()
     sv[...] = jnp.zeros_like(sv)
-    sv[0:1] = jnp.sum(upstream * normal, axis=0, keepdims=True)
-    sv[1:2] = jnp.sum(upstream, axis=0, keepdims=True)
-    sv[2:3] = jnp.sum(du, axis=0, keepdims=True)
-
-    def feed_back(half, part):
-        made = nn(dub[half].reshape(2 * quarter, width), wf[1].reshape(width, width))
-        made = made * gelu_d[half].reshape(2 * quarter, width)
-        dzb[half] = made.astype(BF).reshape(2, quarter, width)
-        back = nt(made.astype(BF), wf[0].reshape(width, width))
-        part[...] = back.reshape(2, quarter, width)
+    sv[0:1] = gain_sum
+    sv[1:2] = shift_sum
+    sv[2:3] = bias_sum
+
+    def feed_back(half, q, partial_ref):
+        made = nn(dub[half, chunk[q]].reshape(2 * part, width), wf[1].reshape(width, width))
+        made = made * gelu_d[half, chunk[q]].reshape(2 * part, width)
+        low = made.astype(BF)
+        dzb[half, chunk[q]] = low.reshape(2, part, width)
+        partial_ref[:, chunk[q]] = nt(low, wf[0].reshape(width, width)).reshape(2, part, width)
         return jnp.sum(made, axis=0, keepdims=True)
 
-    rows_u.near()
-    up_sum = feed_back(near, part_m)
     sum_b = RowSum(1)
-    sum_b.own_half()
-    line_out.step(1)
-    rows_u.middle()
-    rows_u.far()
-    up_sum = up_sum + feed_back(away, part_o)
-    sum_b.hand(1, part_o[1 - c])
-    sum_b.hand(2, part_o[c] + sum_b.take(1))
+    up_sum = 0.0
+    for q in range(2):
+        rows_u.near(q)
+        up_sum = up_sum + feed_back(near, q, part_m)
+        sum_b.near(q)
+    rows_u.middle(0)
+    rows_u.far(0)
+    up_sum = up_sum + feed_back(away, 0, part_o)
+    sum_b.away(0)
+    rows_u.middle(1)
+    sum_b.across(0)
+    rows_u.far(1)
+    up_sum = up_sum + feed_back(away, 1, part_o)
+    sum_b.away(1)
     rank_rows = lax.broadcasted_iota(jnp.int32, (4, width), 0)
-    sv[6:10] = jnp.where(rank_rows == j, up_sum, 0.0)
-
-    ry_b = net.bank(2)
-    theirs = pl.ds(4 * (1 - y), 4)
-    ours = pl.ds(4 * y, 4)
-    def feed_grad(i, left, right):
-        made = tn(left[...].reshape(4 * quarter, width), right[...].reshape(4 * quarter, width))
-        wf[i] = made.astype(BF).reshape(8, strip, width)
+    sv[8:12] = jnp.where(rank_rows == block, up_sum, 0.0)
+    half = width // 2
+
+    class StripSum:
+        def __init__(self, i):
+            self.i, self.bank = i, net.bank(6)
+            self.by_chip = wf.at[i].reshape(2, 2, 2, strip, width)
+
+        def begin(self, left, right):
+            made = tn(left[...].reshape(4 * quarter, width), right[...].reshape(4 * quarter, width))
+            wf[self.i] = made.astype(BF).reshape(8, strip, width)
+            net.start(
+                self.by_chip.at[:, 1 - x, :, :, :half], st_a.at[self.i], self.bank, (xn, t)
+            )
+            net.start(
+                self.by_chip.at[1 - y, :, :, :, half:], st_b.at[self.i], self.bank + 1, (yn, t)
+            )
+
+        def turn(self):
+            i = self.i
+            net.wait(st_a.at[i], self.bank)
+            st_a[i] = (st_a[i].astype(F32) + self.by_chip[:, x, :, :, :half].astype(F32)).astype(BF)
+            net.start(st_a.at[i, 1 - y], st_c.at[i], self.bank + 2, (yn, t))
+            net.wait(st_b.at[i], self.bank + 1)
+            st_b[i] = (st_b[i].astype(F32) + self.by_chip[y, :, :, :, half:].astype(F32)).astype(BF)
+            net.start(st_b.at[i, 1 - x], st_d.at[i], self.bank + 3, (xn, t))
+
+        def deliver(self):
+            i = self.i
+            net.wait(st_c.at[i], self.bank + 2)
+            st_e[i, :, :, :half] = (st_c[i].astype(F32) + st_a[i, y].astype(F32)).astype(BF)
+            net.wait(st_d.at[i], self.bank + 3)
+            st_e[i, :, :, half:] = (st_d[i].astype(F32) + st_b[i, x].astype(F32)).astype(BF)
+            slot = jnp.where(home, 0, 1)
+            for core in range(2):
+                net.start(
+                    st_e.at[i, core], st_f.at[i, slot], self.bank + 4 + slot,
+                    (2 * (d // 2) + core, block),
+                    when=jnp.logical_or(c != core, jnp.logical_not(home)),
+                )
+
+            @pl.when(home)
+            def _():
+                st_f[i, 0] = st_e[i, c]
+
+        def total(self):
+            i = self.i
+            net.wait(st_f.at[i, 0], self.bank + 4, when=host != d)
+            net.wait(st_f.at[i, 1], self.bank + 5)
+            return st_f[i, 0].astype(F32) + st_f[i, 1].astype(F32)
+
+    class SmallSum:
+        def __init__(self, index):
+            self.index, self.bank = index, net.bank(3)
+
+        def start(self, step):
+            ref = small_s.at[self.index, step]
+            net.start(ref, small_r.at[self.index, step], self.bank + step, ((sib, xn, yn)[step], t))
+
+        def begin(self, values):
+            small_s[self.index, 0] = values
+            self.start(0)
+
+        def step(self, n):
+            net.wait(small_r.at[self.index, n - 1], self.bank + n - 1)
+            small_s[self.index, n] = small_s[self.index, n - 1] + small_r[self.index, n - 1]
+            if n < 3:
+                self.start(n)
 
     net.settle("f")
-    feed_grad(1, dub, gl)
-    net.start(wf.at[1, theirs], ry.at[1], ry_b + 1, (yn, t))
-    feed_grad(0, act, dzb)
-    da = a_s[...] + sum_b.total()
-    line_out.step(2)
-    normal = n1_s[...]
-    dh = norm_rows_back(da, normal, r1_s[:, :1], ag_ref[...][None])
-    a_s[...] = dh
-    dhb = dh.astype(BF)
-    dc_z = net.bank(4)
-    for k in range(1, 4):
-        s = (t + k) % 4
-        dct[s] = nn(dhb, wo[s].reshape(width, local)).astype(BF)
-        net.start(dct.at[s], dc.at[t], dc_z + t, (d, s))
-    dc[t] = nn(dhb, wo[t].reshape(width, local)).astype(BF)
-    net.start(wf.at[0, theirs], ry.at[0], ry_b, (yn, t))
-    sv[3:4] = jnp.sum(da * normal, axis=0, keepdims=True)
-    sv[4:5] = jnp.sum(da, axis=0, keepdims=True)
-    sv[5:6] = jnp.sum(dh, axis=0, keepdims=True)
+    down_sum, up_sums = StripSum(1), StripSum(0)
+    down_sum.begin(dub, gl)
+    sum_b.across(1)
+    line_out[1].begin()
+    up_sums.begin(act, dzb)
+    dc_z = net.bank(8)
+    gain_sum, shift_sum, bias_sum, dhb = 0.0, 0.0, 0.0, []
+    for q in range(2):
+        da = a_s[chunk[q]] + sum_b.total(q)
+        normal = n1_s[chunk[q]]
+        dh = norm_rows_back(da, normal, r1_s[chunk[q], :1], ag_ref[...][None])
+        a_s[chunk[q]] = dh
+        dhb.append(dh.astype(BF))
+        for k in (2, 1, 3):
+            s = (t + k) % 4
+            dct[s, chunk[q]] = nn(dhb[q], wo[s].reshape(width, local)).astype(BF)
+            net.start(dct.at[s, chunk[q]], dc.at[t, chunk[q]], dc_z + 4 * q + t, (d, s))
+        dc[t, chunk[q]] = nn(dhb[q], wo[t].reshape(width, local)).astype(BF)
+        gain_sum = gain_sum + jnp.sum(da * normal, axis=0, keepdims=True)
+        shift_sum = shift_sum + jnp.sum(da, axis=0, keepdims=True)
+        bias_sum = bias_sum + jnp.sum(dh, axis=0, keepdims=True)
+    dhb = jnp.concatenate(dhb, axis=0)
+    line_out[0].step(1)
+    line_out[1].step(1)
+    sv[3:4] = gain_sum
+    sv[4:5] = shift_sum
+    sv[5:6] = bias_sum
+    small_a = SmallSum(0)
+    small_a.begin(sv[...])
     net.settle("o")
     for s in range(4):
         wo[s] = tn(dhb, ct[s]).astype(BF).reshape(8, strip, local)
@@ -903,18 +998,17 @@
     go_b = net.bank(1)
     net.start(by_core.at[:, :, 1 - c], go_r, go_b, (sib, t))
 
-    rx_b = net.bank(8)
-
-    def over_y(i):
-        net.wait(ry.at[i], ry_b + i)
-        ry[i] = (wf[i, ours].astype(F32) + ry[i].astype(F32)).astype(BF)
-        for r in (xn, flip_x(sib), sib):
-            net.start(ry.at[i, r % 4], rx.at[i, j], rx_b + 4 * i + j, (r, t))
-        rx[i, j] = ry[i, j]
-
+    down_sum.turn()
+    net.wait(go_r, go_b)
+    go_r[...] = (by_core[:, :, c].astype(F32) + go_r[...].astype(F32)).astype(BF)
+    rp_b = net.bank(4)
+    for r in (xn, yn, dg):
+        net.start(go_r.at[:, r // 2], rp.at[chip], rp_b + chip, (r, t))
+    rp[chip] = go_r[:, chip]
     for k in range(1, 4):
         s = (t + k) % 4
-        net.wait(dc.at[s], dc_z + s)
+        for q in range(2):
+            net.wait(dc.at[s, chunk[q]], dc_z + 4 * q + s)
     dctx = dc[...].reshape(rows, local)
     for h in range(heads):
         dco[:, BLOCK * h : BLOCK * (h + 1)] = jnp.concatenate(
@@ -936,7 +1030,9 @@
             dvv[h][lo:hi] += nn(weights.astype(BF), dco[at_q, at])
             dqq[h][at_q] = nn(kkt[h, :, lo:hi], dsb).T * SCALING
 
-    over_y(1)
+    line_out[0].step(2)
+    line_out[1].step(2)
+    up_sums.turn()
     for h in range(heads):
         base = 6 * HD * h
         first = jnp.where(is_word, dqq[h][...], 0.0)
@@ -944,15 +1040,14 @@
         keys = dkk[h][...]
         keys = jnp.where(is_word, keys, pltpu.roll(keys, HD, 1)) * SCALING
         third = jnp.where(low_half, keys, dvv[h][...])
-        for i, part in enumerate((first, second, third)):
+        for i, piece in enumerate((first, second, third)):
             at = slice(base + BLOCK * i, base + BLOCK * (i + 1))
-            dqkv[:, at] = part.astype(BF)
+            dqkv[:, at] = piece.astype(BF)
             row, col = divmod(base + BLOCK * i, width)
-            sv[10 + row : 11 + row, col : col + BLOCK] = jnp.sum(part, axis=0, keepdims=True)
+            sv[row : row + 1, col : col + BLOCK] = jnp.sum(piece, axis=0, keepdims=True)
 
     made = nt(dqkv[...], wq[...].reshape(width, 6 * local))
     dzb[...] = made.astype(BF).reshape(4, quarter, width)
-    part = quarter // 2
     line_dx, line_in = [], []
     for q in range(2):
         cut = pl.ds(part * q, part)
@@ -969,25 +1064,12 @@
         ig_ref[0, pl.ds(pl.multiple_of(t * quarter + part * q, 16), part)] = total.astype(BF)
         line_in[q].begin()
 
-    line_w = [
-        LineReduce(
-            lambda e, i=i: rx.at[i, place(e)], fr_in.at[i], fr_cross.at[i], fr_back.at[i]
-        )
-        for i in range(2)
-    ]
-
-    def strips_on(i):
-        for m in range(1, 4):
-            r = (j + m) % 4
-            net.wait(rx.at[i, r], rx_b + 4 * i + r)
-        line_w[i].begin()
-
-    line_dx[0].begin()
-    line_dx[1].begin()
-    vb8[d] = sv[...]
-    sv_b = net.bank(8)
-    for m in range(1, 8):
-        net.start(sv, vb8.at[d], sv_b + d, ((d + m) % 8, t))
+    for q, e in ((0, 3), (0, 2), (1, 3), (1, 2), (0, 1), (1, 1)):
+        line_dx[q].depart(e)
+    down_sum.deliver()
+    small_a.step(1)
+    small_b = SmallSum(1)
+    small_b.begin(sv[...])
 
     net.settle("q")
     wq[...] = nn(xt[...], dqkv[...]).astype(BF).reshape(8, strip, 6 * local)
@@ -996,18 +1078,10 @@
     net.start(q_by_core.at[:, 1 - c], gq_r, gq_b, (sib, t))
     line_dx[0].through(3)
     line_dx[0].through(2)
-    net.wait(go_r, go_b)
-    go_r[...] = (by_core[:, :, c].astype(F32) + go_r[...].astype(F32)).astype(BF)
-    rp_b = net.bank(4)
-    for r in (xn, yn, dg):
-        net.start(go_r.at[:, r // 2], rp.at[chip], rp_b + chip, (r, t))
-    rp[chip] = go_r[:, chip]
-
-    strips_on(1)
+    small_a.step(2)
     line_dx[1].through(3)
     line_dx[1].through(2)
     line_dx[0].pass_back()
-    over_y(0)
     net.wait(gq_r, gq_b)
     gq_r[...] = (q_by_core[:, c].astype(F32) + gq_r[...].astype(F32)).astype(BF)
     gp_b = net.bank(4)
@@ -1017,29 +1091,18 @@
 
     line_dx[1].pass_back()
     arrive(0)
-    line_w[1].through(3)
-    line_w[1].through(2)
     arrive(1)
-    for m in range(1, 8):
-        s = (d + m) % 8
-        net.wait(vb8.at[s], sv_b + s)
-    total = vb8[0]
-    for m in range(1, 8):
-        total = total + vb8[m]
-    sw[...] = total
-    vz_b = net.bank(4)
+    up_sums.deliver()
+    small_a.step(3)
+    vz_b = net.bank(5)
+    mine8 = pl.ds(pl.multiple_of(8 * c, 8), 8)
+    sent8 = small_s.at[0, 3, mine8]
     for k in range(1, 4):
-        net.start(sw, vz.at[t], vz_b + t, (d, (t + k) % 4))
-    vz[t] = sw[...]
-
+        net.start(sent8, vz.at[t], vz_b + t, (d, (t + k) % 4))
+    vz[t] = sent8[...]
+    small_b.step(1)
     line_in[0].step(1)
-    strips_on(0)
     line_in[1].step(1)
-    line_w[1].pass_back()
-    line_in[0].step(2)
-    line_in[1].step(2)
-    line_w[0].through(3)
-    line_w[0].through(2)
     for r in (xn, yn, dg):
         net.wait(rp.at[r // 2], rp_b + r // 2)
     total = rp[0].astype(F32)
@@ -1052,20 +1115,23 @@
         net.start(sp.at[s], rz.at[t], rz_b + t, (d, s))
     rz[t] = sp[t]
 
+    small_b.step(2)
     for k in range(1, 4):
-        s = (t + k) % 4
-        net.wait(vz.at[s], vz_b + s)
+        net.wait(vz.at[(t + k) % 4], vz_b + (t + k) % 4)
     total = vz[0]
-    for s in range(1, 4):
-        total = total + vz[s]
-    up_total = jnp.sum(jnp.where(rank_rows == t, total[6:10], 0.0), axis=0, keepdims=True)
-    small_ref[0:6] = total[0:6]
-    small_ref[6:7] = up_total
-    small_ref[8:10] = sw[10:12]
-
-    line_w[0].pass_back()
-    dg_ref[...] = line_w[1].total()
-    ug_ref[...] = line_w[0].total()
+    for k in range(1, 4):
+        total = total + vz[k]
+    sw[mine8] = total
+    net.start(sw.at[mine8], sw.at[mine8], vz_b + 4, (sib, t))
+    line_in[0].step(2)
+    line_in[1].step(2)
+    small_b.step(3)
+    net.wait(sw.at[pl.ds(pl.multiple_of(8 - 8 * c, 8), 8)], vz_b + 4)
+    small_ref[0:6] = sw[0:6]
+    small_ref[6:7] = jnp.sum(jnp.where(rank_rows == t, sw[8:12], 0.0), axis=0, keepdims=True)
+    small_ref[8:10] = small_s[1, 3, 0:2]
+    dg_ref[...] = down_sum.total()
+    ug_ref[...] = up_sums.total()
     for k in range(1, 4):
         s = (t + k) % 4
         net.wait(rz.at[s], rz_b + s)
@@ -1087,7 +1153,8 @@
         kg_ref[:, at] = total[:, base + 4 * HD : base + 5 * HD]
         vg_ref[:, at] = total[:, base + 5 * HD : base + 6 * HD]
 
-    line_out.step(3)
+    line_out[0].step(3)
+    line_out[1].step(3)
     for q in range(2):
         line_in[q].step(3)
     net.settle()
@@ -1138,7 +1205,7 @@
     ]
     v = pltpu.VMEM
     scratch = [
-        v((8, strip, 6 * local), BF), v((4, 8, strip, local), BF), v((2, 4, strip, width), BF), v((4, strip, width), BF),
+        v((8, strip, 6 * local), BF), v((4, 8, strip, local), BF), v((2, strip, width), BF),
         v((2, 8, strip, width), BF), v((4, 8, width), F32), v((rows, BLOCK), F32),
         v((rows, BLOCK), F32), v((width, rows), BF), v((1, 6 * local), F32),
         v((rows, heads * BLOCK), BF), v((rows, heads * BLOCK), BF), v((rows, heads * BLOCK), BF),
@@ -1149,9 +1216,9 @@
         v((4, quarter, width), F32),
         v((6, quarter, width), BF), v((6, quarter, width), BF),
         v((4, quarter, width), BF), v((4, quarter, width), BF),
-        v((2, 4, strip, width), BF),
-        v((2, 4, strip, width), BF), v((2, 3, strip, width), BF),
-        v((2, 2, strip, width), BF), v((2, strip, width), BF),
+        v((2, 2, 2, strip, width // 2), BF), v((2, 2, 2, strip, width // 2), BF),
+        v((2, 2, strip, width // 2), BF), v((2, 2, strip, width // 2), BF),
+        v((2, 2, strip, width), BF), v((2, 2, strip, width), BF),
         v((4, quarter, local), BF), v((4, quarter, local), BF),
         v((rows, heads * BLOCK), BF),
         v((4, 4, strip, local), BF), v((4, 4, strip, local), BF), v((4, strip, local), BF),
@@ -1160,7 +1227,8 @@
         v((2, 3, quarter // 2, width), BF), v((2, 2, quarter // 2, width), BF),
         v((2, quarter // 2, width), BF),
         v((4, strip, 6 * local), BF), v((4, strip, 6 * local), BF),
-        v((16, width), F32), v((8, 16, width), F32), v((16, width), F32), v((4, 16, width), F32),
+        v((16, width), F32), v((2, 4, 16, width), F32), v((2, 3, 16, width), F32),
+        v((16, width), F32), v((4, 8, width), F32),
         pltpu.SemaphoreType.DMA((SENDS,)), pltpu.SemaphoreType.DMA((RECVS,)),
     ]
     spec = pl.BlockSpec(memory_space=pltpu.VMEM)

time: 168 us -> 143 us (0.85)
  Pallas kernels: 167 us -> 142 us
    pallas_call x1, Pallas kernels: 164 us -> 139 us  [fused(): pl.pallas_call(layer_kernel, out_shape=outs, in_specs=[spec] * len(args),...]
where the time goes in v3:
time: 143 us
  Pallas kernels  142 us (99%)
    pallas_call x1, Pallas kernels, fused(): pl.pallas_call(layer_kernel, out_shape=outs, in_specs=[spec] * len(args),...  139 us
    pallas_call x1, Pallas kernels, fused(): pl.pallas_call(end_kernel, out_shape=[like(v, v.dtype) for v in large] +...  3.65 us

profile of v3, /device:TPU:0, one launch (start us, length us, event | category | flops | bytes accessed | tf_op | source)
XLA Modules:
  0.0 143.2 jit_solution(6269754374996042001)
XLA Ops:
  0.7 138.7 %layer.1 = (bf16[1,640,768]{2,1,0:T(8,128)(2,1)}, bf16[1,640,768]{2,1,0:T(8,128)(2,1)}, f32[4,96,192]{2,1,0:T(8,128)}, f32[96,192]{1,0:T(8,128)}, f32[96,192]{1,...) custom-call(bf16[1,640,768]{2,1,0:T(8,128)(2,1)} %x_ref.1, ...), custom_call_target="tpu_custom_call" | custom-call | tf_op jit(solution)/shard_map/layer/pallas_call | solution.py:1235
  139.4 3.6 %finish.1 = (bf16[1,640,768]{2,1,0:T(8,128)(2,1)}, bf16[1,640,768]{2,1,0:T(8,128)(2,1)}, f32[4,96,192]{2,1,0:T(8,128)}, f32[96,192]{1,0:T(8,128)}, f32[96,192]{1...) custom-call(bf16[1,640,768]{2,1,0:T(8,128)(2,1)} %get-tuple-element., ...), custom_call_target="tpu_custom_call" | custom-call | tf_op jit(solution)/shard_map/finish/pallas_call | solution.py:1248

commit v4 on v3

--- a/solution.py
+++ b/solution.py
@@ -365,6 +365,7 @@
     def __init__(self, send, recv, peer):
         self.send, self.recv, self.peer = send, recv, peer
         self.sends = 0
+        self.locals = 0
         self.banks = 0
         self.pending = []
 
@@ -374,8 +375,9 @@
         return base
 
     def start(self, src, dst, sem, device, when=None, group=None):
-        slot = self.sends
+        slot = self.sends % SENDS
         self.sends += 1
+        self.finish([p for p in self.pending if p[3] == slot])
 
         def make():
             return pltpu.make_async_remote_copy(
@@ -391,7 +393,15 @@
             make().start()
         else:
             pl.when(when)(lambda: make().start())
-        self.pending.append((make, when, group))
+        self.pending.append((make, when, group, slot))
+
+    def finish(self, entries):
+        for make, when, _, _ in entries:
+            if when is None:
+                make().wait_send()
+            else:
+                pl.when(when)(lambda make=make: make().wait_send())
+        self.pending = [p for p in self.pending if p not in entries]
 
     def wait(self, dst, sem, when=None):
         def make():
@@ -410,29 +420,24 @@
             pl.when(when)(lambda: make().wait_recv())
 
     def settle(self, *groups):
-        for make, when, group in self.pending:
-            if groups and group not in groups:
-                continue
-            if when is None:
-                make().wait_send()
-            else:
-                pl.when(when)(lambda make=make: make().wait_send())
-        self.pending = [p for p in self.pending if groups and p[2] not in groups]
-
-
-SENDS = 192
-RECVS = 224
+        self.finish([p for p in self.pending if not groups or p[2] in groups])
+
+
+SENDS = 48
+RECVS = 141
 
 
 def layer_kernel(
-    x_ref, seg_ref, typ_ref, qw_ref, kw_ref, vw_ref, ow_ref, uw_ref, dw_ref, qb_ref, vb_ref,
-    ob_ref, ub_ref, db_ref, ag_ref, as_ref, fg_ref, fs_ref, cot_ref,
+    x_in, seg_ref, typ_ref, qw_in, kw_in, vw_in, ow_in, uw_in, dw_in, qb_ref, vb_ref,
+    ob_ref, ub_ref, db_ref, ag_ref, as_ref, fg_ref, fs_ref, cot_in,
+    out_end, ig_end, qg_end, kg_end, vg_end, og_end, ug_end, dg_end, small_end,
+    x_ref, qw_ref, kw_ref, vw_ref, ow_ref, uw_ref, dw_ref, cot_ref,
     out_ref, ig_ref, qg_ref, kg_ref, vg_ref, og_ref, ug_ref, dg_ref, small_ref,
     wq, wo, own, wf, ubs, segc, wordc, xt, bias, qq, kv, kk, kvt, kkt, probs, ctx, ct,
     a_s, n1_s, r1_s, act, gelu_d, gl, parts, rs_send, rs_recv, dub, dzb,
-    st_a, st_b, st_c, st_d, st_e, st_f, dct, dc, dco, go_r, rp, sp, rz,
-    dqkv, dx_in, dx_cross, dx_back, gq_r, gp, sv, small_s, small_r, sw, vz,
-    send_sems, recv_sems,
+    st_a, st_b, st_c, st_d, st_e, st_f, st_g, dct, dc, dco, go_r, rp, sp, rz,
+    dqkv, dx_in, dx_cross, dx_back, gq_r, gp, sv, small_s, small_r, sent8, sw, vz,
+    send_sems, recv_sems, local_sems,
 ):
     d = lax.axis_index("dp")
     t = lax.axis_index("tensor")
@@ -514,10 +519,10 @@
     class LineReduce:
         def __init__(self, own, came, cross, back):
             self.own, self.came, self.cross, self.back = own, came, cross, back
-            self.in_b, self.cross_b, self.back_b = net.bank(4), net.bank(4), net.bank(1)
+            self.in_b, self.cross_b, self.back_b = net.bank(3), net.bank(2), net.bank(1)
 
         def depart(self, e):
-            net.start(self.own(e), self.came.at[e - 1], self.in_b + e, (d, z_out), when=is_end)
+            net.start(self.own(e), self.came.at[e - 1], self.in_b + e - 1, (d, z_out), when=is_end)
 
         def add(self, e, ref):
             @pl.when(is_mid)
@@ -526,7 +531,7 @@
 
         def through(self, e):
             ref = self.came.at[e - 1]
-            net.wait(ref, self.in_b + e, when=is_mid)
+            net.wait(ref, self.in_b + e - 1, when=is_mid)
             self.add(e, ref)
             net.start(ref, self.cross.at[3 - e], self.cross_b + 3 - e, (d, z_out), when=is_mid)
 
@@ -536,12 +541,25 @@
             net.start(self.cross.at[0], self.back, self.back_b, (d, z_back), when=is_mid)
 
         def total(self):
-            net.wait(self.came.at[0], self.in_b + 1, when=is_mid)
+            net.wait(self.came.at[0], self.in_b, when=is_mid)
             net.wait(self.cross.at[1], self.cross_b + 1, when=is_mid)
             net.wait(self.back, self.back_b, when=is_end)
             others = self.came[0].astype(F32) + self.cross[1].astype(F32)
             mine = self.own(jnp.where(is_mid, 1, 0))[...].astype(F32)
             return mine + jnp.where(is_mid, others, self.back[...].astype(F32))
+
+    class Local:
+        def __init__(self, source, target):
+            self.copy = pltpu.make_async_copy(source, target, local_sems.at[net.locals])
+            net.locals += 1
+            self.copy.start()
+
+        def wait(self):
+            self.copy.wait()
+
+    in_q, in_k, in_v = Local(qw_in, qw_ref), Local(kw_in, kw_ref), Local(vw_in, vw_ref)
+    in_o, in_u, in_d = Local(ow_in, ow_ref), Local(uw_in, uw_ref), Local(dw_in, dw_ref)
+    in_x, in_cot = Local(x_in, x_ref), Local(cot_in, cot_ref)
 
     barrier = pltpu.get_barrier_semaphore()
     for m in range(1, 8):
@@ -549,14 +567,17 @@
     for k in range(1, 4):
         pl.semaphore_signal(barrier, 1, device_id=(d, (t + k) % 4), device_id_type=MESH)
     pl.semaphore_signal(barrier, 1, device_id=(sib, zq), device_id_type=MESH)
-    pl.semaphore_wait(barrier, 11)
-
+
+    for arrived in (in_q, in_k, in_v):
+        arrived.wait()
     for h in range(heads):
         at = slice(HD * h, HD * (h + 1))
         piece = jnp.concatenate(
             [qw_ref[i, :, at] for i in range(4)] + [kw_ref[:, at], vw_ref[:, at]], axis=1
         )
         wq[d, :, 6 * HD * h : 6 * HD * (h + 1)] = piece.astype(BF)
+
+    pl.semaphore_wait(barrier, 11)
 
     class PlaneGather:
         def __init__(self, group, *views):
@@ -605,6 +626,8 @@
             value = jnp.concatenate([value, jnp.zeros((high - r, wide), value.dtype)], axis=0)
         return value.T
 
+    for arrived in (in_o, in_u, in_d):
+        arrived.wait()
     wo[t, d] = wide_t(ow_ref[...], 256, 128)[:strip, :local].astype(BF)
     own[0] = uw_ref[...].astype(BF)
     own[1] = dw_ref[...].astype(BF)
@@ -651,15 +674,14 @@
                 self.wait(view, of)
 
     up, down = ChipGather(0), ChipGather(1)
-    wo_z = net.bank(4)
+    wo_z = net.bank(1)
     for k in (2, 1, 3):
-        net.start(wo.at[t, d], wo.at[t, d], wo_z + t, (d, (t + k) % 4), group="o")
-    net.start(ubs.at[t], ubs.at[t], ub_z, (d, zq))
-    up.send()
+        net.start(wo.at[t, d], wo.at[t, d], wo_z, (d, (t + k) % 4), group="o")
     for b in range(blocks):
         at = slice(BLOCK * b, BLOCK * (b + 1))
         segc[at, :] = jnp.broadcast_to(seg_ref[:, at].astype(F32), (BLOCK, BLOCK)).T
         wordc[at, :] = jnp.broadcast_to((typ_ref[:, at] == 0).astype(F32), (BLOCK, BLOCK)).T
+    in_x.wait()
     xt[...] = x_ref[0].T
     for h in range(heads):
         at = slice(HD * h, HD * (h + 1))
@@ -669,12 +691,12 @@
         )
 
     gather_q.middle()
-    down.send()
-    for k in range(1, 4):
-        s = (t + k) % 4
-        net.wait(wo.at[s, d], wo_z + s)
+    net.wait(wo.at[0:3, d], wo_z)
     gather_o = PlaneGather("o", lambda b: wo.at[0:2, b], lambda b: wo.at[2:4, b])
     gather_o.begin()
+    up.send()
+    net.start(ubs.at[t], ubs.at[t], ub_z, (d, zq))
+    down.send()
     gather_q.late()
     gather_q.end()
     low_half = lax.broadcasted_iota(jnp.int32, (rows, BLOCK), 1) < HD
@@ -695,7 +717,7 @@
 
     gather_o.middle()
     up.begin()
-    ct_z = net.bank(4)
+    ct_z = net.bank(1)
 
     def span(b):
         return BLOCK * max(0, b - 2), BLOCK * min(blocks, b + 3)
@@ -723,15 +745,13 @@
         if b > 0:
             s = b - 1
             src = ctx.at[quarter * s : quarter * (s + 1)]
-            net.start(src, ct.at[t], ct_z + t, (d, s), when=t != s)
+            net.start(src, ct.at[t], ct_z, (d, s), when=t != s)
     ct[t] = ctx[own_rows, :]
 
     up.middle()
     gather_o.late()
     gather_o.end()
-    for k in range(1, 4):
-        s = (t + k) % 4
-        net.wait(ct.at[s], ct_z + s)
+    net.wait(ct.at[0:3], ct_z)
     attended = nt(ct[0], wo[0].reshape(width, local))
     for s in range(1, 4):
         attended = attended + nt(ct[s], wo[s].reshape(width, local))
@@ -817,35 +837,33 @@
     near = pl.ds(2 * pair, 2)
     away = pl.ds(2 - 2 * pair, 2)
 
-    def feed(half, q):
-        hidden = nn(act[half, chunk[q]].reshape(2 * part, width), wf[0].reshape(width, width))
+    def feed(half):
+        hidden = nn(act[half].reshape(2 * quarter, width), wf[0].reshape(width, width))
         hidden = hidden + ubs[block][:1]
         bell = 0.5 * (1.0 + lax.erf(hidden * 0.7071067811865476))
         slope = bell + hidden * (0.3989422804014327 * jnp.exp(-0.5 * hidden * hidden))
-        gelu_d[half, chunk[q]] = slope.reshape(2, part, width)
-        gl[half, chunk[q]] = (hidden * bell).astype(BF).reshape(2, part, width)
-
-    def feed_out(half, q, partial_ref):
-        made = nt(gl[half, chunk[q]].reshape(2 * part, width), wf[1].reshape(width, width))
-        partial_ref[:, chunk[q]] = made.reshape(2, part, width)
-
-    feed(near, 0)
-    feed(near, 1)
-    for q in range(2):
-        rows_a.far(q)
-        feed(away, q)
+        gelu_d[half] = slope.reshape(2, quarter, width)
+        gl[half] = (hidden * bell).astype(BF).reshape(2, quarter, width)
+
+    def feed_out(half, partial_ref):
+        made = nt(gl[half].reshape(2 * quarter, width), wf[1].reshape(width, width))
+        partial_ref[...] = made.reshape(2, quarter, width)
+
+    feed(near)
+    rows_a.far(0)
+    rows_a.far(1)
+    feed(away)
     down.end()
     sum_f = RowSum(0)
-    feed_out(away, 0, part_o)
+    feed_out(away, part_o)
     sum_f.away(0)
-    feed_out(near, 0, part_m)
+    sum_f.away(1)
+    feed_out(near, part_m)
+    sum_f.across(0)
+    sum_f.across(1)
     sum_f.near(0)
-    feed_out(away, 1, part_o)
-    sum_f.away(1)
-    sum_f.across(0)
-    feed_out(near, 1, part_m)
     sum_f.near(1)
-    sum_f.across(1)
+    in_cot.wait()
     rows_u = RowGather(dub)
     gain_sum, shift_sum, bias_sum = 0.0, 0.0, 0.0
     for q in range(2):
@@ -868,41 +886,43 @@
     sv[1:2] = shift_sum
     sv[2:3] = bias_sum
 
-    def feed_back(half, q, partial_ref):
-        made = nn(dub[half, chunk[q]].reshape(2 * part, width), wf[1].reshape(width, width))
-        made = made * gelu_d[half, chunk[q]].reshape(2 * part, width)
+    def feed_back(half, rows_q, partial_ref):
+        count = 2 * (rows_q.stop - rows_q.start)
+        made = nn(dub[half, rows_q].reshape(count, width), wf[1].reshape(width, width))
+        made = made * gelu_d[half, rows_q].reshape(count, width)
         low = made.astype(BF)
-        dzb[half, chunk[q]] = low.reshape(2, part, width)
-        partial_ref[:, chunk[q]] = nt(low, wf[0].reshape(width, width)).reshape(2, part, width)
+        dzb[half, rows_q] = low.reshape(2, count // 2, width)
+        partial_ref[:, rows_q] = nt(low, wf[0].reshape(width, width)).reshape(2, count // 2, width)
         return jnp.sum(made, axis=0, keepdims=True)
 
     sum_b = RowSum(1)
-    up_sum = 0.0
-    for q in range(2):
-        rows_u.near(q)
-        up_sum = up_sum + feed_back(near, q, part_m)
-        sum_b.near(q)
+    rows_u.near(0)
+    rows_u.near(1)
+    up_sum = feed_back(near, slice(0, quarter), part_m)
+    sum_b.near(0)
+    sum_b.near(1)
     rows_u.middle(0)
     rows_u.far(0)
-    up_sum = up_sum + feed_back(away, 0, part_o)
+    up_sum = up_sum + feed_back(away, chunk[0], part_o)
     sum_b.away(0)
     rows_u.middle(1)
     sum_b.across(0)
     rows_u.far(1)
-    up_sum = up_sum + feed_back(away, 1, part_o)
+    up_sum = up_sum + feed_back(away, chunk[1], part_o)
     sum_b.away(1)
-    rank_rows = lax.broadcasted_iota(jnp.int32, (4, width), 0)
-    sv[8:12] = jnp.where(rank_rows == block, up_sum, 0.0)
+    sv[6:7] = up_sum
     half = width // 2
 
     class StripSum:
         def __init__(self, i):
-            self.i, self.bank = i, net.bank(6)
+            self.i, self.bank = i, net.bank(9)
             self.by_chip = wf.at[i].reshape(2, 2, 2, strip, width)
 
-        def begin(self, left, right):
+        def make(self, left, right):
             made = tn(left[...].reshape(4 * quarter, width), right[...].reshape(4 * quarter, width))
             wf[self.i] = made.astype(BF).reshape(8, strip, width)
+
+        def begin(self):
             net.start(
                 self.by_chip.at[:, 1 - x, :, :, :half], st_a.at[self.i], self.bank, (xn, t)
             )
@@ -914,60 +934,80 @@
             i = self.i
             net.wait(st_a.at[i], self.bank)
             st_a[i] = (st_a[i].astype(F32) + self.by_chip[:, x, :, :, :half].astype(F32)).astype(BF)
-            net.start(st_a.at[i, 1 - y], st_c.at[i], self.bank + 2, (yn, t))
+            for core in range(2):
+                net.start(
+                    st_a.at[i, 1 - y, core], st_c.at[i, c], self.bank + 2 + c,
+                    (2 * (yn // 2) + core, t),
+                )
+            net.start(st_a.at[i, y, 1 - c], st_g.at[i, 0], self.bank + 6, (sib, t))
             net.wait(st_b.at[i], self.bank + 1)
             st_b[i] = (st_b[i].astype(F32) + self.by_chip[y, :, :, :, half:].astype(F32)).astype(BF)
-            net.start(st_b.at[i, 1 - x], st_d.at[i], self.bank + 3, (xn, t))
-
-        def deliver(self):
-            i = self.i
-            net.wait(st_c.at[i], self.bank + 2)
-            st_e[i, :, :, :half] = (st_c[i].astype(F32) + st_a[i, y].astype(F32)).astype(BF)
-            net.wait(st_d.at[i], self.bank + 3)
-            st_e[i, :, :, half:] = (st_d[i].astype(F32) + st_b[i, x].astype(F32)).astype(BF)
-            slot = jnp.where(home, 0, 1)
             for core in range(2):
                 net.start(
-                    st_e.at[i, core], st_f.at[i, slot], self.bank + 4 + slot,
-                    (2 * (d // 2) + core, block),
-                    when=jnp.logical_or(c != core, jnp.logical_not(home)),
+                    st_b.at[i, 1 - x, core], st_d.at[i, c], self.bank + 4 + c,
+                    (2 * (xn // 2) + core, t),
                 )
-
-            @pl.when(home)
-            def _():
-                st_f[i, 0] = st_e[i, c]
+            net.start(st_b.at[i, x, 1 - c], st_g.at[i, 1], self.bank + 7, (sib, t))
+
+        def gather(self):
+            i = self.i
+            for core in range(2):
+                net.wait(st_c.at[i, core], self.bank + 2 + core)
+                net.wait(st_d.at[i, core], self.bank + 4 + core)
+            net.wait(st_g.at[i, 0], self.bank + 6)
+            net.wait(st_g.at[i, 1], self.bank + 7)
+            for whose, first, second in (
+                (c, st_a.at[i, y, c], st_b.at[i, x, c]), (1 - c, st_g.at[i, 0], st_g.at[i, 1])
+            ):
+                st_e[i, whose, :, :half] = (
+                    first[...].astype(F32) + st_c[i, whose].astype(F32)
+                ).astype(BF)
+                st_e[i, whose, :, half:] = (
+                    second[...].astype(F32) + st_d[i, whose].astype(F32)
+                ).astype(BF)
+
+        def deliver(self, when=None):
+            i = self.i
+            net.start(st_e.at[i, 1 - t // 2], st_f.at[i], self.bank + 8, (d, zq), when=when)
 
         def total(self):
             i = self.i
-            net.wait(st_f.at[i, 0], self.bank + 4, when=host != d)
-            net.wait(st_f.at[i, 1], self.bank + 5)
-            return st_f[i, 0].astype(F32) + st_f[i, 1].astype(F32)
+            net.wait(st_f.at[i], self.bank + 8)
+            return st_e[i, t // 2].astype(F32) + st_f[i].astype(F32)
 
     class SmallSum:
         def __init__(self, index):
-            self.index, self.bank = index, net.bank(3)
-
-        def start(self, step):
-            ref = small_s.at[self.index, step]
-            net.start(ref, small_r.at[self.index, step], self.bank + step, ((sib, xn, yn)[step], t))
+            self.index, self.bank = index, net.bank(2)
 
         def begin(self, values):
-            small_s[self.index, 0] = values
-            self.start(0)
-
-        def step(self, n):
-            net.wait(small_r.at[self.index, n - 1], self.bank + n - 1)
-            small_s[self.index, n] = small_s[self.index, n - 1] + small_r[self.index, n - 1]
-            if n < 3:
-                self.start(n)
+            i = self.index
+            small_s[i, 0] = values
+            for r in (xn, yn, dg):
+                net.start(small_s.at[i, 0], small_r.at[i, chip], self.bank, (r, t))
+            small_r[i, chip] = values
+
+        def plane(self):
+            i = self.index
+            net.wait(small_r.at[i, 0:3], self.bank)
+            total = small_r[i, 0]
+            for k in range(1, 4):
+                total = total + small_r[i, k]
+            small_s[i, 1] = total
+            net.start(small_s.at[i, 1], small_r.at[i, 4], self.bank + 1, (sib, t))
+
+        def cores(self):
+            net.wait(small_r.at[self.index, 4], self.bank + 1)
+            return small_s[self.index, 1], small_r[self.index, 4]
 
     net.settle("f")
     down_sum, up_sums = StripSum(1), StripSum(0)
-    down_sum.begin(dub, gl)
+    down_sum.make(dub, gl)
+    down_sum.begin()
     sum_b.across(1)
     line_out[1].begin()
-    up_sums.begin(act, dzb)
-    dc_z = net.bank(8)
+    up_sums.make(act, dzb)
+    up_sums.begin()
+    dc_z = net.bank(1)
     gain_sum, shift_sum, bias_sum, dhb = 0.0, 0.0, 0.0, []
     for q in range(2):
         da = a_s[chunk[q]] + sum_b.total(q)
@@ -978,7 +1018,7 @@
         for k in (2, 1, 3):
             s = (t + k) % 4
             dct[s, chunk[q]] = nn(dhb[q], wo[s].reshape(width, local)).astype(BF)
-            net.start(dct.at[s, chunk[q]], dc.at[t, chunk[q]], dc_z + 4 * q + t, (d, s))
+            net.start(dct.at[s, chunk[q]], dc.at[t, chunk[q]], dc_z, (d, s))
         dc[t, chunk[q]] = nn(dhb[q], wo[t].reshape(width, local)).astype(BF)
         gain_sum = gain_sum + jnp.sum(da * normal, axis=0, keepdims=True)
         shift_sum = shift_sum + jnp.sum(da, axis=0, keepdims=True)
@@ -991,6 +1031,7 @@
     sv[5:6] = bias_sum
     small_a = SmallSum(0)
     small_a.begin(sv[...])
+    down_sum.turn()
     net.settle("o")
     for s in range(4):
         wo[s] = tn(dhb, ct[s]).astype(BF).reshape(8, strip, local)
@@ -998,17 +1039,14 @@
     go_b = net.bank(1)
     net.start(by_core.at[:, :, 1 - c], go_r, go_b, (sib, t))
 
-    down_sum.turn()
+    net.wait(dc.at[0:3], dc_z)
+    up_sums.turn()
     net.wait(go_r, go_b)
     go_r[...] = (by_core[:, :, c].astype(F32) + go_r[...].astype(F32)).astype(BF)
-    rp_b = net.bank(4)
+    rp_b = net.bank(1)
     for r in (xn, yn, dg):
-        net.start(go_r.at[:, r // 2], rp.at[chip], rp_b + chip, (r, t))
+        net.start(go_r.at[:, r // 2], rp.at[chip], rp_b, (r, t))
     rp[chip] = go_r[:, chip]
-    for k in range(1, 4):
-        s = (t + k) % 4
-        for q in range(2):
-            net.wait(dc.at[s, chunk[q]], dc_z + 4 * q + s)
     dctx = dc[...].reshape(rows, local)
     for h in range(heads):
         dco[:, BLOCK * h : BLOCK * (h + 1)] = jnp.concatenate(
@@ -1030,9 +1068,9 @@
             dvv[h][lo:hi] += nn(weights.astype(BF), dco[at_q, at])
             dqq[h][at_q] = nn(kkt[h, :, lo:hi], dsb).T * SCALING
 
-    line_out[0].step(2)
-    line_out[1].step(2)
-    up_sums.turn()
+    down_sum.gather()
+    down_sum.deliver()
+    small_a.plane()
     for h in range(heads):
         base = 6 * HD * h
         first = jnp.where(is_word, dqq[h][...], 0.0)
@@ -1046,8 +1084,15 @@
             row, col = divmod(base + BLOCK * i, width)
             sv[row : row + 1, col : col + BLOCK] = jnp.sum(piece, axis=0, keepdims=True)
 
-    made = nt(dqkv[...], wq[...].reshape(width, 6 * local))
-    dzb[...] = made.astype(BF).reshape(4, quarter, width)
+    first_rows = pl.ds(pl.multiple_of(jnp.where(low_z, rows // 2, 0), 16), rows // 2)
+    other_rows = pl.ds(pl.multiple_of(jnp.where(low_z, 0, rows // 2), 16), rows // 2)
+    first_two = pl.ds(jnp.where(low_z, 2, 0), 2)
+    other_two = pl.ds(jnp.where(low_z, 0, 2), 2)
+
+    def back_to_input(rows_b, quarters):
+        made = nt(dqkv[rows_b, :], wq[...].reshape(width, 6 * local))
+        dzb[quarters] = made.astype(BF).reshape(2, quarter, width)
+
     line_dx, line_in = [], []
     for q in range(2):
         cut = pl.ds(part * q, part)
@@ -1064,10 +1109,24 @@
         ig_ref[0, pl.ds(pl.multiple_of(t * quarter + part * q, 16), part)] = total.astype(BF)
         line_in[q].begin()
 
-    for q, e in ((0, 3), (0, 2), (1, 3), (1, 2), (0, 1), (1, 1)):
+    back_to_input(first_rows, first_two)
+    for q, e in ((0, 3), (0, 2), (1, 3), (1, 2)):
         line_dx[q].depart(e)
-    down_sum.deliver()
-    small_a.step(1)
+    plane_sum, other_sum = small_a.cores()
+    first_core = c == 0
+    own_units, other_units = plane_sum[6:7], other_sum[6:7]
+    sent8[0:6] = plane_sum[0:6] + other_sum[0:6]
+    sent8[6:7] = jnp.where(first_core, own_units, other_units)
+    sent8[7:8] = jnp.where(first_core, other_units, own_units)
+    vz_b = net.bank(2)
+    for k in (2, 1, 3):
+        net.start(sent8, vz.at[t], vz_b, (d, (t + k) % 4), when=first_core)
+    vz[t] = sent8[...]
+    back_to_input(other_rows, other_two)
+    line_dx[0].depart(1)
+    line_dx[1].depart(1)
+    up_sums.gather()
+    up_sums.deliver(is_mid)
     small_b = SmallSum(1)
     small_b.begin(sv[...])
 
@@ -1076,72 +1135,76 @@
     q_by_core = wq.reshape(4, 2, strip, 6 * local)
     gq_b = net.bank(1)
     net.start(q_by_core.at[:, 1 - c], gq_r, gq_b, (sib, t))
+    line_out[0].step(2)
+    line_out[1].step(2)
     line_dx[0].through(3)
     line_dx[0].through(2)
-    small_a.step(2)
-    line_dx[1].through(3)
-    line_dx[1].through(2)
-    line_dx[0].pass_back()
     net.wait(gq_r, gq_b)
     gq_r[...] = (q_by_core[:, c].astype(F32) + gq_r[...].astype(F32)).astype(BF)
-    gp_b = net.bank(4)
+    gp_b = net.bank(1)
     for r in (xn, yn, dg):
-        net.start(gq_r.at[r // 2], gp.at[chip], gp_b + chip, (r, t))
+        net.start(gq_r.at[r // 2], gp.at[chip], gp_b, (r, t))
     gp[chip] = gq_r[chip]
 
-    line_dx[1].pass_back()
-    arrive(0)
-    arrive(1)
-    up_sums.deliver()
-    small_a.step(3)
-    vz_b = net.bank(5)
-    mine8 = pl.ds(pl.multiple_of(8 * c, 8), 8)
-    sent8 = small_s.at[0, 3, mine8]
-    for k in range(1, 4):
-        net.start(sent8, vz.at[t], vz_b + t, (d, (t + k) % 4))
-    vz[t] = sent8[...]
-    small_b.step(1)
-    line_in[0].step(1)
-    line_in[1].step(1)
-    for r in (xn, yn, dg):
-        net.wait(rp.at[r // 2], rp_b + r // 2)
+    line_dx[0].pass_back()
+    net.wait(rp.at[0:3], rp_b)
     total = rp[0].astype(F32)
     for k in range(1, 4):
         total = total + rp[k].astype(F32)
     sp[...] = total.astype(BF)
-    rz_b = net.bank(4)
-    for k in range(1, 4):
-        s = (t + k) % 4
-        net.start(sp.at[s], rz.at[t], rz_b + t, (d, s))
+    rz_b = net.bank(1)
     rz[t] = sp[t]
 
-    small_b.step(2)
-    for k in range(1, 4):
-        net.wait(vz.at[(t + k) % 4], vz_b + (t + k) % 4)
-    total = vz[0]
-    for k in range(1, 4):
-        total = total + vz[k]
-    sw[mine8] = total
-    net.start(sw.at[mine8], sw.at[mine8], vz_b + 4, (sib, t))
+    def send_rz(when):
+        for k in range(1, 4):
+            s = (t + k) % 4
+            net.start(sp.at[s], rz.at[t], rz_b, (d, s), when=when)
+
+    send_rz(is_mid)
+    line_dx[1].through(3)
+    line_dx[1].through(2)
+    line_dx[1].pass_back()
+    line_out[0].step(3)
+    line_out[1].step(3)
+    ends = [Local(out_ref, out_end)]
+    arrive(0)
+    arrive(1)
+
+    up_sums.deliver(is_end)
+    send_rz(is_end)
+    line_in[0].step(1)
+    line_in[1].step(1)
     line_in[0].step(2)
     line_in[1].step(2)
-    small_b.step(3)
-    net.wait(sw.at[pl.ds(pl.multiple_of(8 - 8 * c, 8), 8)], vz_b + 4)
-    small_ref[0:6] = sw[0:6]
-    small_ref[6:7] = jnp.sum(jnp.where(rank_rows == t, sw[8:12], 0.0), axis=0, keepdims=True)
-    small_ref[8:10] = small_s[1, 3, 0:2]
+    small_b.plane()
+    net.wait(vz.at[0:3], vz_b, when=first_core)
+
+    @pl.when(first_core)
+    def _():
+        total = vz[0]
+        for k in range(1, 4):
+            total = total + vz[k]
+        sw[0:6] = total[0:6]
+        units = vz[t] + vz[zq]
+        sw[6:7] = jnp.where(t < 2, units[6:7], units[7:8])
+        sw[7:8] = units[7:8]
+
+    net.start(sw, sw, vz_b + 1, (sib, t), when=first_core)
+    net.wait(sw, vz_b + 1, when=c == 1)
+    small_ref[0:8] = sw[...]
+    plane_sum, other_sum = small_b.cores()
+    small_ref[8:16] = plane_sum + other_sum
     dg_ref[...] = down_sum.total()
     ug_ref[...] = up_sums.total()
-    for k in range(1, 4):
-        s = (t + k) % 4
-        net.wait(rz.at[s], rz_b + s)
+    ends += [Local(dg_ref, dg_end), Local(ug_ref, ug_end), Local(small_ref, small_end)]
+    net.wait(rz.at[0:3], rz_b)
     total = rz[0].astype(F32)
     for s in range(1, 4):
         total = total + rz[s].astype(F32)
     og_ref[...] = wide_t(total, BLOCK, 256)[:local, :strip]
 
-    for r in (xn, yn, dg):
-        net.wait(gp.at[r // 2], gp_b + r // 2)
+    ends += [Local(og_ref, og_end)]
+    net.wait(gp.at[0:3], gp_b)
     total = gp[0].astype(F32)
     for k in range(1, 4):
         total = total + gp[k].astype(F32)
@@ -1153,12 +1216,14 @@
         kg_ref[:, at] = total[:, base + 4 * HD : base + 5 * HD]
         vg_ref[:, at] = total[:, base + 5 * HD : base + 6 * HD]
 
-    line_out[0].step(3)
-    line_out[1].step(3)
+    ends += [Local(qg_ref, qg_end), Local(kg_ref, kg_end), Local(vg_ref, vg_end)]
     for q in range(2):
         line_in[q].step(3)
+    ends += [Local(ig_ref, ig_end)]
     net.settle()
-    assert net.sends <= SENDS and net.banks <= RECVS, (net.sends, net.banks)
+    for copy in ends:
+        copy.wait()
+    assert net.banks == RECVS, net.banks
 
 
 def end_kernel(*refs):
@@ -1205,6 +1270,10 @@
     ]
     v = pltpu.VMEM
     scratch = [
+        v(layer_input.shape, BF), v(query_weight.shape, F32), v(key_weight.shape, F32),
+        v(value_weight.shape, F32), v(out_weight.shape, F32), v(up_weight.shape, F32),
+        v((strip, width), F32), v(cotangent.shape, BF),
+    ] + [v(o.shape, o.dtype) for o in outs] + [
         v((8, strip, 6 * local), BF), v((4, 8, strip, local), BF), v((2, strip, width), BF),
         v((2, 8, strip, width), BF), v((4, 8, width), F32), v((rows, BLOCK), F32),
         v((rows, BLOCK), F32), v((width, rows), BF), v((1, 6 * local), F32),
@@ -1218,7 +1287,8 @@
         v((4, quarter, width), BF), v((4, quarter, width), BF),
         v((2, 2, 2, strip, width // 2), BF), v((2, 2, 2, strip, width // 2), BF),
         v((2, 2, strip, width // 2), BF), v((2, 2, strip, width // 2), BF),
-        v((2, 2, strip, width), BF), v((2, 2, strip, width), BF),
+        v((2, 2, strip, width), BF), v((2, strip, width), BF),
+        v((2, 2, strip, width // 2), BF),
         v((4, quarter, local), BF), v((4, quarter, local), BF),
         v((rows, heads * BLOCK), BF),
         v((4, 4, strip, local), BF), v((4, 4, strip, local), BF), v((4, strip, local), BF),
@@ -1227,16 +1297,19 @@
         v((2, 3, quarter // 2, width), BF), v((2, 2, quarter // 2, width), BF),
         v((2, quarter // 2, width), BF),
         v((4, strip, 6 * local), BF), v((4, strip, 6 * local), BF),
-        v((16, width), F32), v((2, 4, 16, width), F32), v((2, 3, 16, width), F32),
-        v((16, width), F32), v((4, 8, width), F32),
+        v((8, width), F32), v((2, 2, 8, width), F32), v((2, 5, 8, width), F32),
+        v((8, width), F32), v((8, width), F32), v((4, 8, width), F32),
         pltpu.SemaphoreType.DMA((SENDS,)), pltpu.SemaphoreType.DMA((RECVS,)),
+        pltpu.SemaphoreType.DMA((17,)),
     ]
     spec = pl.BlockSpec(memory_space=pltpu.VMEM)
+    anywhere = pl.BlockSpec(memory_space=pl.ANY)
+    large_args = (0, 3, 4, 5, 6, 7, 8, 18)
     made = pl.pallas_call(
         layer_kernel,
         out_shape=outs,
-        in_specs=[spec] * len(args),
-        out_specs=[spec] * len(outs),
+        in_specs=[anywhere if n in large_args else spec for n in range(len(args))],
+        out_specs=[anywhere] * len(outs),
         scratch_shapes=scratch,
         compiler_params=pltpu.CompilerParams(
             collective_id=0, has_side_effects=True, vmem_limit_bytes=58 << 20

time: 143 us -> 135 us (0.944)
  Pallas kernels: 142 us -> 134 us
    pallas_call x1, Pallas kernels: 139 us -> 131 us  [fused(): pl.pallas_call(layer_kernel, out_shape=outs, in_specs=[anywhere if n in l...]
where the time goes in v4:
time: 135 us
  Pallas kernels  134 us (99%)
    pallas_call x1, Pallas kernels, fused(): pl.pallas_call(layer_kernel, out_shape=outs, in_specs=[anywhere if n in l...  131 us
    pallas_call x1, Pallas kernels, fused(): pl.pallas_call(end_kernel, out_shape=[like(v, v.dtype) for v in large] +...  3.65 us

profile of v4, /device:TPU:0, one launch (start us, length us, event | category | flops | bytes accessed | tf_op | source)
XLA Modules:
  0.0 135.1 jit_solution(14006848414978336436)
XLA Ops:
  0.7 130.6 %layer.1 = (bf16[1,640,768]{2,1,0:T(8,128)(2,1)}, bf16[1,640,768]{2,1,0:T(8,128)(2,1)}, f32[4,96,192]{2,1,0:T(8,128)}, f32[96,192]{1,0:T(8,128)}, f32[96,192]{1,...) custom-call(bf16[1,640,768]{2,1,0:T(8,128)(2,1)} %x_in.1, ...), custom_call_target="tpu_custom_call" | custom-call | tf_op jit(solution)/shard_map/layer/pallas_call | solution.py:1308
  131.3 3.6 %finish.1 = (bf16[1,640,768]{2,1,0:T(8,128)(2,1)}, bf16[1,640,768]{2,1,0:T(8,128)(2,1)}, f32[4,96,192]{2,1,0:T(8,128)}, f32[96,192]{1,0:T(8,128)}, f32[96,192]{1...) custom-call(bf16[1,640,768]{2,1,0:T(8,128)(2,1)} %get-tuple-element., ...), custom_call_target="tpu_custom_call" | custom-call | tf_op jit(solution)/shard_map/finish/pallas_call | solution.py:1321

commit v5 on v4

--- a/solution.py
+++ b/solution.py
@@ -433,7 +433,7 @@
     out_end, ig_end, qg_end, kg_end, vg_end, og_end, ug_end, dg_end, small_end,
     x_ref, qw_ref, kw_ref, vw_ref, ow_ref, uw_ref, dw_ref, cot_ref,
     out_ref, ig_ref, qg_ref, kg_ref, vg_ref, og_ref, ug_ref, dg_ref, small_ref,
-    wq, wo, own, wf, ubs, segc, wordc, xt, bias, qq, kv, kk, kvt, kkt, probs, ctx, ct,
+    wq, wop, wo, own, wf, ubs, segc, wordc, xt, bias, qq, kv, kk, kvt, kkt, probs, ctx, ctp, ct, ctc,
     a_s, n1_s, r1_s, act, gelu_d, gl, parts, rs_send, rs_recv, dub, dzb,
     st_a, st_b, st_c, st_d, st_e, st_f, st_g, dct, dc, dco, go_r, rp, sp, rz,
     dqkv, dx_in, dx_cross, dx_back, gq_r, gp, sv, small_s, small_r, sent8, sw, vz,
@@ -628,7 +628,18 @@
 
     for arrived in (in_o, in_u, in_d):
         arrived.wait()
-    wo[t, d] = wide_t(ow_ref[...], 256, 128)[:strip, :local].astype(BF)
+    def pack(block):
+        most = block.shape[0] // 2
+        rest = block[:, BLOCK:]
+        return jnp.concatenate(
+            [block[:, :BLOCK], jnp.concatenate([rest[:most], rest[most:]], axis=1)], axis=0
+        )
+
+    def rest_of(packed, count):
+        below = packed[count:]
+        return jnp.concatenate([below[:, :HD], below[: count - below.shape[0], HD:]], axis=0)
+
+    wop[t, d] = pack(wide_t(ow_ref[...], 256, 128)[:strip, :local]).astype(BF)
     own[0] = uw_ref[...].astype(BF)
     own[1] = dw_ref[...].astype(BF)
     ubs[t] = jnp.broadcast_to(ub_ref[...][None], ubs.shape[1:])
@@ -676,7 +687,7 @@
     up, down = ChipGather(0), ChipGather(1)
     wo_z = net.bank(1)
     for k in (2, 1, 3):
-        net.start(wo.at[t, d], wo.at[t, d], wo_z, (d, (t + k) % 4), group="o")
+        net.start(wop.at[t, d], wop.at[t, d], wo_z, (d, (t + k) % 4))
     for b in range(blocks):
         at = slice(BLOCK * b, BLOCK * (b + 1))
         segc[at, :] = jnp.broadcast_to(seg_ref[:, at].astype(F32), (BLOCK, BLOCK)).T
@@ -691,8 +702,8 @@
         )
 
     gather_q.middle()
-    net.wait(wo.at[0:3, d], wo_z)
-    gather_o = PlaneGather("o", lambda b: wo.at[0:2, b], lambda b: wo.at[2:4, b])
+    net.wait(wop.at[0:3, d], wo_z)
+    gather_o = PlaneGather("o", lambda b: wop.at[0:2, b], lambda b: wop.at[2:4, b])
     gather_o.begin()
     up.send()
     net.start(ubs.at[t], ubs.at[t], ub_z, (d, zq))
@@ -744,17 +755,30 @@
             down.begin()
         if b > 0:
             s = b - 1
-            src = ctx.at[quarter * s : quarter * (s + 1)]
-            net.start(src, ct.at[t], ct_z, (d, s), when=t != s)
-    ct[t] = ctx[own_rows, :]
+            ctp[s] = pack(ctx[quarter * s : quarter * (s + 1), :])
+            net.start(ctp.at[s], ct.at[t], ct_z, (d, s), when=t != s)
+    ct[t] = ctp[t]
 
     up.middle()
     gather_o.late()
     gather_o.end()
+    for s in range(4):
+        wo[:, :, BLOCK * s : BLOCK * (s + 1)] = wop[s, :, :strip]
+    most = strip // 2
+    for s in (0, 2):
+        at = slice(4 * BLOCK + HD * s, 4 * BLOCK + HD * (s + 2))
+        one, other = wop[s, :, strip:], wop[s + 1, :, strip:]
+        wo[:, :most, at] = jnp.concatenate([one[:, :, :HD], other[:, :, :HD]], axis=2)
+        wo[:, most:, at] = jnp.concatenate([one[:, :, HD:], other[:, :, HD:]], axis=2)
     net.wait(ct.at[0:3], ct_z)
-    attended = nt(ct[0], wo[0].reshape(width, local))
-    for s in range(1, 4):
-        attended = attended + nt(ct[s], wo[s].reshape(width, local))
+    for s in range(4):
+        ctc[:, BLOCK * s : BLOCK * (s + 1)] = ct[s, :quarter]
+    for s in (0, 2):
+        ctc[:, 4 * BLOCK + HD * s : 4 * BLOCK + HD * (s + 2)] = jnp.concatenate(
+            [rest_of(ct[s], quarter), rest_of(ct[s + 1], quarter)], axis=1
+        )
+    whole_wo = wo.reshape(width, width)
+    attended = nt(ctc[...], whole_wo[...])
     normal, inverse = norm_rows(x_ref[0, own_rows, :].astype(F32) + attended + ob_ref[...][None])
     n1_s[...] = normal
     r1_s[...] = jnp.broadcast_to(inverse, r1_s.shape)
@@ -1015,11 +1039,22 @@
         dh = norm_rows_back(da, normal, r1_s[chunk[q], :1], ag_ref[...][None])
         a_s[chunk[q]] = dh
         dhb.append(dh.astype(BF))
+        made = nn(dhb[q], whole_wo[...])
+        for s in range(4):
+            rest = made[:, 4 * BLOCK + HD * s : 4 * BLOCK + HD * (s + 1)]
+            rest = jnp.concatenate([rest, jnp.zeros((16, HD), F32)], axis=0)
+            most = (part + 16) // 2
+            dct[s, q] = jnp.concatenate(
+                [
+                    made[:, BLOCK * s : BLOCK * (s + 1)],
+                    jnp.concatenate([rest[:most], rest[most:]], axis=1),
+                ],
+                axis=0,
+            ).astype(BF)
         for k in (2, 1, 3):
             s = (t + k) % 4
-            dct[s, chunk[q]] = nn(dhb[q], wo[s].reshape(width, local)).astype(BF)
-            net.start(dct.at[s, chunk[q]], dc.at[t, chunk[q]], dc_z, (d, s))
-        dc[t, chunk[q]] = nn(dhb[q], wo[t].reshape(width, local)).astype(BF)
+            net.start(dct.at[s, q], dc.at[t, q], dc_z, (d, s))
+        dc[t, q] = dct[t, q]
         gain_sum = gain_sum + jnp.sum(da * normal, axis=0, keepdims=True)
         shift_sum = shift_sum + jnp.sum(da, axis=0, keepdims=True)
         bias_sum = bias_sum + jnp.sum(dh, axis=0, keepdims=True)
@@ -1032,26 +1067,29 @@
     small_a = SmallSum(0)
     small_a.begin(sv[...])
     down_sum.turn()
-    net.settle("o")
-    for s in range(4):
-        wo[s] = tn(dhb, ct[s]).astype(BF).reshape(8, strip, local)
-    by_core = wo.reshape(4, 4, 2, strip, local)
+    wo[...] = tn(dhb, ctc[...]).astype(BF).reshape(8, strip, width)
+    by_core = wo.reshape(4, 2, strip, width)
     go_b = net.bank(1)
-    net.start(by_core.at[:, :, 1 - c], go_r, go_b, (sib, t))
+    net.start(by_core.at[:, 1 - c], go_r, go_b, (sib, t))
 
     net.wait(dc.at[0:3], dc_z)
     up_sums.turn()
     net.wait(go_r, go_b)
-    go_r[...] = (by_core[:, :, c].astype(F32) + go_r[...].astype(F32)).astype(BF)
+    go_r[...] = (by_core[:, c].astype(F32) + go_r[...].astype(F32)).astype(BF)
     rp_b = net.bank(1)
     for r in (xn, yn, dg):
-        net.start(go_r.at[:, r // 2], rp.at[chip], rp_b, (r, t))
-    rp[chip] = go_r[:, chip]
-    dctx = dc[...].reshape(rows, local)
-    for h in range(heads):
-        dco[:, BLOCK * h : BLOCK * (h + 1)] = jnp.concatenate(
-            [jnp.zeros((rows, HD), BF), dctx[:, HD * h : HD * (h + 1)]], axis=1
-        )
+        net.start(go_r.at[r // 2], rp.at[chip], rp_b, (r, t))
+    rp[chip] = go_r[chip]
+    upper = lax.broadcasted_iota(jnp.int32, (part, BLOCK), 1) >= HD
+    for s in range(4):
+        for q in range(2):
+            got = dc[s, q]
+            at_q = slice(quarter * s + part * q, quarter * s + part * (q + 1))
+            first = got[:part].astype(F32)
+            blank = jnp.zeros((part, HD), BF)
+            dco[at_q, :BLOCK] = jnp.concatenate([blank, got[:part, :HD]], axis=1)
+            dco[at_q, BLOCK : 2 * BLOCK] = jnp.where(upper, first, 0.0).astype(BF)
+            dco[at_q, 2 * BLOCK :] = jnp.concatenate([blank, rest_of(got, part)], axis=1)
     for h in range(heads):
         dkk[h][...] = jnp.zeros((rows, BLOCK), F32)
         dvv[h][...] = jnp.zeros((rows, BLOCK), F32)
@@ -1151,7 +1189,11 @@
     total = rp[0].astype(F32)
     for k in range(1, 4):
         total = total + rp[k].astype(F32)
-    sp[...] = total.astype(BF)
+    for s in range(4):
+        rest = total[:, 4 * BLOCK + HD * s : 4 * BLOCK + HD * (s + 1)]
+        sp[s] = pack(
+            jnp.concatenate([total[:, BLOCK * s : BLOCK * (s + 1)], rest], axis=1)
+        ).astype(BF)
     rz_b = net.bank(1)
     rz[t] = sp[t]
 
@@ -1160,13 +1202,10 @@
             s = (t + k) % 4
             net.start(sp.at[s], rz.at[t], rz_b, (d, s), when=when)
 
-    send_rz(is_mid)
     line_dx[1].through(3)
     line_dx[1].through(2)
     line_dx[1].pass_back()
-    line_out[0].step(3)
-    line_out[1].step(3)
-    ends = [Local(out_ref, out_end)]
+    send_rz(is_mid)
     arrive(0)
     arrive(1)
 
@@ -1174,6 +1213,9 @@
     send_rz(is_end)
     line_in[0].step(1)
     line_in[1].step(1)
+    line_out[0].step(3)
+    line_out[1].step(3)
+    ends = [Local(out_ref, out_end)]
     line_in[0].step(2)
     line_in[1].step(2)
     small_b.plane()
@@ -1201,6 +1243,7 @@
     total = rz[0].astype(F32)
     for s in range(1, 4):
         total = total + rz[s].astype(F32)
+    total = jnp.concatenate([total[:strip], rest_of(total, strip)], axis=1)
     og_ref[...] = wide_t(total, BLOCK, 256)[:local, :strip]
 
     ends += [Local(og_ref, og_end)]
@@ -1274,12 +1317,14 @@
         v(value_weight.shape, F32), v(out_weight.shape, F32), v(up_weight.shape, F32),
         v((strip, width), F32), v(cotangent.shape, BF),
     ] + [v(o.shape, o.dtype) for o in outs] + [
-        v((8, strip, 6 * local), BF), v((4, 8, strip, local), BF), v((2, strip, width), BF),
+        v((8, strip, 6 * local), BF), v((4, 8, 3 * strip // 2, BLOCK), BF), v((8, strip, width), BF),
+        v((2, strip, width), BF),
         v((2, 8, strip, width), BF), v((4, 8, width), F32), v((rows, BLOCK), F32),
         v((rows, BLOCK), F32), v((width, rows), BF), v((1, 6 * local), F32),
         v((rows, heads * BLOCK), BF), v((rows, heads * BLOCK), BF), v((rows, heads * BLOCK), BF),
         v((heads, HD, rows), BF), v((heads, BLOCK, rows), BF),
-        v((heads, kept, BLOCK), F32), v((rows, local), BF), v((4, quarter, local), BF),
+        v((heads, kept, BLOCK), F32), v((rows, local), BF), v((4, 3 * quarter // 2, BLOCK), BF),
+        v((4, 3 * quarter // 2, BLOCK), BF), v((quarter, width), BF),
         v((quarter, width), F32), v((quarter, width), F32), v((quarter, BLOCK), F32),
         v((4, quarter, width), BF), v((4, quarter, width), F32), v((4, quarter, width), BF),
         v((4, quarter, width), F32),
@@ -1289,10 +1334,10 @@
         v((2, 2, strip, width // 2), BF), v((2, 2, strip, width // 2), BF),
         v((2, 2, strip, width), BF), v((2, strip, width), BF),
         v((2, 2, strip, width // 2), BF),
-        v((4, quarter, local), BF), v((4, quarter, local), BF),
+        v((4, 2, BLOCK, BLOCK), BF), v((4, 2, BLOCK, BLOCK), BF),
         v((rows, heads * BLOCK), BF),
-        v((4, 4, strip, local), BF), v((4, 4, strip, local), BF), v((4, strip, local), BF),
-        v((4, strip, local), BF),
+        v((4, strip, width), BF), v((4, strip, width), BF), v((4, 3 * strip // 2, BLOCK), BF),
+        v((4, 3 * strip // 2, BLOCK), BF),
         v((rows, 6 * local), BF),
         v((2, 3, quarter // 2, width), BF), v((2, 2, quarter // 2, width), BF),
         v((2, quarter // 2, width), BF),

time: 135 us -> 132 us (0.978)
  Pallas kernels: 134 us -> 131 us
    pallas_call x1, Pallas kernels: 131 us -> 128 us  [fused(): pl.pallas_call(layer_kernel, out_shape=outs, in_specs=[anywhere if n in l...]
where the time goes in v5:
time: 132 us
  Pallas kernels  131 us (99%)
    pallas_call x1, Pallas kernels, fused(): pl.pallas_call(layer_kernel, out_shape=outs, in_specs=[anywhere if n in l...  128 us
    pallas_call x1, Pallas kernels, fused(): pl.pallas_call(end_kernel, out_shape=[like(v, v.dtype) for v in large] +...  3.65 us

profile of v5, /device:TPU:0, one launch (start us, length us, event | category | flops | bytes accessed | tf_op | source)
XLA Modules:
  0.0 132.1 jit_solution(6208243720007701198)
XLA Ops:
  0.7 127.7 %layer.1 = (bf16[1,640,768]{2,1,0:T(8,128)(2,1)}, bf16[1,640,768]{2,1,0:T(8,128)(2,1)}, f32[4,96,192]{2,1,0:T(8,128)}, f32[96,192]{1,0:T(8,128)}, f32[96,192]{1,...) custom-call(bf16[1,640,768]{2,1,0:T(8,128)(2,1)} %x_in.1, ...), custom_call_target="tpu_custom_call" | custom-call | tf_op jit(solution)/shard_map/layer/pallas_call | solution.py:1353
  128.3 3.6 %finish.1 = (bf16[1,640,768]{2,1,0:T(8,128)(2,1)}, bf16[1,640,768]{2,1,0:T(8,128)(2,1)}, f32[4,96,192]{2,1,0:T(8,128)}, f32[96,192]{1,0:T(8,128)}, f32[96,192]{1...) custom-call(bf16[1,640,768]{2,1,0:T(8,128)(2,1)} %get-tuple-element., ...), custom_call_target="tpu_custom_call" | custom-call | tf_op jit(solution)/shard_map/finish/pallas_call | solution.py:1366

commit v6 on v5

--- a/solution.py
+++ b/solution.py
@@ -601,6 +601,8 @@
             self.copy(1, xn, yn)
             self.copy(0, yn, sib)
             self.copy(1, xn, sib)
+
+        def middle2(self):
             for view, block in ((1, yn), (0, xn)):
                 self.wait(view, block)
                 self.copy(view, block, sib)
@@ -651,28 +653,31 @@
         def __init__(self, i):
             self.i, self.bank = i, net.bank(8)
 
-        def send(self):
+        def send_near(self):
             i = self.i
-            for plane, when in ((zq, None), (t, host != d)):
-                net.start(own.at[i], wf.at[i, d], wf_a + 2 * i + c, (host, plane), when=when)
+            net.start(own.at[i], wf.at[i, d], wf_a + 2 * i + c, (host, t), when=host != d)
 
             @pl.when(host == d)
             def _():
                 wf[i, d] = own[i]
 
-        def copy(self, view, of, device):
+        def send_far(self):
+            net.start(own.at[self.i], wf.at[self.i, d], wf_a + 2 * self.i + c, (host, zq))
+
+        def copy(self, view, of, device, when=None):
             ref = wf.at[self.i, 2 * (of // 2) + view]
-            net.start(ref, ref, self.bank + 2 * (of // 2) + view, (device, t), group="f")
+            net.start(ref, ref, self.bank + 2 * (of // 2) + view, (device, t), when=when, group="f")
 
         def wait(self, view, of):
             net.wait(wf.at[self.i, 2 * (of // 2) + view], self.bank + 2 * (of // 2) + view)
 
-        def begin(self):
-            i = self.i
-            net.wait(wf.at[i, d], wf_a + 2 * i + c, when=jnp.logical_not(home))
-            net.wait(wf.at[i, sib], wf_a + 2 * i + 1 - c)
+        def begin(self, at_home):
+            i, when = self.i, home if at_home else jnp.logical_not(home)
+            if not at_home:
+                net.wait(wf.at[i, d], wf_a + 2 * i + c, when=when)
+            net.wait(wf.at[i, sib], wf_a + 2 * i + 1 - c, when=when)
             for view, device in ((0, yn), (1, xn), (1, yn), (0, xn)):
-                self.copy(view, d, device)
+                self.copy(view, d, device, when)
 
         def middle(self):
             self.wait(0, yn)
@@ -688,6 +693,8 @@
     wo_z = net.bank(1)
     for k in (2, 1, 3):
         net.start(wop.at[t, d], wop.at[t, d], wo_z, (d, (t + k) % 4))
+    up.send_near()
+    down.send_near()
     for b in range(blocks):
         at = slice(BLOCK * b, BLOCK * (b + 1))
         segc[at, :] = jnp.broadcast_to(seg_ref[:, at].astype(F32), (BLOCK, BLOCK)).T
@@ -702,12 +709,14 @@
         )
 
     gather_q.middle()
+    up.send_far()
+    net.start(ubs.at[t], ubs.at[t], ub_z, (d, zq))
+    down.send_far()
+    gather_q.middle2()
     net.wait(wop.at[0:3, d], wo_z)
     gather_o = PlaneGather("o", lambda b: wop.at[0:2, b], lambda b: wop.at[2:4, b])
     gather_o.begin()
-    up.send()
-    net.start(ubs.at[t], ubs.at[t], ub_z, (d, zq))
-    down.send()
+    up.begin(True)
     gather_q.late()
     gather_q.end()
     low_half = lax.broadcasted_iota(jnp.int32, (rows, BLOCK), 1) < HD
@@ -727,7 +736,7 @@
         kkt[h] = keys.T.astype(BF)
 
     gather_o.middle()
-    up.begin()
+    gather_o.middle2()
     ct_z = net.bank(1)
 
     def span(b):
@@ -751,16 +760,18 @@
             found.append(nn(kvt[h, :, lo:hi], weights.astype(BF)))
         found.append(jnp.zeros((HD, BLOCK), F32))
         ctx[at_q, :] = jnp.concatenate(found, axis=0).T[:, :local].astype(BF)
-        if b == 3:
-            down.begin()
+        if b == 2:
+            up.begin(False)
         if b > 0:
             s = b - 1
             ctp[s] = pack(ctx[quarter * s : quarter * (s + 1), :])
             net.start(ctp.at[s], ct.at[t], ct_z, (d, s), when=t != s)
     ct[t] = ctp[t]
 
+    down.begin(True)
+    gather_o.late()
+    down.begin(False)
     up.middle()
-    gather_o.late()
     gather_o.end()
     for s in range(4):
         wo[:, :, BLOCK * s : BLOCK * (s + 1)] = wop[s, :, :strip]
@@ -1029,6 +1040,7 @@
     down_sum.begin()
     sum_b.across(1)
     line_out[1].begin()
+    line_out[0].step(1)
     up_sums.make(act, dzb)
     up_sums.begin()
     dc_z = net.bank(1)
@@ -1059,7 +1071,6 @@
         shift_sum = shift_sum + jnp.sum(da, axis=0, keepdims=True)
         bias_sum = bias_sum + jnp.sum(dh, axis=0, keepdims=True)
     dhb = jnp.concatenate(dhb, axis=0)
-    line_out[0].step(1)
     line_out[1].step(1)
     sv[3:4] = gain_sum
     sv[4:5] = shift_sum
@@ -1080,6 +1091,7 @@
     for r in (xn, yn, dg):
         net.start(go_r.at[r // 2], rp.at[chip], rp_b, (r, t))
     rp[chip] = go_r[chip]
+    line_out[0].step(2)
     upper = lax.broadcasted_iota(jnp.int32, (part, BLOCK), 1) >= HD
     for s in range(4):
         for q in range(2):
@@ -1096,6 +1108,9 @@
     for b in range(blocks):
         lo, hi = span(b)
         at_q = slice(BLOCK * b, BLOCK * (b + 1))
+        if b == 4:
+            down_sum.gather()
+            down_sum.deliver()
         for h in range(heads):
             at = slice(BLOCK * h, BLOCK * (h + 1))
             weights = probs[h, kept[b] : kept[b + 1]]
@@ -1106,8 +1121,7 @@
             dvv[h][lo:hi] += nn(weights.astype(BF), dco[at_q, at])
             dqq[h][at_q] = nn(kkt[h, :, lo:hi], dsb).T * SCALING
 
-    down_sum.gather()
-    down_sum.deliver()
+    line_out[1].step(2)
     small_a.plane()
     for h in range(heads):
         base = 6 * HD * h
@@ -1150,6 +1164,8 @@
     back_to_input(first_rows, first_two)
     for q, e in ((0, 3), (0, 2), (1, 3), (1, 2)):
         line_dx[q].depart(e)
+    up_sums.gather()
+    up_sums.deliver(is_mid)
     plane_sum, other_sum = small_a.cores()
     first_core = c == 0
     own_units, other_units = plane_sum[6:7], other_sum[6:7]
@@ -1163,8 +1179,6 @@
     back_to_input(other_rows, other_two)
     line_dx[0].depart(1)
     line_dx[1].depart(1)
-    up_sums.gather()
-    up_sums.deliver(is_mid)
     small_b = SmallSum(1)
     small_b.begin(sv[...])
 
@@ -1173,8 +1187,6 @@
     q_by_core = wq.reshape(4, 2, strip, 6 * local)
     gq_b = net.bank(1)
     net.start(q_by_core.at[:, 1 - c], gq_r, gq_b, (sib, t))
-    line_out[0].step(2)
-    line_out[1].step(2)
     line_dx[0].through(3)
     line_dx[0].through(2)
     net.wait(gq_r, gq_b)
@@ -1205,14 +1217,13 @@
     line_dx[1].through(3)
     line_dx[1].through(2)
     line_dx[1].pass_back()
-    send_rz(is_mid)
     arrive(0)
     arrive(1)
 
-    up_sums.deliver(is_end)
-    send_rz(is_end)
     line_in[0].step(1)
     line_in[1].step(1)
+    up_sums.deliver(is_end)
+    send_rz(None)
     line_out[0].step(3)
     line_out[1].step(3)
     ends = [Local(out_ref, out_end)]

time: 132 us -> 129 us (0.977)
  Pallas kernels: 131 us -> 128 us
    pallas_call x1, Pallas kernels: 128 us -> 125 us  [fused(): pl.pallas_call(layer_kernel, out_shape=outs, in_specs=[anywhere if n in l...]
where the time goes in v6:
time: 129 us
  Pallas kernels  128 us (99%)
    pallas_call x1, Pallas kernels, fused(): pl.pallas_call(layer_kernel, out_shape=outs, in_specs=[anywhere if n in l...  125 us
    pallas_call x1, Pallas kernels, fused(): pl.pallas_call(end_kernel, out_shape=[like(v, v.dtype) for v in large] +...  3.65 us

profile of v6, /device:TPU:0, one launch (start us, length us, event | category | flops | bytes accessed | tf_op | source)
XLA Modules:
  0.0 129.1 jit_solution(1534548266022566679)
XLA Ops:
  0.7 124.7 %layer.1 = (bf16[1,640,768]{2,1,0:T(8,128)(2,1)}, bf16[1,640,768]{2,1,0:T(8,128)(2,1)}, f32[4,96,192]{2,1,0:T(8,128)}, f32[96,192]{1,0:T(8,128)}, f32[96,192]{1,...) custom-call(bf16[1,640,768]{2,1,0:T(8,128)(2,1)} %x_in.1, ...), custom_call_target="tpu_custom_call" | custom-call | tf_op jit(solution)/shard_map/layer/pallas_call | solution.py:1364
  125.3 3.6 %finish.1 = (bf16[1,640,768]{2,1,0:T(8,128)(2,1)}, bf16[1,640,768]{2,1,0:T(8,128)(2,1)}, f32[4,96,192]{2,1,0:T(8,128)}, f32[96,192]{1,0:T(8,128)}, f32[96,192]{1...) custom-call(bf16[1,640,768]{2,1,0:T(8,128)(2,1)} %get-tuple-element., ...), custom_call_target="tpu_custom_call" | custom-call | tf_op jit(solution)/shard_map/finish/pallas_call | solution.py:1377

commit v7 on v6

--- a/solution.py
+++ b/solution.py
@@ -1039,10 +1039,7 @@
     down_sum.make(dub, gl)
     down_sum.begin()
     sum_b.across(1)
-    line_out[1].begin()
-    line_out[0].step(1)
     up_sums.make(act, dzb)
-    up_sums.begin()
     dc_z = net.bank(1)
     gain_sum, shift_sum, bias_sum, dhb = 0.0, 0.0, 0.0, []
     for q in range(2):
@@ -1071,27 +1068,21 @@
         shift_sum = shift_sum + jnp.sum(da, axis=0, keepdims=True)
         bias_sum = bias_sum + jnp.sum(dh, axis=0, keepdims=True)
     dhb = jnp.concatenate(dhb, axis=0)
-    line_out[1].step(1)
+    line_out[1].begin()
+    line_out[0].step(1)
     sv[3:4] = gain_sum
     sv[4:5] = shift_sum
     sv[5:6] = bias_sum
     small_a = SmallSum(0)
     small_a.begin(sv[...])
     down_sum.turn()
+    up_sums.begin()
     wo[...] = tn(dhb, ctc[...]).astype(BF).reshape(8, strip, width)
     by_core = wo.reshape(4, 2, strip, width)
     go_b = net.bank(1)
     net.start(by_core.at[:, 1 - c], go_r, go_b, (sib, t))
 
     net.wait(dc.at[0:3], dc_z)
-    up_sums.turn()
-    net.wait(go_r, go_b)
-    go_r[...] = (by_core[:, c].astype(F32) + go_r[...].astype(F32)).astype(BF)
-    rp_b = net.bank(1)
-    for r in (xn, yn, dg):
-        net.start(go_r.at[r // 2], rp.at[chip], rp_b, (r, t))
-    rp[chip] = go_r[chip]
-    line_out[0].step(2)
     upper = lax.broadcasted_iota(jnp.int32, (part, BLOCK), 1) >= HD
     for s in range(4):
         for q in range(2):
@@ -1108,7 +1099,10 @@
     for b in range(blocks):
         lo, hi = span(b)
         at_q = slice(BLOCK * b, BLOCK * (b + 1))
+        if b == 3:
+            line_out[1].step(1)
         if b == 4:
+            line_out[0].step(2)
             down_sum.gather()
             down_sum.deliver()
         for h in range(heads):
@@ -1121,7 +1115,6 @@
             dvv[h][lo:hi] += nn(weights.astype(BF), dco[at_q, at])
             dqq[h][at_q] = nn(kkt[h, :, lo:hi], dsb).T * SCALING
 
-    line_out[1].step(2)
     small_a.plane()
     for h in range(heads):
         base = 6 * HD * h
@@ -1164,8 +1157,25 @@
     back_to_input(first_rows, first_two)
     for q, e in ((0, 3), (0, 2), (1, 3), (1, 2)):
         line_dx[q].depart(e)
-    up_sums.gather()
-    up_sums.deliver(is_mid)
+    back_to_input(other_rows, other_two)
+    line_dx[0].depart(1)
+    line_dx[1].depart(1)
+    line_out[1].step(2)
+    small_b = SmallSum(1)
+    small_b.begin(sv[...])
+
+    net.settle("q")
+    wq[...] = nn(xt[...], dqkv[...]).astype(BF).reshape(8, strip, 6 * local)
+    q_by_core = wq.reshape(4, 2, strip, 6 * local)
+    gq_b = net.bank(1)
+    net.start(q_by_core.at[:, 1 - c], gq_r, gq_b, (sib, t))
+    up_sums.turn()
+    net.wait(go_r, go_b)
+    go_r[...] = (by_core[:, c].astype(F32) + go_r[...].astype(F32)).astype(BF)
+    rp_b = net.bank(1)
+    for r in (xn, yn, dg):
+        net.start(go_r.at[r // 2], rp.at[chip], rp_b, (r, t))
+    rp[chip] = go_r[chip]
     plane_sum, other_sum = small_a.cores()
     first_core = c == 0
     own_units, other_units = plane_sum[6:7], other_sum[6:7]
@@ -1176,17 +1186,6 @@
     for k in (2, 1, 3):
         net.start(sent8, vz.at[t], vz_b, (d, (t + k) % 4), when=first_core)
     vz[t] = sent8[...]
-    back_to_input(other_rows, other_two)
-    line_dx[0].depart(1)
-    line_dx[1].depart(1)
-    small_b = SmallSum(1)
-    small_b.begin(sv[...])
-
-    net.settle("q")
-    wq[...] = nn(xt[...], dqkv[...]).astype(BF).reshape(8, strip, 6 * local)
-    q_by_core = wq.reshape(4, 2, strip, 6 * local)
-    gq_b = net.bank(1)
-    net.start(q_by_core.at[:, 1 - c], gq_r, gq_b, (sib, t))
     line_dx[0].through(3)
     line_dx[0].through(2)
     net.wait(gq_r, gq_b)
@@ -1197,6 +1196,17 @@
     gp[chip] = gq_r[chip]
 
     line_dx[0].pass_back()
+    line_dx[1].through(3)
+    line_dx[1].through(2)
+    line_dx[1].pass_back()
+    up_sums.gather()
+    up_sums.deliver(is_mid)
+    arrive(0)
+    arrive(1)
+
+    line_in[0].step(1)
+    line_in[1].step(1)
+    up_sums.deliver(is_end)
     net.wait(rp.at[0:3], rp_b)
     total = rp[0].astype(F32)
     for k in range(1, 4):
@@ -1214,15 +1224,6 @@
             s = (t + k) % 4
             net.start(sp.at[s], rz.at[t], rz_b, (d, s), when=when)
 
-    line_dx[1].through(3)
-    line_dx[1].through(2)
-    line_dx[1].pass_back()
-    arrive(0)
-    arrive(1)
-
-    line_in[0].step(1)
-    line_in[1].step(1)
-    up_sums.deliver(is_end)
     send_rz(None)
     line_out[0].step(3)
     line_out[1].step(3)

time: 129 us -> 127 us (0.984)
  Pallas kernels: 128 us -> 126 us
    pallas_call x1, Pallas kernels: 125 us -> 122 us  [fused(): pl.pallas_call(layer_kernel, out_shape=outs, in_specs=[anywhere if n in l...]
where the time goes in v7:
time: 127 us
  Pallas kernels  126 us (99%)
    pallas_call x1, Pallas kernels, fused(): pl.pallas_call(layer_kernel, out_shape=outs, in_specs=[anywhere if n in l...  122 us
    pallas_call x1, Pallas kernels, fused(): pl.pallas_call(end_kernel, out_shape=[like(v, v.dtype) for v in large] +...  3.65 us

profile of v7, /device:TPU:0, one launch (start us, length us, event | category | flops | bytes accessed | tf_op | source)
XLA Modules:
  0.0 126.5 jit_solution(16131438281846297074)
XLA Ops:
  0.7 122.1 %layer.1 = (bf16[1,640,768]{2,1,0:T(8,128)(2,1)}, bf16[1,640,768]{2,1,0:T(8,128)(2,1)}, f32[4,96,192]{2,1,0:T(8,128)}, f32[96,192]{1,0:T(8,128)}, f32[96,192]{1,...) custom-call(bf16[1,640,768]{2,1,0:T(8,128)(2,1)} %x_in.1, ...), custom_call_target="tpu_custom_call" | custom-call | tf_op jit(solution)/shard_map/layer/pallas_call | solution.py:1365
  122.7 3.6 %finish.1 = (bf16[1,640,768]{2,1,0:T(8,128)(2,1)}, bf16[1,640,768]{2,1,0:T(8,128)(2,1)}, f32[4,96,192]{2,1,0:T(8,128)}, f32[96,192]{1,0:T(8,128)}, f32[96,192]{1...) custom-call(bf16[1,640,768]{2,1,0:T(8,128)(2,1)} %get-tuple-element., ...), custom_call_target="tpu_custom_call" | custom-call | tf_op jit(solution)/shard_map/finish/pallas_call | solution.py:1378

commit v8 on v7

--- a/solution.py
+++ b/solution.py
@@ -424,7 +424,7 @@
 
 
 SENDS = 48
-RECVS = 141
+RECVS = 109
 
 
 def layer_kernel(
@@ -580,44 +580,43 @@
     pl.semaphore_wait(barrier, 11)
 
     class PlaneGather:
-        def __init__(self, group, *views):
-            self.views, self.bank, self.group = views, net.bank(8 * len(views)), group
-
-        def copy(self, view, block, device):
-            ref = self.views[view](block)
-            net.start(ref, ref, self.bank + 8 * view + block, (device, t), group=self.group)
-
-        def wait(self, view, block):
-            net.wait(self.views[view](block), self.bank + 8 * view + block)
+        def __init__(self, group, view, whole):
+            self.view, self.whole, self.group, self.bank = view, whole, group, net.bank(5)
+
+        def copy(self, half, block, device, sem):
+            ref = self.whole(block) if half is None else self.view(half, block)
+            net.start(ref, ref, self.bank + sem, (device, t), group=self.group)
 
         def begin(self):
-            for view, device in ((0, yn), (1, xn), (1, yn), (0, xn), (0, sib), (1, sib)):
-                self.copy(view, d, device)
+            self.copy(0, d, yn, 0)
+            self.copy(1, d, xn, 1)
+            self.copy(1, d, yn, 2)
+            self.copy(0, d, xn, 2)
+            self.copy(None, d, sib, 4)
 
         def middle(self):
-            self.wait(0, yn)
-            self.copy(0, yn, xn)
-            self.wait(1, xn)
-            self.copy(1, xn, yn)
-            self.copy(0, yn, sib)
-            self.copy(1, xn, sib)
+            net.wait(self.view(0, yn), self.bank)
+            self.copy(0, yn, xn, 3)
+            net.wait(self.view(1, xn), self.bank + 1)
+            self.copy(1, xn, yn, 3)
 
         def middle2(self):
-            for view, block in ((1, yn), (0, xn)):
-                self.wait(view, block)
-                self.copy(view, block, sib)
+            net.wait(self.whole(d), self.bank + 2)
+            self.copy(None, yn, sib, 4)
+            self.copy(None, xn, sib, 4)
 
         def late(self):
-            for view in range(2):
-                self.wait(view, dg)
-                self.copy(view, dg, sib)
+            net.wait(self.whole(dg), self.bank + 3)
+            self.copy(None, dg, sib, 4)
 
         def end(self):
-            for block in (sib, flip_x(sib), flip_y(sib), flip_x(flip_y(sib))):
-                for view in range(len(self.views)):
-                    self.wait(view, block)
-
-    gather_q = PlaneGather("q", lambda b: wq.at[b, : strip // 2], lambda b: wq.at[b, strip // 2 :])
+            net.wait(self.whole(slice(0, 4)), self.bank + 4)
+
+    most = strip // 2
+
+    gather_q = PlaneGather(
+        "q", lambda half, b: wq.at[b, most * half : most * (half + 1)], lambda b: wq.at[b]
+    )
     gather_q.begin()
 
     def wide_t(value, high, wide):
@@ -651,7 +650,7 @@
 
     class ChipGather:
         def __init__(self, i):
-            self.i, self.bank = i, net.bank(8)
+            self.i, self.bank = i, net.bank(3)
 
         def send_near(self):
             i = self.i
@@ -664,30 +663,29 @@
         def send_far(self):
             net.start(own.at[self.i], wf.at[self.i, d], wf_a + 2 * self.i + c, (host, zq))
 
-        def copy(self, view, of, device, when=None):
+        def copy(self, view, of, device, sem, when=None):
             ref = wf.at[self.i, 2 * (of // 2) + view]
-            net.start(ref, ref, self.bank + 2 * (of // 2) + view, (device, t), when=when, group="f")
-
-        def wait(self, view, of):
-            net.wait(wf.at[self.i, 2 * (of // 2) + view], self.bank + 2 * (of // 2) + view)
+            net.start(ref, ref, self.bank + sem, (device, t), when=when, group="f")
+
+        def wait(self, view, of, sem):
+            net.wait(wf.at[self.i, 2 * (of // 2) + view], self.bank + sem)
 
         def begin(self, at_home):
             i, when = self.i, home if at_home else jnp.logical_not(home)
             if not at_home:
                 net.wait(wf.at[i, d], wf_a + 2 * i + c, when=when)
             net.wait(wf.at[i, sib], wf_a + 2 * i + 1 - c, when=when)
-            for view, device in ((0, yn), (1, xn), (1, yn), (0, xn)):
-                self.copy(view, d, device, when)
+            for view, device, sem in ((0, yn, 0), (1, xn, 1), (1, yn, 2), (0, xn, 2)):
+                self.copy(view, d, device, sem, when)
 
         def middle(self):
-            self.wait(0, yn)
-            self.copy(0, yn, xn)
-            self.wait(1, xn)
-            self.copy(1, xn, yn)
+            self.wait(0, yn, 0)
+            self.copy(0, yn, xn, 2)
+            self.wait(1, xn, 1)
+            self.copy(1, xn, yn, 2)
 
         def end(self):
-            for view, of in ((1, yn), (0, xn), (0, dg), (1, dg)):
-                self.wait(view, of)
+            net.wait(wf.at[self.i, 0:4], self.bank + 2)
 
     up, down = ChipGather(0), ChipGather(1)
     wo_z = net.bank(1)
@@ -710,12 +708,14 @@
 
     gather_q.middle()
     up.send_far()
-    net.start(ubs.at[t], ubs.at[t], ub_z, (d, zq))
-    down.send_far()
     gather_q.middle2()
     net.wait(wop.at[0:3, d], wo_z)
-    gather_o = PlaneGather("o", lambda b: wop.at[0:2, b], lambda b: wop.at[2:4, b])
+    gather_o = PlaneGather(
+        "o", lambda half, b: wop.at[2 * half : 2 * half + 2, b], lambda b: wop.at[:, b]
+    )
     gather_o.begin()
+    down.send_far()
+    net.start(ubs.at[t], ubs.at[t], ub_z, (d, zq))
     up.begin(True)
     gather_q.late()
     gather_q.end()
@@ -775,7 +775,6 @@
     gather_o.end()
     for s in range(4):
         wo[:, :, BLOCK * s : BLOCK * (s + 1)] = wop[s, :, :strip]
-    most = strip // 2
     for s in (0, 2):
         at = slice(4 * BLOCK + HD * s, 4 * BLOCK + HD * (s + 2))
         one, other = wop[s, :, strip:], wop[s + 1, :, strip:]
@@ -1182,10 +1181,6 @@
     sent8[0:6] = plane_sum[0:6] + other_sum[0:6]
     sent8[6:7] = jnp.where(first_core, own_units, other_units)
     sent8[7:8] = jnp.where(first_core, other_units, own_units)
-    vz_b = net.bank(2)
-    for k in (2, 1, 3):
-        net.start(sent8, vz.at[t], vz_b, (d, (t + k) % 4), when=first_core)
-    vz[t] = sent8[...]
     line_dx[0].through(3)
     line_dx[0].through(2)
     net.wait(gq_r, gq_b)
@@ -1225,6 +1220,10 @@
             net.start(sp.at[s], rz.at[t], rz_b, (d, s), when=when)
 
     send_rz(None)
+    vz_b = net.bank(2)
+    for k in (2, 1, 3):
+        net.start(sent8, vz.at[t], vz_b, (d, (t + k) % 4), when=first_core)
+    vz[t] = sent8[...]
     line_out[0].step(3)
     line_out[1].step(3)
     ends = [Local(out_ref, out_end)]

time: 127 us -> 126 us (level)
  no operation moved by 1% of the time
where the time goes in v8:
time: 126 us
  Pallas kernels  125 us (99%)
    pallas_call x1, Pallas kernels, fused(): pl.pallas_call(layer_kernel, out_shape=outs, in_specs=[anywhere if n in l...  121 us
    pallas_call x1, Pallas kernels, fused(): pl.pallas_call(end_kernel, out_shape=[like(v, v.dtype) for v in large] +...  3.65 us

profile of v8, /device:TPU:0, one launch (start us, length us, event | category | flops | bytes accessed | tf_op | source)
XLA Modules:
  0.0 125.5 jit_solution(4135409074659194258)
XLA Ops:
  0.7 121.1 %layer.1 = (bf16[1,640,768]{2,1,0:T(8,128)(2,1)}, bf16[1,640,768]{2,1,0:T(8,128)(2,1)}, f32[4,96,192]{2,1,0:T(8,128)}, f32[96,192]{1,0:T(8,128)}, f32[96,192]{1,...) custom-call(bf16[1,640,768]{2,1,0:T(8,128)(2,1)} %x_in.1, ...), custom_call_target="tpu_custom_call" | custom-call | tf_op jit(solution)/shard_map/layer/pallas_call | solution.py:1364
  121.7 3.6 %finish.1 = (bf16[1,640,768]{2,1,0:T(8,128)(2,1)}, bf16[1,640,768]{2,1,0:T(8,128)(2,1)}, f32[4,96,192]{2,1,0:T(8,128)}, f32[96,192]{1,0:T(8,128)}, f32[96,192]{1...) custom-call(bf16[1,640,768]{2,1,0:T(8,128)(2,1)} %get-tuple-element., ...), custom_call_target="tpu_custom_call" | custom-call | tf_op jit(solution)/shard_map/finish/pallas_call | solution.py:1377

commit v9 on v8

--- a/solution.py
+++ b/solution.py
@@ -424,7 +424,7 @@
 
 
 SENDS = 48
-RECVS = 109
+RECVS = 119
 
 
 def layer_kernel(
@@ -749,15 +749,18 @@
         lo, hi = span(b)
         at_q = slice(BLOCK * b, BLOCK * (b + 1))
         same = segc[lo:hi, :] == seg_ref[:, at_q].astype(F32)
-        found = []
+        found, raw = [], []
         for h in range(heads):
             at = slice(BLOCK * h, BLOCK * (h + 1))
-            scores = nt(kk[lo:hi, at], qq[at_q, at]) * SCALING
-            scores = jnp.where(same, scores, NEGATIVE)
+            raw.append(nt(kk[lo:hi, at], qq[at_q, at]))
+        for h in range(heads):
+            scores = jnp.where(same, raw[h] * SCALING, NEGATIVE)
             weights = jnp.exp(scores - jnp.max(scores, axis=0, keepdims=True))
             weights = weights * (1.0 / jnp.sum(weights, axis=0, keepdims=True))
             probs[h, kept[b] : kept[b + 1]] = weights
-            found.append(nn(kvt[h, :, lo:hi], weights.astype(BF)))
+            raw[h] = weights.astype(BF)
+        for h in range(heads):
+            found.append(nn(kvt[h, :, lo:hi], raw[h]))
         found.append(jnp.zeros((HD, BLOCK), F32))
         ctx[at_q, :] = jnp.concatenate(found, axis=0).T[:, :local].astype(BF)
         if b == 2:
@@ -1104,15 +1107,27 @@
             line_out[0].step(2)
             down_sum.gather()
             down_sum.deliver()
-        for h in range(heads):
-            at = slice(BLOCK * h, BLOCK * (h + 1))
+        columns = [slice(BLOCK * h, BLOCK * (h + 1)) for h in range(heads)]
+        lows = []
+        for h, at in enumerate(columns):
+            dp = nt(kv[lo:hi, at], dco[at_q, at])
             weights = probs[h, kept[b] : kept[b + 1]]
-            dp = nt(kv[lo:hi, at], dco[at_q, at])
             ds = weights * (dp - jnp.sum(weights * dp, axis=0, keepdims=True))
-            dsb = ds.astype(BF)
-            dkk[h][lo:hi] += nn(dsb, qq[at_q, at])
-            dvv[h][lo:hi] += nn(weights.astype(BF), dco[at_q, at])
-            dqq[h][at_q] = nn(kkt[h, :, lo:hi], dsb).T * SCALING
+            lows.append((ds.astype(BF), weights.astype(BF)))
+        for h, at in enumerate(columns):
+            low, weights = lows[h]
+            blank = jnp.zeros((BLOCK, BLOCK), BF)
+            beside = jnp.concatenate(
+                [
+                    jnp.concatenate([qq[at_q, at], blank], axis=1),
+                    jnp.concatenate([blank, dco[at_q, at]], axis=1),
+                ],
+                axis=0,
+            )
+            made = nn(jnp.concatenate([low, weights], axis=1), beside)
+            dkk[h][lo:hi] += made[:, :BLOCK]
+            dvv[h][lo:hi] += made[:, BLOCK:]
+            dqq[h][at_q] = nn(kkt[h, :, lo:hi], low).T * SCALING
 
     small_a.plane()
     for h in range(heads):
@@ -1137,28 +1152,35 @@
         made = nt(dqkv[rows_b, :], wq[...].reshape(width, 6 * local))
         dzb[quarters] = made.astype(BF).reshape(2, quarter, width)
 
+    third = [slice(width // 3 * q, width // 3 * (q + 1)) for q in range(3)]
     line_dx, line_in = [], []
-    for q in range(2):
-        cut = pl.ds(part * q, part)
+    for q, cut in enumerate(third):
         line_dx.append(
             LineReduce(
-                lambda e, cut=cut: dzb.at[place(e), cut],
+                lambda e, cut=cut: dzb.at[place(e), :, cut],
                 dx_in.at[q], dx_cross.at[q], dx_back.at[q],
             )
         )
-        line_in.append(LineGather(rows_of(ig_ref, part * q, part)))
+        line_in.append(
+            LineGather(
+                lambda owner, cut=cut: ig_ref.at[
+                    0, pl.ds(pl.multiple_of(owner * quarter, 16), quarter), cut
+                ]
+            )
+        )
 
     def arrive(q):
-        total = line_dx[q].total() + a_s[part * q : part * (q + 1)]
-        ig_ref[0, pl.ds(pl.multiple_of(t * quarter + part * q, 16), part)] = total.astype(BF)
+        total = line_dx[q].total() + a_s[:, third[q]]
+        ig_ref[0, own_rows, third[q]] = total.astype(BF)
         line_in[q].begin()
 
     back_to_input(first_rows, first_two)
-    for q, e in ((0, 3), (0, 2), (1, 3), (1, 2)):
-        line_dx[q].depart(e)
+    for q in range(3):
+        line_dx[q].depart(3)
+        line_dx[q].depart(2)
     back_to_input(other_rows, other_two)
-    line_dx[0].depart(1)
-    line_dx[1].depart(1)
+    for q in range(3):
+        line_dx[q].depart(1)
     line_out[1].step(2)
     small_b = SmallSum(1)
     small_b.begin(sv[...])
@@ -1194,14 +1216,17 @@
     line_dx[1].through(3)
     line_dx[1].through(2)
     line_dx[1].pass_back()
-    up_sums.gather()
-    up_sums.deliver(is_mid)
+    line_dx[2].through(3)
+    line_dx[2].through(2)
+    line_dx[2].pass_back()
     arrive(0)
     arrive(1)
-
-    line_in[0].step(1)
-    line_in[1].step(1)
-    up_sums.deliver(is_end)
+    arrive(2)
+
+    for q in range(3):
+        line_in[q].step(1)
+    up_sums.gather()
+    up_sums.deliver()
     net.wait(rp.at[0:3], rp_b)
     total = rp[0].astype(F32)
     for k in range(1, 4):
@@ -1227,8 +1252,8 @@
     line_out[0].step(3)
     line_out[1].step(3)
     ends = [Local(out_ref, out_end)]
-    line_in[0].step(2)
-    line_in[1].step(2)
+    for q in range(3):
+        line_in[q].step(2)
     small_b.plane()
     net.wait(vz.at[0:3], vz_b, when=first_core)
 
@@ -1271,7 +1296,7 @@
         vg_ref[:, at] = total[:, base + 5 * HD : base + 6 * HD]
 
     ends += [Local(qg_ref, qg_end), Local(kg_ref, kg_end), Local(vg_ref, vg_end)]
-    for q in range(2):
+    for q in range(3):
         line_in[q].step(3)
     ends += [Local(ig_ref, ig_end)]
     net.settle()
@@ -1350,8 +1375,8 @@
         v((4, strip, width), BF), v((4, strip, width), BF), v((4, 3 * strip // 2, BLOCK), BF),
         v((4, 3 * strip // 2, BLOCK), BF),
         v((rows, 6 * local), BF),
-        v((2, 3, quarter // 2, width), BF), v((2, 2, quarter // 2, width), BF),
-        v((2, quarter // 2, width), BF),
+        v((3, 3, quarter, width // 3), BF), v((3, 2, quarter, width // 3), BF),
+        v((3, quarter, width // 3), BF),
         v((4, strip, 6 * local), BF), v((4, strip, 6 * local), BF),
         v((8, width), F32), v((2, 2, 8, width), F32), v((2, 5, 8, width), F32),
         v((8, width), F32), v((8, width), F32), v((4, 8, width), F32),

time: 126 us -> 125 us (level)
  no operation moved by 1% of the time
where the time goes in v9:
time: 125 us
  Pallas kernels  124 us (99%)
    pallas_call x1, Pallas kernels, fused(): pl.pallas_call(layer_kernel, out_shape=outs, in_specs=[anywhere if n in l...  120 us
    pallas_call x1, Pallas kernels, fused(): pl.pallas_call(end_kernel, out_shape=[like(v, v.dtype) for v in large] +...  3.65 us

profile of v9, /device:TPU:0, one launch (start us, length us, event | category | flops | bytes accessed | tf_op | source)
XLA Modules:
  0.0 124.8 jit_solution(369198618489210815)
XLA Ops:
  0.7 120.3 %layer.1 = (bf16[1,640,768]{2,1,0:T(8,128)(2,1)}, bf16[1,640,768]{2,1,0:T(8,128)(2,1)}, f32[4,96,192]{2,1,0:T(8,128)}, f32[96,192]{1,0:T(8,128)}, f32[96,192]{1,...) custom-call(bf16[1,640,768]{2,1,0:T(8,128)(2,1)} %x_in.1, ...), custom_call_target="tpu_custom_call" | custom-call | tf_op jit(solution)/shard_map/layer/pallas_call | solution.py:1389
  121.0 3.6 %finish.1 = (bf16[1,640,768]{2,1,0:T(8,128)(2,1)}, bf16[1,640,768]{2,1,0:T(8,128)(2,1)}, f32[4,96,192]{2,1,0:T(8,128)}, f32[96,192]{1,0:T(8,128)}, f32[96,192]{1...) custom-call(bf16[1,640,768]{2,1,0:T(8,128)(2,1)} %get-tuple-element., ...), custom_call_target="tpu_custom_call" | custom-call | tf_op jit(solution)/shard_map/finish/pallas_call | solution.py:1402
